TPU v7x, 512 devices: a whole 4x8x8 slice. The times are simulated.
512 devices in a mesh: inst: 8 (over z), axial: 16 (over y, core), span: 4 (over x).
Axes of the slice: x: 4, y: 8, z: 8, core: 2. Of those that a mesh axis runs over, the one named last changes fastest.
Arguments:
- state: float32 [8, 256, 5, 2048], P('inst', 'axial', None, 'span'), may hold values from -6 to 6
- source_terms: float32 [8, 256, 5, 2048], P('inst', 'axial', None, 'span'), may hold values from -6 to 6
- pivot_inverse: float32 [8, 256, 5, 5, 2048], P('inst', 'axial', None, None, 'span'), may hold values from -0.002 to 0.024
- coupling: float32 [8, 256, 5, 5, 2048], P('inst', 'axial', None, None, 'span'), may hold values from -1 to 1
- back_coupling: float32 [8, 256, 5, 5, 2048], P('inst', 'axial', None, None, 'span'), may hold values from -1 to 1
- wall_flags: int32 [256, 2048], P('axial', 'span'), may hold values 0 or 1
Outputs:
- smoothed: float32 [8, 256, 5, 2048], P('inst', 'axial', None, 'span')
All inputs are finite; a program needn't handle non-finite values. No bound on the sum of `wall_flags` on one device may be relied on, other than what follows from the above.
Results may differ from a plain program's by a relative error of at most 0.0003.
Values sent between devices are 32-bit elements; how exact they have to be, the bound alone decides.
No kernel may reach another device: no remote copies, remote signals or barrier semaphores. Data moves between devices by JAX's collectives and lax.ppermute only.
A program may use at most 64 MiB of HBM per device.

v0:
```python
import math

import jax
import jax.numpy as jnp
from jax import lax
from jax.sharding import PartitionSpec as P

INST = 8
SWEEPS = 2


time_weight = 0.5
convection_term = 0.6
viscosity = 0.2
circular = 0.2
dissipation = 0.5


def shifted(value, axis, steps):
    count = lax.axis_size(axis)
    initial, last = (max(0, -steps), min(count, count - steps))
    return lax.ppermute(value, axis, [(source, source + steps) for source in range(initial, last)])


def with_halo(value, sides, width, wrap):
    for axis, dim in sides:
        peers, length = (lax.axis_size(axis), value.shape[dim])
        up = [(i, (i + 1) % peers) for i in range(peers if wrap else peers - 1)]
        down = [(j, i) for i, j in up]
        last = lax.slice_in_dim(value, length - width, length, axis=dim)
        initial = lax.slice_in_dim(value, 0, width, axis=dim)
        before = lax.ppermute(last, axis, up)
        after = lax.ppermute(initial, axis, down)
        value = jnp.concatenate([before, value, after], axis=dim)
    return value


def spectral(rows, cols):
    diff = rows[:, None] - cols[None, :]
    sign = (1 - 2 * jnp.mod(diff, 2)).astype(jnp.float32)
    angle = math.pi * diff.astype(jnp.float32) / INST
    safe = jnp.where(diff == 0, 0.5 * math.pi, angle)
    first = jnp.where(diff == 0, 0.0, 0.5 * sign * jnp.cos(safe) / jnp.sin(safe))
    sine = jnp.sin(safe)
    second = jnp.where(diff == 0, -(INST * INST + 2.0) / 12.0, -0.5 * sign / (sine * sine))
    return first - dissipation * second


def cell_apply(matrix, vector):
    return jnp.sum(matrix * vector[:, None, :, :], axis=2)


def compose(later, earlier):
    return jnp.sum(later[:, :, :, None, :] * earlier[:, None, :, :, :], axis=2)


def identity_like(vector):
    count = vector.shape[1]
    eye = (jnp.arange(count)[:, None] == jnp.arange(count)[None, :]).astype(jnp.float32)
    return jnp.broadcast_to(eye[None, :, :, None], (vector.shape[0], count, count, vector.shape[2]))


def run_chain(source, coupling, start, reverse, with_maps):
    count = source.shape[1]
    order = jnp.arange(count)
    if reverse:
        order = order[::-1]
    if with_maps:
        total_init = identity_like(start)
    else:
        total_init = jnp.zeros((), jnp.float32)

    def advance(carry, index):
        prev, total = carry
        src = lax.dynamic_index_in_dim(source, index, 1, keepdims=False)
        cpl = lax.dynamic_index_in_dim(coupling, index, 1, keepdims=False)
        now = src - cell_apply(cpl, prev)
        if with_maps:
            total = compose(-cpl, total)
        return ((now, total), now)

    (last, total), values = lax.scan(advance, (start, total_init), order)
    if reverse:
        values = values[::-1]
    return (jnp.moveaxis(values, 0, 1), last, total)


def forward_entry(maps, end_zero):
    position = lax.axis_index("axial")
    count = lax.axis_size("axial")

    def forward_turn(step, carry):
        current, entry = carry
        received = shifted(current, "axial", 1)
        mine = position == step + 1
        current = jnp.where(mine, cell_apply(maps, received) + end_zero, current)
        entry = jnp.where(mine, received, entry)
        return (current, entry)

    _, entry = lax.fori_loop(0, count - 1, forward_turn, (end_zero, jnp.zeros_like(end_zero)))
    return entry


def backward_entry(maps, first_zero):
    position = lax.axis_index("axial")
    count = lax.axis_size("axial")

    def backward_turn(step, carry):
        current, entry = carry
        received = shifted(current, "axial", -1)
        mine = position == count - 2 - step
        current = jnp.where(mine, cell_apply(maps, received) + first_zero, current)
        entry = jnp.where(mine, received, entry)
        return (current, entry)

    _, entry = lax.fori_loop(0, count - 1, backward_turn, (first_zero, jnp.zeros_like(first_zero)))
    return entry


def time_term(state):
    rows = lax.axis_index("inst") * state.shape[0] + jnp.arange(state.shape[0])
    piece = lax.all_gather(state, "inst", axis=0, tiled=True)
    cols = jnp.arange(piece.shape[0])
    weights = spectral(rows, cols)
    return jnp.sum(weights[:, :, None, None, None] * piece[None], axis=1)


def body(state, source_terms, pivot_inverse, coupling, back_coupling, wall_flags):
    keep = (1 - wall_flags).astype(jnp.float32)[None, :, None, :]
    for sweep in range(SWEEPS):
        time = time_term(state)
        rim_cells = with_halo(state, (("axial", 1),), 1, False)
        below = rim_cells[:, :-2]
        above = rim_cells[:, 2:]
        cycle_cells = with_halo(state, (("span", 3),), 1, True)
        left = cycle_cells[:, :, :, :-2]
        right = cycle_cells[:, :, :, 2:]
        rhs = keep * (
            source_terms
            - time_weight * time
            - 0.5 * convection_term * (above - below)
            + viscosity * (above - 2.0 * state + below)
            + circular * (right - 2.0 * state + left)
        )
        source = jnp.sum(pivot_inverse * rhs[:, :, None], axis=3)
        zeros = jnp.zeros((state.shape[0], state.shape[2], state.shape[3]), jnp.float32)
        _, end_zero, maps = run_chain(source, coupling, zeros, False, True)
        entry = forward_entry(maps, end_zero)
        downstream_elimination, _, _ = run_chain(source, coupling, entry, False, False)
        _, first_zero, back_maps = run_chain(
            downstream_elimination, back_coupling, zeros, True, True
        )
        back_entry = backward_entry(back_maps, first_zero)
        backward, _, _ = run_chain(downstream_elimination, back_coupling, back_entry, True, False)
        state = state + backward
    return state


def solution(mesh):
    return jax.shard_map(
        body,
        mesh=mesh,
        in_specs=(
            P("inst", "axial", None, "span"),
            P("inst", "axial", None, "span"),
            P("inst", "axial", None, None, "span"),
            P("inst", "axial", None, None, "span"),
            P("inst", "axial", None, None, "span"),
            P("axial", "span"),
        ),
        out_specs=P("inst", "axial", None, "span"),
        check_vma=False,
    )
```

profile of v0, /device:TPU:25, one launch (start us, length us, event | category | flops | bytes accessed | tf_op | source)
XLA Modules:
  0.0 918.8 jit_solution(6461353594654589770)
XLA Ops:
  28.1 23.9 %all-gather.3.cloned.1.call-done = f32[8,16,5,512]{3,1,2,0:T(8,128)} async-done(((f32[1,16,5,512]{3,1,2,0:T(8,128)}), f32[8,16,5,512]{3,1,2,0:T(8,128)}) %all-gather.3.cloned.1.call-update) | async-done | bytes 1310736 | tf_op jit(solution)/shard_map/all_gather | solution.py:122
  54.9 47.5 %while.168 = (s32[]{:T(128)}, f32[1,5,512]{2,1,0:T(8,128)S(1)}, f32[1,5,5,512]{3,2,1,0:T(8,128)S(1)}, s32[16]{0:T(128)S(1)}, f32[1,16,5,512]{3,2,1,0:T(8,128)S(1...) while((s32[]{:T(128)}, f32[1,5,512]{2,1,0:T(8,128)S(1)}, ...), condition=%wide.region_5.6_spmd.clone, body=%wide.region_2.5_spmd.clone.sunk | while | flops 156166 | bytes 481441 | solution.py:82
  102.4 99.2 %while.169 = (s32[]{:T(128)}, f32[1,5,512]{2,1,0:T(8,128)S(1)}, f32[1,5,512]{2,1,0:T(8,128)S(1)}, s32[]{:T(128)}, f32[1,5,5,512]{3,2,1,0:T(8,128)S(1)}, /*index=5*/f32[1,5,512]{2,1,0:T(8,128)S(1)}, s32[]{:T(128)}, s32[]{:T(128)}) while((s32[]{:T(128)}, f32[1,5,512]{2,1,0:T(8,128)S(1)}, f32[1,5,512]{2,1,0:T(8,128)S(1)}, s32[]{:T(128)}, ...), condition=%wide.region_8.9_spmd.clone, body=%wide.region_6.8_spmd.clone.sunk | while | flops 33284 | bytes 184473 | solution.py:100
  102.4 9.6 %collective-permute-start = (f32[1,5,512]{2,1,0:T(8,128)S(1)}, f32[1,5,512]{2,1,0:T(8,128)S(1)}, u32[]{:S(2)}, u32[]{:S(2)}) collective-permute-start(f32[1,5,512]{2,1,0:T(8,128)S(1)} %get-tuple-element.1637), channel_id=1, source_target_pairs={{0,4},{4,8},{8,12},{12,16},{16,20},{20,24},{24,28},{28,32},{32,36}... | collective-permute-start | bytes 30728 | tf_op jit(solution)/shard_map/while/body/eval_jaxpr/ppermute | solution.py:22
  112.9 5.4 collective-permute-start
  119.3 5.4 collective-permute-start
  125.6 5.4 collective-permute-start
  138.3 5.4 collective-permute-start
  144.6 5.4 collective-permute-start
  150.9 5.4 collective-permute-start
  157.3 5.4 collective-permute-start
  163.6 5.4 collective-permute-start
  169.9 5.4 collective-permute-start
  176.3 5.4 collective-permute-start
  182.6 5.4 collective-permute-start
  189.0 5.4 collective-permute-start
  195.3 5.4 collective-permute-start
  201.7 58.9 %while.164 = (s32[]{:T(128)}, f32[1,5,512]{2,1,0:T(8,128)S(1)}, f32[16,1,5,512]{3,2,1,0:T(8,128)S(1)}, s32[16]{0:T(128)S(1)}, f32[1,16,5,512]{3,2,1,0:T(8,128)S(...) while((s32[]{:T(128)}, f32[1,5,512]{2,1,0:T(8,128)S(1)}, ...), condition=%wide.region_11.12_spmd, body=%wide.region_9.11_spmd.sunk | while | flops 28165 | bytes 151707 | solution.py:82
  260.7 47.4 %while.170 = (s32[]{:T(128)}, f32[1,5,512]{2,1,0:T(8,128)S(1)}, f32[1,5,5,512]{3,2,1,0:T(8,128)S(1)}, s32[16]{0:T(128)S(1)}, f32[1,16,5,512]{3,2,1,0:T(8,128)S(1...) while((s32[]{:T(128)}, f32[1,5,512]{2,1,0:T(8,128)S(1)}, ...), condition=%wide.region_15.16_spmd.clone, body=%wide.region_12.15_spmd.clone.sunk | while | flops 156166 | bytes 481441 | solution.py:82
  308.2 95.8 %while.171 = (s32[]{:T(128)}, f32[1,5,512]{2,1,0:T(8,128)S(1)}, f32[1,5,512]{2,1,0:T(8,128)S(1)}, s32[]{:T(128)}, f32[1,5,5,512]{3,2,1,0:T(8,128)S(1)}, /*index=...) while((s32[]{:T(128)}, f32[1,5,512]{2,1,0:T(8,128)S(1)}, ...), condition=%wide.region_18.19_spmd.clone, body=%wide.region_16.18_spmd.clone.sunk | while | flops 33285 | bytes 184485 | solution.py:116
  404.0 60.8 %while.165 = (s32[]{:T(128)}, f32[1,5,512]{2,1,0:T(8,128)S(1)}, f32[16,1,5,512]{3,0,2,1:T(8,128)S(1)}, s32[16]{0:T(128)S(1)}, f32[1,16,5,512]{3,2,1,0:T(8,128)S(...) while((s32[]{:T(128)}, f32[1,5,512]{2,1,0:T(8,128)S(1)}, ...), condition=%wide.region_21.22_spmd, body=%wide.region_19.21_spmd.sunk | while | flops 28165 | bytes 174235 | solution.py:82
  480.5 18.9 %all-gather.5.cloned.1.call-done = f32[8,16,5,512]{3,1,2,0:T(8,128)} async-done(((f32[1,16,5,512]{3,1,2,0:T(8,128)}), f32[8,16,5,512]{3,1,2,0:T(8,128)}) %all-gather.5.cloned.1.call-update) | async-done | bytes 1310736 | tf_op jit(solution)/shard_map/all_gather | solution.py:122
  501.6 47.5 %while.172 = (s32[]{:T(128)}, f32[1,5,512]{2,1,0:T(8,128)S(1)}, f32[1,5,5,512]{3,2,1,0:T(8,128)S(1)}, s32[16]{0:T(128)S(1)}, f32[1,16,5,512]{3,2,1,0:T(8,128)S(1...) while((s32[]{:T(128)}, f32[1,5,512]{2,1,0:T(8,128)S(1)}, ...), condition=%wide.region_27.28_spmd.clone, body=%wide.region_24.27_spmd.clone.sunk | while | flops 156166 | bytes 481441 | solution.py:82
  549.0 99.0 %while.173 = (s32[]{:T(128)}, f32[1,5,512]{2,1,0:T(8,128)S(1)}, f32[1,5,512]{2,1,0:T(8,128)S(1)}, s32[]{:T(128)}, f32[1,5,5,512]{3,2,1,0:T(8,128)S(1)}, /*index=5*/f32[1,5,512]{2,1,0:T(8,128)S(1)}, s32[]{:T(128)}, s32[]{:T(128)}) while((s32[]{:T(128)}, f32[1,5,512]{2,1,0:T(8,128)S(1)}, f32[1,5,512]{2,1,0:T(8,128)S(1)}, ...), condition=%wide.region_30.31_spmd.clone, body=%wide.region_28.30_spmd.clone.sunk | while | flops 33284 | bytes 184473 | solution.py:100
  549.0 9.4 %collective-permute-start.2 = (f32[1,5,512]{2,1,0:T(8,128)S(1)}, f32[1,5,512]{2,1,0:T(8,128)S(1)}, u32[]{:S(2)}, u32[]{:S(2)}) collective-permute-start(f32[1,5,512]{2,1,0:T(8,128)S(1)} %get-tuple-element.1796), channel_id=1, source_target_pairs={{0,4},{4,8},{8,12},{12,16},{16,20},{20,24},{24,28},{28,32},{32,36}... | collective-permute-start | bytes 30728 | tf_op jit(solution)/shard_map/while/body/eval_jaxpr/ppermute | solution.py:22
  565.7 5.4 collective-permute-start.2
  572.1 5.4 collective-permute-start.2
  578.4 5.4 collective-permute-start.2
  648.1 58.9 %while.166 = (s32[]{:T(128)}, f32[1,5,512]{2,1,0:T(8,128)S(1)}, f32[16,1,5,512]{3,2,1,0:T(8,128)S(1)}, s32[16]{0:T(128)S(1)}, f32[1,16,5,512]{3,2,1,0:T(8,128)S(...) while((s32[]{:T(128)}, f32[1,5,512]{2,1,0:T(8,128)S(1)}, ...), condition=%wide.region_33.34_spmd, body=%wide.region_31.33_spmd.sunk | while | flops 28165 | bytes 151707 | solution.py:82
  707.1 47.4 %while.174 = (s32[]{:T(128)}, f32[1,5,512]{2,1,0:T(8,128)S(1)}, f32[1,5,5,512]{3,2,1,0:T(8,128)S(1)}, s32[16]{0:T(128)S(1)}, f32[1,16,5,512]{3,2,1,0:T(8,128)S(1...) while((s32[]{:T(128)}, f32[1,5,512]{2,1,0:T(8,128)S(1)}, ...), condition=%wide.region_37.38_spmd.clone, body=%wide.region_34.37_spmd.clone.sunk | while | flops 156166 | bytes 481441 | solution.py:82
  754.6 95.7 %while.175 = (s32[]{:T(128)}, f32[1,5,512]{2,1,0:T(8,128)S(1)}, f32[1,5,512]{2,1,0:T(8,128)S(1)}, s32[]{:T(128)}, f32[1,5,5,512]{3,2,1,0:T(8,128)S(1)}, /*index=...) while((s32[]{:T(128)}, f32[1,5,512]{2,1,0:T(8,128)S(1)}, ...), condition=%wide.region_40.41_spmd.clone, body=%wide.region_38.40_spmd.clone.sunk | while | flops 33285 | bytes 184485 | solution.py:116
  850.3 60.8 %while.167 = (s32[]{:T(128)}, f32[1,5,512]{2,1,0:T(8,128)S(1)}, f32[16,1,5,512]{3,0,2,1:T(8,128)S(1)}, s32[16]{0:T(128)S(1)}, f32[1,16,5,512]{3,2,1,0:T(8,128)S(...) while((s32[]{:T(128)}, f32[1,5,512]{2,1,0:T(8,128)S(1)}, ...), condition=%wide.region_43.44_spmd, body=%wide.region_41.43_spmd.sunk | while | flops 28165 | bytes 174235 | solution.py:82
  (1077 shorter events, 498.2 us)
Async XLA Ops:
  6.5 45.5 %all-gather.3.cloned.1.call-start = ((), (), s32[]{:S(2)}) async-start(), calls=%async_computation | async-start | bytes 1474560 | tf_op jit(solution)/shard_map/all_gather | solution.py:122
  7.3 492.1 %all-gather.5.cloned.1.call-start = ((), (), s32[]{:S(2)}) async-start(), calls=%async_computation.1 | async-start | bytes 1474560 | tf_op jit(solution)/shard_map/all_gather | solution.py:122
  8.8 44.8 %collective-permute-start.6 = (f32[1,16,5,1]{3,1,2,0:T(8,128)}, f32[1,16,5,1]{3,1,2,0:T(8,128)}, u32[]{:S(2)}, u32[]{:S(2)}) collective-permute-start(f32[1,16,5,1]{3,1,2,0:T(8,128)} %get-tuple-element.1139), channel_id=1, source_target_pairs={{1,0},{2,1},{3,2},{0,3},{5,4},{6,5},{7,6},{4,7},{9,8},{10,9},{11,1... | collective-permute-start | bytes 968 | tf_op jit(solution)/shard_map/ppermute | solution.py:33
  13.2 40.4 %collective-permute-start.7 = (f32[1,16,5,1]{3,1,2,0:T(8,128)}, f32[1,16,5,1]{3,1,2,0:T(8,128)}, u32[]{:S(2)}, u32[]{:S(2)}) collective-permute-start(f32[1,16,5,1]{3,1,2,0:T(8,128)} %get-tuple-element.1140), channel_id=1, source_target_pairs={{0,1},{1,2},{2,3},{3,0},{4,5},{5,6},{6,7},{7,4},{8,9},{9,10},{10,1... | collective-permute-start | bytes 968 | tf_op jit(solution)/shard_map/ppermute | solution.py:32
  16.6 37.0 %collective-permute-start.4 = (f32[1,1,5,512]{3,1,2,0:T(1,128)}, f32[1,1,5,512]{3,1,2,0:T(1,128)}, u32[]{:S(2)}, u32[]{:S(2)}) collective-permute-start(f32[1,1,5,512]{3,1,2,0:T(1,128)} %get-tuple-element.1138), channel_id=1, source_target_pairs={{4,0},{8,4},{12,8},{16,12},{20,16},{24,20},{28,24},{32,28},{36,32}... | collective-permute-start | bytes 30728 | tf_op jit(solution)/shard_map/ppermute | solution.py:33
  19.5 34.1 %collective-permute-start.5 = (f32[1,1,5,512]{3,1,2,0:T(1,128)S(1)}, f32[1,1,5,512]{3,1,2,0:T(1,128)}, u32[]{:S(2)}, u32[]{:S(2)}) collective-permute-start(f32[1,1,5,512]{3,1,2,0:T(1,128)S(1)} %get-tuple-element.1137), channel_id=1, source_target_pairs={{0,4},{4,8},{8,12},{12,16},{16,20},{20,24},{24,28},{28,32},{32,36}... | collective-permute-start | bytes 30728 | tf_op jit(solution)/shard_map/ppermute | solution.py:32
  102.4 10.4 %collective-permute-start = (f32[1,5,512]{2,1,0:T(8,128)S(1)}, f32[1,5,512]{2,1,0:T(8,128)S(1)}, u32[]{:S(2)}, u32[]{:S(2)}) collective-permute-start(f32[1,5,512]{2,1,0:T(8,128)S(1)} %get-tuple-element.1637), channel_id=1, source_target_pairs={{0,4},{4,8},{8,12},{12,16},{16,20},{20,24},{24,28},{28,32},{32,36}... | collective-permute-start | bytes 30728 | tf_op jit(solution)/shard_map/while/body/eval_jaxpr/ppermute | solution.py:22
  112.9 6.3 collective-permute-start
  119.3 6.3 collective-permute-start
  125.6 6.3 collective-permute-start
  131.9 6.3 collective-permute-start
  138.3 6.3 collective-permute-start
  144.6 6.3 collective-permute-start
  150.9 6.3 collective-permute-start
  157.3 6.3 collective-permute-start
  163.6 6.3 collective-permute-start
  169.9 6.3 collective-permute-start
  176.3 6.3 collective-permute-start
  182.6 6.3 collective-permute-start
  189.0 6.3 collective-permute-start
  308.2 7.0 collective-permute-start.1
  466.6 34.3 %collective-permute-start.10 = (f32[1,16,5,1]{3,1,2,0:T(8,128)S(1)}, f32[1,16,5,1]{3,1,2,0:T(8,128)S(1)}, u32[]{:S(2)}, u32[]{:S(2)}) collective-permute-start(f32[1,16,5,1]{3,1,2,0:T(8,128)S(1)} %get-tuple-element.1135), channel_id=1, source_target_pairs={{1,0},{2,1},{3,2},{0,3},{5,4},{6,5},{7,6},{4,7},{9,8},{10,9},{11,1... | collective-permute-start | bytes 968 | tf_op jit(solution)/shard_map/ppermute | solution.py:33
  470.8 30.2 %collective-permute-start.11 = (f32[1,16,5,1]{3,1,2,0:T(8,128)S(1)}, f32[1,16,5,1]{3,1,2,0:T(8,128)S(1)}, u32[]{:S(2)}, u32[]{:S(2)}) collective-permute-start(f32[1,16,5,1]{3,1,2,0:T(8,128)S(1)} %get-tuple-element.1136), channel_id=1, source_target_pairs={{0,1},{1,2},{2,3},{3,0},{4,5},{5,6},{6,7},{7,4},{8,9},{9,10},{10,1... | collective-permute-start | bytes 968 | tf_op jit(solution)/shard_map/ppermute | solution.py:32
  473.7 27.3 %collective-permute-start.8 = (f32[1,1,5,512]{3,1,2,0:T(1,128)S(1)}, f32[1,1,5,512]{3,1,2,0:T(1,128)S(1)}, u32[]{:S(2)}, u32[]{:S(2)}) collective-permute-start(f32[1,1,5,512]{3,1,2,0:T(1,128)S(1)} %get-tuple-element.1134), channel_id=1, source_target_pairs={{4,0},{8,4},{12,8},{16,12},{20,16},{24,20},{28,24},{32,28},{36,32}... | collective-permute-start | bytes 30728 | tf_op jit(solution)/shard_map/ppermute | solution.py:33
  475.6 25.4 %collective-permute-start.9 = (f32[1,1,5,512]{3,1,2,0:T(1,128)S(1)}, f32[1,1,5,512]{3,1,2,0:T(1,128)S(1)}, u32[]{:S(2)}, u32[]{:S(2)}) collective-permute-start(f32[1,1,5,512]{3,1,2,0:T(1,128)S(1)} %get-tuple-element.1133), channel_id=1, source_target_pairs={{0,4},{4,8},{8,12},{12,16},{16,20},{20,24},{24,28},{28,32},{32,36}... | collective-permute-start | bytes 30728 | tf_op jit(solution)/shard_map/ppermute | solution.py:32
  549.0 10.3 %collective-permute-start.2 = (f32[1,5,512]{2,1,0:T(8,128)S(1)}, f32[1,5,512]{2,1,0:T(8,128)S(1)}, u32[]{:S(2)}, u32[]{:S(2)}) collective-permute-start(f32[1,5,512]{2,1,0:T(8,128)S(1)} %get-tuple-element.1796), channel_id=1, source_target_pairs={{0,4},{4,8},{8,12},{12,16},{16,20},{20,24},{24,28},{28,32},{32,36}... | collective-permute-start | bytes 30728 | tf_op jit(solution)/shard_map/while/body/eval_jaxpr/ppermute | solution.py:22
  584.7 6.3 collective-permute-start.2
  591.1 6.3 collective-permute-start.2
  622.7 6.3 collective-permute-start.2
  629.1 6.3 collective-permute-start.2
  635.4 6.3 collective-permute-start.2
  754.6 6.8 collective-permute-start.3
  (48 other events, 773.0 us)
Sparse Core Ops, SparseCore 0:
  9.4 42.5 all-gather.2
  465.8 33.5 all-gather.4
where the time goes:
time: 930 us; the launch traced here: 919 us
  loops' own time  258 us (28%)
  starting transfers between devices  255 us (27%)
  waiting for transfers between devices  200 us (22%)
  other arithmetic  105 us (11%)
  local copies, waits for them, and re-layouts  87.3 us (9%)
  between operations  14 us (2%)
    another operation x8, loops' own time, run_chain(): (last, total), values = lax.scan(advance, (start, total_init), order)  256 us
    ppermute x60, starting transfers between devices, shifted(): lax.ppermute(value, axis, [(source, source + steps) for source in range(i...  228 us
    ppermute x60, waiting for transfers between devices, shifted(): lax.ppermute(value, axis, [(source, source + steps) for source in range(i...  156 us
    dynamic_slice x128, local copies, waits for them, and re-layouts, run_chain(): (last, total), values = lax.scan(advance, (start, total_init), order)  75.1 us
    reduce_sum x188, other arithmetic, cell_apply(): return jnp.sum(matrix * vector[:, None, :, :], axis=2)  74.5 us
    all_gather x2, waiting for transfers between devices, time_term(): piece = lax.all_gather(state, 'inst', axis=0, tiled=True)  42.8 us
  transfers between devices with their start and end apart: 70, of which 62 were waited for; matrix products, arithmetic and copies ran while one was open for 1% of the time, Pallas kernels for 0%

commit v1 on v0

v1 whole, which is shorter than its diff:
```python
import math

import jax
import jax.numpy as jnp
import numpy as np
from jax import lax
from jax.experimental import pallas as pl
from jax.experimental.pallas import tpu as pltpu
from jax.sharding import PartitionSpec as P

INST = 8
SWEEPS = 2
VARS = 5
STEPS = 8
TILES = 4
SEGMENTS = 16
F32 = jnp.float32
FIELD = STEPS * VARS * 8
MATRIX = STEPS * VARS * VARS * 8
FULL_GROUPS = 24
VEC_GROUPS = 4


def spectral():
    index = np.arange(INST)
    diff = index[:, None] - index[None, :]
    sign = 1.0 - 2.0 * np.mod(diff, 2)
    safe = np.where(diff == 0, 0.5 * math.pi, math.pi * diff / INST)
    first = np.where(diff == 0, 0.0, 0.5 * sign * np.cos(safe) / np.sin(safe))
    second = np.where(diff == 0, -(INST * INST + 2.0) / 12.0, -0.5 * sign / np.sin(safe) ** 2)
    return first - 0.5 * second


def iotas():
    sub = lax.broadcasted_iota(jnp.int32, (8, 128), 0)
    lane = lax.broadcasted_iota(jnp.int32, (8, 128), 1)
    return sub, lane


def row(ref, index):
    return ref[pl.ds(pl.multiple_of(index * 8, 8), 8), :]


def rows(ref, start, count):
    return [row(ref, start + n) for n in range(count)]


def put(ref, index, value):
    ref[pl.ds(pl.multiple_of(index * 8, 8), 8), :] = value


def total(terms):
    terms = list(terms)
    while len(terms) > 1:
        terms = [terms[n] + terms[n + 1] if n + 1 < len(terms) else terms[n] for n in range(0, len(terms), 2)]
    return terms[0]


def matvec(m, v):
    return [total(m[i * VARS + j] * v[j] for j in range(VARS)) for i in range(VARS)]


def matmul(a, b):
    return [
        total(a[i * VARS + j] * b[j * VARS + m] for j in range(VARS))
        for i in range(VARS)
        for m in range(VARS)
    ]


def plus(a, b):
    return [x + y for x, y in zip(a, b)]


def minus(a, b):
    return [x - y for x, y in zip(a, b)]


def swap(a):
    return [pltpu.roll(x, 4, 0) for x in a]


def pick(mask, a, b):
    return [jnp.where(mask, x, y) for x, y in zip(a, b)]


def lane_roll(x, shift):
    shift = shift % 128
    return x if shift == 0 else pltpu.roll(x, shift, 1)


def blocks4(block, parts):
    out = parts[0]
    for p in range(1, 4):
        out = jnp.where(block == p, parts[p], out)
    return out


def pack_lines(out_ref, block, values, first, groups):
    for g in range((len(values) + 3) // 4):
        four = [values[min(4 * g + p, len(values) - 1)] for p in range(4)]
        for q in range(4):
            chunk = blocks4(block, [lane_roll(four[p], 32 * (p - q)) for p in range(4)])
            out_ref[pl.ds(q * groups + first + g, 4, stride=4 * groups), :] = chunk[:4]


def edge_lines(sub, lane, u, last_ref, first_ref):
    last = jnp.zeros((8, 128), F32)
    initial = jnp.zeros((8, 128), F32)
    for n in range(STEPS * VARS):
        last = jnp.where(lane == n, lane_roll(u[n], n - 127), last)
        initial = jnp.where(lane == n, lane_roll(u[n], n), initial)
    last_ref[...] = pltpu.roll(last, 5, 0)
    first_ref[...] = pltpu.roll(initial, 3, 0)


def field_to_packed(raw_ref, out_ref):
    for k in range(2 * STEPS):
        for t in range(TILES):
            start = (k % STEPS) * VARS * 8 + (k // STEPS) * TILES + t
            out_ref[pl.ds(start, VARS, stride=8), :] = raw_ref[k, :, t * 128 : (t + 1) * 128]


def pack_kernel(state_ref, u_ref, last_ref, first_ref):
    sub, lane = iotas()
    field_to_packed(state_ref, u_ref)
    edge_lines(sub, lane, rows(u_ref, 0, STEPS * VARS), last_ref, first_ref)


def maps_kernel(
    u_ref, source_ref, flags_ref, pivot_raw, coupling_raw, back_raw,
    src_ref, keep_ref, pivot_ref, coupling_ref, back_ref, halves_ref, packed_ref, up_ref,
    prefix_ref,
):
    sub, lane = iotas()
    block = lane // 32
    field_to_packed(source_ref, src_ref)
    for k in range(2 * STEPS):
        for t in range(TILES):
            start = (k % STEPS) * 8 + (k // STEPS) * TILES + t
            keep_ref[start : start + 1, :] = (1 - flags_ref[k : k + 1, t * 128 : (t + 1) * 128]).astype(F32)

    def relayout(k, carry):
        for raw, out in ((pivot_raw, pivot_ref), (coupling_raw, coupling_ref), (back_raw, back_ref)):
            for half in range(2):
                for i in range(VARS):
                    for t in range(TILES):
                        start = (k * VARS + i) * VARS * 8 + half * TILES + t
                        out[pl.ds(start, VARS, stride=8), :] = raw[k + half * STEPS, i, :, t * 128 : (t + 1) * 128]
        return carry

    lax.fori_loop(0, STEPS, relayout, 0)
    size = VARS * VARS

    def forward(k, p):
        p = [-x for x in matmul(rows(coupling_ref, k * size, size), p)]
        for n in range(size):
            put(prefix_ref, k * size + n, p[n])
        return p

    first = [-x for x in rows(coupling_ref, 0, size)]
    for n in range(size):
        put(prefix_ref, n, first[n])
    ahead = lax.fori_loop(1, STEPS, forward, first)

    def backward(step, carry):
        k = STEPS - 2 - step
        return minus(rows(prefix_ref, k * size, size), matmul(rows(back_ref, k * size, size), carry))

    mixed = lax.fori_loop(0, STEPS - 1, backward, ahead)

    def behind_step(step, carry):
        k = STEPS - 2 - step
        return [-x for x in matmul(rows(back_ref, k * size, size), carry)]

    behind = lax.fori_loop(0, STEPS - 1, behind_step, [-x for x in rows(back_ref, (STEPS - 1) * size, size)])
    for n in range(size):
        put(halves_ref, n, ahead[n])
        put(halves_ref, size + n, mixed[n])
        put(halves_ref, 2 * size + n, behind[n])
    whole_ahead = matmul(swap(ahead), ahead)
    for n in range(size):
        put(prefix_ref, n, whole_ahead[n])
    whole_mixed = plus(mixed, matmul(behind, matmul(swap(mixed), ahead)))
    for n in range(size):
        put(prefix_ref, size + n, whole_mixed[n])
    whole_behind = matmul(behind, swap(behind))
    for n in range(size):
        put(prefix_ref, 2 * size + n, whole_behind[n])
    pack_lines(packed_ref, block, rows(prefix_ref, 0, 3 * size), VEC_GROUPS, FULL_GROUPS)
    up_ref[: VARS * 8, :] = u_ref[(STEPS - 1) * VARS * 8 :, :]
    up_ref[VARS * 8 :, :] = back_ref[(STEPS - 1) * size * 8 :, :]


def time_kernel(weights, u_ref, out_ref):
    for v in range(VARS):
        fields = [row(u_ref, j * VARS + v) for j in range(INST)]
        for i in range(INST):
            put(out_ref, i * VARS + v, total(fields[j] * F32(weights[i, j]) for j in range(INST)))


def stencil_kernel(u_ref, src_ref, below_ref, above_ref, left_ref, right_ref, out_ref):
    sub, lane = iotas()
    top = sub < TILES
    left_all = left_ref[...]
    right_all = right_ref[...]
    for k in range(STEPS):
        for v in range(VARS):
            n = k * VARS + v
            u = row(u_ref, n)
            if k == 0:
                below = pltpu.roll(jnp.where(top, row(u_ref, (STEPS - 1) * VARS + v), row(below_ref, v)), 4, 0)
            else:
                below = row(u_ref, n - VARS)
            if k == STEPS - 1:
                above = pltpu.roll(jnp.where(top, row(above_ref, v), row(u_ref, v)), 4, 0)
            else:
                above = row(u_ref, n + VARS)
            turned = pltpu.roll(u, 1, 1)
            edge = jnp.where(sub % TILES == 0, lane_roll(left_all, -n), pltpu.roll(turned, 1, 0))
            left = jnp.where(lane == 0, edge, turned)
            turned = pltpu.roll(u, 127, 1)
            edge = jnp.where(sub % TILES == TILES - 1, lane_roll(right_all, 127 - n), pltpu.roll(turned, 7, 0))
            right = jnp.where(lane == 127, edge, turned)
            value = row(src_ref, n) - 0.1 * above + 0.5 * below - 0.8 * u + 0.2 * (left + right)
            put(out_ref, n, value)


def local_kernel(base_ref, time_ref, keep_ref, pivot_ref, coupling_ref, back_ref, halves_ref, *rest):
    if len(rest) == 5:
        maps_ref, source_ref, ends_ref, packed_ref, y_ref = rest
        groups = FULL_GROUPS
        packed_ref[...] = maps_ref[...]
    else:
        source_ref, ends_ref, packed_ref, y_ref = rest
        groups = VEC_GROUPS
    sub, lane = iotas()
    block = lane // 32
    size = VARS * VARS

    def source_step(k, carry):
        keep = row(keep_ref, k)
        rhs = [keep * (row(base_ref, k * VARS + v) + row(time_ref, k * VARS + v)) for v in range(VARS)]
        for v, value in enumerate(matvec(rows(pivot_ref, k * size, size), rhs)):
            put(source_ref, k * VARS + v, value)
        return carry

    lax.fori_loop(0, STEPS, source_step, 0)
    y = rows(source_ref, 0, VARS)
    kept = [y]
    for k in range(1, STEPS):
        y = minus(rows(source_ref, k * VARS, VARS), matvec(rows(coupling_ref, k * size, size), y))
        kept.append(y)
    end = y
    x = y
    for k in range(STEPS - 2, -1, -1):
        x = minus(kept[k], matvec(rows(back_ref, k * size, size), x))
    for v in range(VARS):
        put(ends_ref, v, end[v])
        put(ends_ref, VARS + v, x[v])
    ahead = rows(halves_ref, 0, size)
    mixed = rows(halves_ref, size, size)
    behind = rows(halves_ref, 2 * size, size)
    whole_end = plus(swap(end), matvec(swap(ahead), end))
    inner = plus(swap(x), matvec(swap(mixed), end))
    whole_first = plus(x, matvec(behind, inner))
    values = whole_end + whole_first + [jnp.zeros((8, 128), F32)] * (4 * VEC_GROUPS - 2 * VARS)
    pack_lines(packed_ref, block, values, 0, groups)


def shift_in(sub, values, entry):
    return [jnp.where(sub == 0, e, pltpu.roll(x, 1, 0)) for x, e in zip(values, entry)]


def shift_out(sub, values, entry):
    return [jnp.where(sub == 7, e, pltpu.roll(x, 7, 0)) for x, e in zip(values, entry)]


def reduced_kernel(first, recv_ref, maps_in_ref, out_ref, *rest):
    sub, lane = iotas()
    block = lane // 32
    size = VARS * VARS
    groups = FULL_GROUPS if first else VEC_GROUPS

    def value(r, part):
        stacked = recv_ref[pl.ds(part * 8 * groups + r // 4, 8, stride=groups), :]
        return lane_roll(stacked, -32 * (r % 4))

    if first:
        maps_ref = rest[0]
        for r in range(3 * size):
            for part in range(2):
                put(maps_ref, part * 3 * size + r, value(4 * VEC_GROUPS + r, part))
    else:
        maps_ref = maps_in_ref
    zero = [jnp.zeros((8, 128), F32)] * VARS

    def solve(part, which, source, entry, shift):
        maps = rows(maps_ref, part * 3 * size + which * size, size)

        def step(_, now):
            return plus(source, matvec(maps, shift(sub, now, entry)))

        out = lax.fori_loop(0, 7, step, plus(source, matvec(maps, shift(sub, zero, entry))))
        return out, shift(sub, out, entry)

    ends = [[value(r, part) for r in range(VARS)] for part in range(2)]
    firsts = [[value(VARS + r, part) for r in range(VARS)] for part in range(2)]
    out, low_entry = solve(0, 0, ends[0], zero, shift_in)
    out, high_entry = solve(1, 0, ends[1], [pltpu.roll(x, 1, 0) for x in out], shift_in)
    entries = [low_entry, high_entry]
    drive = [
        plus(firsts[part], matvec(rows(maps_ref, part * 3 * size + size, size), entries[part])) for part in range(2)
    ]
    out, high_next = solve(1, 2, drive[1], zero, shift_out)
    out, low_next = solve(0, 2, drive[0], [pltpu.roll(x, 7, 0) for x in out], shift_out)
    nexts = [low_next, high_next]
    for part in range(2):
        values = entries[part] + nexts[part] + zero + zero[:1]
        for g in range(VEC_GROUPS):
            packed = blocks4(block, [lane_roll(values[4 * g + p], 32 * p) for p in range(4)])
            out_ref[pl.ds(part * 8 * VEC_GROUPS + g, 8, stride=VEC_GROUPS), :] = packed


def finish_kernel(
    last, recv_ref, u_ref, source_ref, ends_ref, coupling_ref, back_ref, halves_ref, *rest
):
    if last:
        out_ref, new_ref = rest
    else:
        up_ref, above_ref, new_ref, last_ref, first_ref, new_below_ref, new_above_ref = rest
    sub, lane = iotas()
    block = lane // 32
    top = sub < TILES
    size = VARS * VARS
    stacked = [
        [
            recv_ref[pl.ds(q * VEC_GROUPS + g, TILES, stride=4 * VEC_GROUPS), :]
            for g in range((2 * VARS + 3) // 4)
        ]
        for q in range(4)
    ]
    stacked = [[jnp.concatenate([x, x], axis=0) for x in line] for line in stacked]

    def value(r):
        return blocks4(block, [lane_roll(stacked[q][r // 4], 32 * (q - r % 4)) for q in range(4)])

    entry = [value(r) for r in range(VARS)]
    after = [value(VARS + r) for r in range(VARS)]
    end = rows(ends_ref, 0, VARS)
    begin = rows(ends_ref, VARS, VARS)
    middle = plus(end, matvec(rows(halves_ref, 0, size), entry))
    start = pick(top, entry, swap(middle))
    follow = plus(
        plus(begin, matvec(rows(halves_ref, size, size), start)),
        matvec(rows(halves_ref, 2 * size, size), after),
    )
    finish = pick(top, swap(follow), after)
    y = start
    kept = []
    for k in range(STEPS):
        y = minus(rows(source_ref, k * VARS, VARS), matvec(rows(coupling_ref, k * size, size), y))
        kept.append(y)
    x = finish
    for k in range(STEPS - 1, -1, -1):
        x = minus(kept[k], matvec(rows(back_ref, k * size, size), x))
        for v in range(VARS):
            put(new_ref, k * VARS + v, row(u_ref, k * VARS + v) + x[v])
    if last:
        for k in range(2 * STEPS):
            for t in range(TILES):
                begin_row = (k % STEPS) * VARS * 8 + (k // STEPS) * TILES + t
                out_ref[k, :, t * 128 : (t + 1) * 128] = new_ref[pl.ds(begin_row, VARS, stride=8), :]
    else:
        edge_lines(sub, lane, rows(new_ref, 0, STEPS * VARS), last_ref, first_ref)
        before = minus(entry, matvec(rows(up_ref, VARS, size), swap(x)))
        for v in range(VARS):
            put(new_below_ref, v, row(up_ref, v) + before[v])
            put(new_above_ref, v, row(above_ref, v) + after[v])


def call(kernel, shapes, *args, scratch=(), flops=100_000, limit=24):
    outs = [jax.ShapeDtypeStruct(shape, F32) for shape in shapes]
    moved = 4 * (sum(math.prod(shape) for shape in shapes) + sum(a.size for a in args))
    return pl.pallas_call(
        kernel,
        out_shape=outs,
        scratch_shapes=[pltpu.VMEM(shape, F32) for shape in scratch],
        cost_estimate=pl.CostEstimate(flops=flops, bytes_accessed=moved, transcendentals=0),
        compiler_params=pltpu.CompilerParams(vmem_limit_bytes=limit * 1024 * 1024),
    )(*args)


def exchange(value, axis, count):
    shape = value.shape
    out = lax.all_to_all(value.reshape(count, shape[0] // count, 128), axis, 0, 0)
    return out.reshape(shape)


def moved(value, axis, step, wrap):
    count = lax.axis_size(axis)
    pairs = [(i, (i + step) % count) for i in range(count) if wrap or 0 <= i + step < count]
    return lax.ppermute(value, axis, pairs)


def body(state, source_terms, pivot_inverse, coupling, back_coupling, wall_flags):
    weights = np.float32(-0.5 * spectral())
    edge = (8, 128)
    u, last_line, first_line = call(pack_kernel, [(FIELD, 128), edge, edge], state[0])
    src, keep, pivot, forth, back, halves, packed_maps, up = call(
        maps_kernel,
        [
            (FIELD, 128), (STEPS * 8, 128), (MATRIX, 128), (MATRIX, 128), (MATRIX, 128),
            (3 * VARS * VARS * 8, 128), (SEGMENTS * FULL_GROUPS, 128), ((VARS + VARS * VARS) * 8, 128),
        ],
        u, source_terms[0], wall_flags, pivot_inverse[0], coupling[0], back_coupling[0],
        scratch=[(MATRIX, 128)],
        flops=8_000_000,
    )
    above = below = None
    maps = None
    for sweep in range(SWEEPS):
        first = sweep == 0
        left = moved(last_line, "span", 1, True)
        right = moved(first_line, "span", -1, True)
        if first:
            up = moved(up, "axial", 1, False)
            above = moved(u[: VARS * 8], "axial", -1, False)
            below = up[: VARS * 8]
        spread = exchange(u, "inst", INST)
        (term,) = call(lambda *refs: time_kernel(weights, *refs), [(FIELD, 128)], spread)
        time = exchange(term, "inst", INST)
        (base,) = call(stencil_kernel, [(FIELD, 128)], u, src, below, above, left, right)
        groups = FULL_GROUPS if first else VEC_GROUPS
        source, ends, packed = call(
            local_kernel,
            [(FIELD, 128), (2 * VARS * 8, 128), (SEGMENTS * groups, 128)],
            base, time, keep, pivot, forth, back, halves, *((packed_maps,) if first else ()),
            scratch=[(8, 128)],
        )
        recv = exchange(packed, "axial", SEGMENTS)
        shapes = [(SEGMENTS * VEC_GROUPS, 128)]
        if first:
            shapes.append((6 * VARS * VARS * 8, 128))
        out = call(
            lambda *refs, f=first: reduced_kernel(f, *((refs[0], None) + refs[1:] if f else refs)),
            shapes, recv, *(() if first else (maps,)),
        )
        if first:
            maps = out[1]
        back_recv = exchange(out[0], "axial", SEGMENTS)
        last = sweep == SWEEPS - 1
        common = (back_recv, u, source, ends, forth, back, halves)
        if last:
            (result,) = call(
                lambda *refs: finish_kernel(True, *refs), [(2 * STEPS, VARS, TILES * 128)], *common,
                scratch=[(FIELD, 128)],
            )
        else:
            halo = (VARS * 8, 128)
            u, last_line, first_line, below, above = call(
                lambda *refs: finish_kernel(False, *refs), [(FIELD, 128), edge, edge, halo, halo],
                *common, up, above,
            )
    return result[None]


def solution(mesh):
    return jax.shard_map(
        body,
        mesh=mesh,
        in_specs=(
            P("inst", "axial", None, "span"),
            P("inst", "axial", None, "span"),
            P("inst", "axial", None, None, "span"),
            P("inst", "axial", None, None, "span"),
            P("inst", "axial", None, None, "span"),
            P("axial", "span"),
        ),
        out_specs=P("inst", "axial", None, "span"),
        check_vma=False,
    )
```

time: 930 us -> 134 us (0.14)
  the two profiles are of different devices: /device:TPU:25 before, /device:TPU:1 now
where the time goes in v1:
time: 134 us; the launch traced here: 133 us
  blocking collectives  87.9 us (66%)
  starting transfers between devices  27.3 us (20%)
  local copies, waits for them, and re-layouts  8.52 us (6%)
  Pallas kernels  6.61 us (5%)
  waiting for transfers between devices  2.2 us (2%)
    all_to_all x6, blocking collectives, exchange(): lax.all_to_all(value.reshape(count, shape[0] // count, 128), axis, 0, 0)  87.9 us
    ppermute x6, starting transfers between devices, moved(): return lax.ppermute(value, axis, pairs)  20.6 us
    all_to_all x2, starting transfers between devices, exchange(): lax.all_to_all(value.reshape(count, shape[0] // count, 128), axis, 0, 0)  6.76 us
    unnamed x39, local copies, waits for them, and re-layouts  6.73 us
    pallas_call x12, Pallas kernels, call(): pl.pallas_call(kernel, out_shape=outs, scratch_shapes=[pltpu.VMEM(shape,...  6.61 us
  transfers between devices with their start and end apart: 8, of which 2 were waited for; matrix products, arithmetic and copies ran while one was open for 1% of the time, Pallas kernels for 2%

profile of v1, /device:TPU:1, one launch (start us, length us, event | category | flops | bytes accessed | tf_op | source)
XLA Modules:
  0.0 132.9 jit_solution(17231664539880928017)
XLA Ops:
  0.0 1.1 copy.20
  1.3 18.8 %all_to_all.40 = f32[8,40,128]{2,1,0:T(8,128)S(1)} all-to-all(f32[8,40,128]{2,1,0:T(8,128)S(1)} %bitcast.31), channel_id=1, replica_groups=mesh['inst'=8,'axial'=16,'span'=4] {'inst'}, dimensions={0} | all-to-all | bytes 327680 | tf_op jit(solution)/shard_map/all_to_all | solution.py:396
  20.1 0.7 shard_map.67
  20.9 3.4 %all-to-all-start.1 = ((f32[8,40,128]{2,1,0:T(8,128)}), f32[8,40,128]{2,1,0:T(8,128)S(1)}, u32[]{:S(2)}, u32[]{:S(2)}) async-start(f32[8,40,128]{2,1,0:T(8,128)} %bitcast.7), calls=%async_computation.1 | async-start | bytes 327680 | tf_op jit(solution)/shard_map/all_to_all | solution.py:396
  24.3 1.0 copy_bitcast_fusion
  25.4 0.5 copy.18
  25.9 0.4 copy-done.17
  26.5 2.0 %shard_map.65 = (f32[320,128]{1,0:T(8,128)S(1)}, f32[64,128]{1,0:T(8,128)S(1)}, f32[1600,128]{1,0:T(8,128)S(1)}, f32[1600,128]{1,0:T(8,128)S(1)}, f32[1600,128]{...) custom-call(f32[320,128]{1,0:T(8,128)S(1)} %get-tuple-element.29.u_ref.refs_1_, ...), custom_call_target="tpu_custom_call" | custom-call | flops 8000000 | bytes 6098944 | tf_op jit(solution)/shard_map/pallas_call | solution.py:385
  28.5 0.7 copy-done.2
  29.1 5.7 %collective-permute-start = (f32[240,128]{1,0:T(8,128)S(1)}, f32[240,128]{1,0:T(8,128)S(1)}, u32[]{:S(2)}, u32[]{:S(2)}) collective-permute-start(f32[240,128]{1,0:T(8,128)S(1)} %get-tuple-element.31), channel_id=1, source_target_pairs={{0,4},{4,8},{8,12},{12,16},{16,20},{20,24},{24,28},{28,32},{32,36}... | collective-permute-start | bytes 368648 | tf_op jit(solution)/shard_map/ppermute | solution.py:403
  34.8 1.9 %collective-permute-start.1 = (f32[40,128]{1,0:T(8,128)S(1)}, f32[40,128]{1,0:T(8,128)S(1)}, u32[]{:S(2)}, u32[]{:S(2)}) collective-permute-start(f32[40,128]{1,0:T(8,128)S(1)} %slice.7), channel_id=1, source_target_pairs={{4,0},{8,4},{12,8},{16,12},{20,16},{24,20},{28,24},{32,28},{36,32}... | collective-permute-start | bytes 61448 | tf_op jit(solution)/shard_map/ppermute | solution.py:403
  36.8 3.1 %collective-permute-start.2 = (f32[8,128]{1,0:T(8,128)S(1)}, f32[8,128]{1,0:T(8,128)S(1)}, u32[]{:S(2)}, u32[]{:S(2)}) collective-permute-start(f32[8,128]{1,0:T(8,128)S(1)} %get-tuple-element.32), channel_id=1, source_target_pairs={{0,1},{1,2},{2,3},{3,0},{4,5},{5,6},{6,7},{7,4},{8,9},{9,10},{10,1... | collective-permute-start | bytes 12296 | tf_op jit(solution)/shard_map/ppermute | solution.py:403
  39.9 3.4 %collective-permute-start.3 = (f32[8,128]{1,0:T(8,128)S(1)}, f32[8,128]{1,0:T(8,128)S(1)}, u32[]{:S(2)}, u32[]{:S(2)}) collective-permute-start(f32[8,128]{1,0:T(8,128)S(1)} %get-tuple-element.33), channel_id=1, source_target_pairs={{0,3},{1,0},{2,1},{3,2},{4,7},{5,4},{6,5},{7,6},{8,11},{9,8},{10,9... | collective-permute-start | bytes 12296 | tf_op jit(solution)/shard_map/ppermute | solution.py:403
  43.3 0.9 collective-permute-done.3.right_ref
  44.5 0.6 copy-done.7
  45.1 0.9 copy-done.3
  46.0 0.8 copy-done.5
  47.1 20.4 %all_to_all.41 = f32[16,24,128]{2,1,0:T(8,128)S(1)} all-to-all(f32[16,24,128]{2,1,0:T(8,128)S(1)} %bitcast.41), channel_id=1, replica_groups=mesh['inst'=8,'axial'=16,'span'=4] {'axial'}, dimensions={0} | all-to-all | bytes 393216 | tf_op jit(solution)/shard_map/all_to_all | solution.py:396
  67.6 0.7 shard_map.69
  68.2 10.1 %all_to_all.42 = f32[16,4,128]{2,1,0:T(4,128)S(1)} all-to-all(f32[16,4,128]{2,1,0:T(4,128)S(1)} %bitcast.47), channel_id=1, replica_groups=mesh['inst'=8,'axial'=16,'span'=4] {'axial'}, dimensions={0} | all-to-all | bytes 65536 | tf_op jit(solution)/shard_map/all_to_all | solution.py:396
  78.7 15.2 %all_to_all.43 = f32[8,40,128]{2,1,0:T(8,128)S(1)} all-to-all(f32[8,40,128]{2,1,0:T(8,128)S(1)} %bitcast.32), channel_id=1, replica_groups=mesh['inst'=8,'axial'=16,'span'=4] {'inst'}, dimensions={0} | all-to-all | bytes 327680 | tf_op jit(solution)/shard_map/all_to_all | solution.py:396
  93.9 0.7 shard_map.72
  94.6 3.4 %all-to-all-start.5 = ((f32[8,40,128]{2,1,0:T(8,128)}), f32[8,40,128]{2,1,0:T(8,128)S(1)}, u32[]{:S(2)}, u32[]{:S(2)}) async-start(f32[8,40,128]{2,1,0:T(8,128)} %bitcast.15), calls=%async_computation.5 | async-start | bytes 327680 | tf_op jit(solution)/shard_map/all_to_all | solution.py:396
  98.0 3.1 %collective-permute-start.4 = (f32[8,128]{1,0:T(8,128)S(1)}, f32[8,128]{1,0:T(8,128)S(1)}, u32[]{:S(2)}, u32[]{:S(2)}) collective-permute-start(f32[8,128]{1,0:T(8,128)S(1)} %get-tuple-element.47), channel_id=1, source_target_pairs={{0,1},{1,2},{2,3},{3,0},{4,5},{5,6},{6,7},{7,4},{8,9},{9,10},{10,1... | collective-permute-start | bytes 12296 | tf_op jit(solution)/shard_map/ppermute | solution.py:403
  101.2 3.4 %collective-permute-start.5 = (f32[8,128]{1,0:T(8,128)S(1)}, f32[8,128]{1,0:T(8,128)S(1)}, u32[]{:S(2)}, u32[]{:S(2)}) collective-permute-start(f32[8,128]{1,0:T(8,128)S(1)} %get-tuple-element.48), channel_id=1, source_target_pairs={{0,3},{1,0},{2,1},{3,2},{4,7},{5,4},{6,5},{7,6},{8,11},{9,8},{10,9... | collective-permute-start | bytes 12296 | tf_op jit(solution)/shard_map/ppermute | solution.py:403
  104.6 1.2 collective-permute-done.5.right_ref
  105.8 0.7 copy-done.11
  106.5 0.7 copy-done.13
  107.9 13.2 %all_to_all.44 = f32[16,4,128]{2,1,0:T(4,128)S(1)} all-to-all(f32[16,4,128]{2,1,0:T(4,128)S(1)} %bitcast.46), channel_id=1, replica_groups=mesh['inst'=8,'axial'=16,'span'=4] {'axial'}, dimensions={0} | all-to-all | bytes 65536 | tf_op jit(solution)/shard_map/all_to_all | solution.py:396
  121.0 0.5 shard_map.74
  121.6 10.3 %all_to_all.45 = f32[16,4,128]{2,1,0:T(4,128)S(1)} all-to-all(f32[16,4,128]{2,1,0:T(4,128)S(1)} %bitcast.45), channel_id=1, replica_groups=mesh['inst'=8,'axial'=16,'span'=4] {'axial'}, dimensions={0} | all-to-all | bytes 65536 | tf_op jit(solution)/shard_map/all_to_all | solution.py:396
  132.1 0.8 copy.12
  (45 shorter events, 2.2 us)
Async XLA Ops:
  0.0 24.3 %copy-start.15 = (f32[1,16,5,5,512]{4,1,3,2,0:T(8,128)S(1)}, f32[1,16,5,5,512]{4,1,3,2,0:T(8,128)}, u32[]{:S(2)}) copy-start(f32[1,16,5,5,512]{4,1,3,2,0:T(8,128)} %param.10) | copy-start | bytes 2457604
  0.0 24.3 %copy-start.16 = (f32[1,16,5,5,512]{4,1,3,2,0:T(8,128)S(1)}, f32[1,16,5,5,512]{4,1,3,2,0:T(8,128)}, u32[]{:S(2)}) copy-start(f32[1,16,5,5,512]{4,1,3,2,0:T(8,128)} %param.9) | copy-start | bytes 2457604
  20.9 24.2 %all-to-all-start.1 = ((f32[8,40,128]{2,1,0:T(8,128)}), f32[8,40,128]{2,1,0:T(8,128)S(1)}, u32[]{:S(2)}, u32[]{:S(2)}) async-start(f32[8,40,128]{2,1,0:T(8,128)} %bitcast.7), calls=%async_computation.1 | async-start | bytes 327680 | tf_op jit(solution)/shard_map/all_to_all | solution.py:396
  24.3 1.1 copy-start.14
  25.4 0.9 copy-start.17
  25.4 1.0 copy-start.9
  28.5 0.7 copy-start.2
  29.1 15.1 %copy-start.4 = (f32[64,128]{1,0:T(8,128)}, f32[64,128]{1,0:T(8,128)S(1)}, u32[]{:S(2)}) copy-start(f32[64,128]{1,0:T(8,128)S(1)} %get-tuple-element.34.keep_ref) | copy-start | bytes 98308
  29.1 14.1 %collective-permute-start = (f32[240,128]{1,0:T(8,128)S(1)}, f32[240,128]{1,0:T(8,128)S(1)}, u32[]{:S(2)}, u32[]{:S(2)}) collective-permute-start(f32[240,128]{1,0:T(8,128)S(1)} %get-tuple-element.31), channel_id=1, source_target_pairs={{0,4},{4,8},{8,12},{12,16},{16,20},{20,24},{24,28},{28,32},{32,36}... | collective-permute-start | bytes 368648 | tf_op jit(solution)/shard_map/ppermute | solution.py:403
  34.8 9.4 %collective-permute-start.1 = (f32[40,128]{1,0:T(8,128)S(1)}, f32[40,128]{1,0:T(8,128)S(1)}, u32[]{:S(2)}, u32[]{:S(2)}) collective-permute-start(f32[40,128]{1,0:T(8,128)S(1)} %slice.7), channel_id=1, source_target_pairs={{4,0},{8,4},{12,8},{16,12},{20,16},{24,20},{28,24},{32,28},{36,32}... | collective-permute-start | bytes 61448 | tf_op jit(solution)/shard_map/ppermute | solution.py:403
  36.8 6.5 %collective-permute-start.2 = (f32[8,128]{1,0:T(8,128)S(1)}, f32[8,128]{1,0:T(8,128)S(1)}, u32[]{:S(2)}, u32[]{:S(2)}) collective-permute-start(f32[8,128]{1,0:T(8,128)S(1)} %get-tuple-element.32), channel_id=1, source_target_pairs={{0,1},{1,2},{2,3},{3,0},{4,5},{5,6},{6,7},{7,4},{8,9},{9,10},{10,1... | collective-permute-start | bytes 12296 | tf_op jit(solution)/shard_map/ppermute | solution.py:403
  39.9 4.4 %collective-permute-start.3 = (f32[8,128]{1,0:T(8,128)S(1)}, f32[8,128]{1,0:T(8,128)S(1)}, u32[]{:S(2)}, u32[]{:S(2)}) collective-permute-start(f32[8,128]{1,0:T(8,128)S(1)} %get-tuple-element.33), channel_id=1, source_target_pairs={{0,3},{1,0},{2,1},{3,2},{4,7},{5,4},{6,5},{7,6},{8,11},{9,8},{10,9... | collective-permute-start | bytes 12296 | tf_op jit(solution)/shard_map/ppermute | solution.py:403
  44.5 0.6 copy-start.7
  45.1 0.9 copy-start.3
  46.0 0.8 copy-start.5
  46.8 31.5 %copy-start.8 = (f32[40,128]{1,0:T(8,128)S(1)}, f32[40,128]{1,0:T(8,128)}, u32[]{:S(2)}) copy-start(f32[40,128]{1,0:T(8,128)} %copy-done.7) | copy-start | bytes 61444
  68.2 25.7 %copy-start = (f32[1200,128]{1,0:T(8,128)}, f32[1200,128]{1,0:T(8,128)S(1)}, u32[]{:S(2)}) copy-start(f32[1200,128]{1,0:T(8,128)S(1)} %get-tuple-element.50.refs_1_) | copy-start | bytes 1843204
  78.6 16.0 %copy-start.10 = (f32[40,128]{1,0:T(8,128)}, f32[40,128]{1,0:T(8,128)S(1)}, u32[]{:S(2)}) copy-start(f32[40,128]{1,0:T(8,128)S(1)} %get-tuple-element.45.below_ref) | copy-start | bytes 61444
  78.7 27.1 %copy-start.12 = (f32[40,128]{1,0:T(8,128)}, f32[40,128]{1,0:T(8,128)S(1)}, u32[]{:S(2)}) copy-start(f32[40,128]{1,0:T(8,128)S(1)} %get-tuple-element.46.above_ref) | copy-start | bytes 61444
  78.7 28.8 %copy-start.6 = (f32[64,128]{1,0:T(8,128)S(1)}, f32[64,128]{1,0:T(8,128)}, u32[]{:S(2)}) copy-start(f32[64,128]{1,0:T(8,128)} %copy-done.4) | copy-start | bytes 98308
  94.6 12.9 %all-to-all-start.5 = ((f32[8,40,128]{2,1,0:T(8,128)}), f32[8,40,128]{2,1,0:T(8,128)S(1)}, u32[]{:S(2)}, u32[]{:S(2)}) async-start(f32[8,40,128]{2,1,0:T(8,128)} %bitcast.15), calls=%async_computation.5 | async-start | bytes 327680 | tf_op jit(solution)/shard_map/all_to_all | solution.py:396
  98.0 6.5 %collective-permute-start.4 = (f32[8,128]{1,0:T(8,128)S(1)}, f32[8,128]{1,0:T(8,128)S(1)}, u32[]{:S(2)}, u32[]{:S(2)}) collective-permute-start(f32[8,128]{1,0:T(8,128)S(1)} %get-tuple-element.47), channel_id=1, source_target_pairs={{0,1},{1,2},{2,3},{3,0},{4,5},{5,6},{6,7},{7,4},{8,9},{9,10},{10,1... | collective-permute-start | bytes 12296 | tf_op jit(solution)/shard_map/ppermute | solution.py:403
  101.2 4.6 %collective-permute-start.5 = (f32[8,128]{1,0:T(8,128)S(1)}, f32[8,128]{1,0:T(8,128)S(1)}, u32[]{:S(2)}, u32[]{:S(2)}) collective-permute-start(f32[8,128]{1,0:T(8,128)S(1)} %get-tuple-element.48), channel_id=1, source_target_pairs={{0,3},{1,0},{2,1},{3,2},{4,7},{5,4},{6,5},{7,6},{8,11},{9,8},{10,9... | collective-permute-start | bytes 12296 | tf_op jit(solution)/shard_map/ppermute | solution.py:403
  105.8 0.7 copy-start.11
  106.5 0.7 copy-start.13
  107.5 13.5 %copy-start.1 = (f32[1200,128]{1,0:T(8,128)S(1)}, f32[1200,128]{1,0:T(8,128)}, u32[]{:S(2)}) copy-start(f32[1200,128]{1,0:T(8,128)} %copy-done) | copy-start | bytes 1843204

commit v2 on v1

v2 whole, which is shorter than its diff:
```python
import math

import jax
import jax.numpy as jnp
import numpy as np
from jax import lax
from jax.experimental import pallas as pl
from jax.experimental.pallas import tpu as pltpu
from jax.sharding import PartitionSpec as P

INST = 8
SWEEPS = 2
VARS = 5
STEPS = 8
TILES = 4
SEGMENTS = 16
F32 = jnp.float32
FIELD = STEPS * VARS * 8
MATRIX = STEPS * VARS * VARS * 8
SIZE = VARS * VARS
MAP_BLOCKS = SIZE + (SIZE + 1) // 2


def spectral():
    index = np.arange(INST)
    diff = index[:, None] - index[None, :]
    sign = 1.0 - 2.0 * np.mod(diff, 2)
    safe = np.where(diff == 0, 0.5 * math.pi, math.pi * diff / INST)
    first = np.where(diff == 0, 0.0, 0.5 * sign * np.cos(safe) / np.sin(safe))
    second = np.where(diff == 0, -(INST * INST + 2.0) / 12.0, -0.5 * sign / np.sin(safe) ** 2)
    return first - 0.5 * second


def iotas():
    sub = lax.broadcasted_iota(jnp.int32, (8, 128), 0)
    lane = lax.broadcasted_iota(jnp.int32, (8, 128), 1)
    return sub, lane


def row(ref, index):
    return ref[pl.ds(pl.multiple_of(index * 8, 8), 8), :]


def rows(ref, start, count):
    return [row(ref, start + n) for n in range(count)]


def put(ref, index, value):
    ref[pl.ds(pl.multiple_of(index * 8, 8), 8), :] = value


def total(terms):
    terms = list(terms)
    while len(terms) > 1:
        terms = [terms[n] + terms[n + 1] if n + 1 < len(terms) else terms[n] for n in range(0, len(terms), 2)]
    return terms[0]


def matvec(m, v):
    return [total(m[i * VARS + j] * v[j] for j in range(VARS)) for i in range(VARS)]


def matmul(a, b):
    return [
        total(a[i * VARS + j] * b[j * VARS + m] for j in range(VARS))
        for i in range(VARS)
        for m in range(VARS)
    ]


def plus(a, b):
    return [x + y for x, y in zip(a, b)]


def minus(a, b):
    return [x - y for x, y in zip(a, b)]


def swap(a):
    return [pltpu.roll(x, 4, 0) for x in a]


def pick(mask, a, b):
    return [jnp.where(mask, x, y) for x, y in zip(a, b)]


def lane_roll(x, shift):
    shift = shift % 128
    return x if shift == 0 else pltpu.roll(x, shift, 1)


def blocks4(block, parts):
    out = parts[0]
    for p in range(1, 4):
        out = jnp.where(block == p, parts[p], out)
    return out


def halves_of(top, a, b):
    return jnp.where(top, a, pltpu.roll(b, 4, 0))


def both(top, a):
    return [jnp.where(top, x, pltpu.roll(x, 4, 0)) for x in a]


def both_low(top, a):
    return [jnp.where(top, pltpu.roll(x, 4, 0), x) for x in a]


def edge_lines(sub, lane, u, last_ref, first_ref):
    last = jnp.zeros((8, 128), F32)
    initial = jnp.zeros((8, 128), F32)
    for n in range(STEPS * VARS):
        last = jnp.where(lane == n, lane_roll(u[n], n - 127), last)
        initial = jnp.where(lane == n, lane_roll(u[n], n), initial)
    last_ref[...] = pltpu.roll(last, 5, 0)
    first_ref[...] = pltpu.roll(initial, 3, 0)


def field_to_packed(raw_ref, out_ref, start=0):
    for v in range(VARS):
        for half in range(2):
            for t in range(TILES):
                tile = raw_ref[v, half * STEPS : (half + 1) * STEPS, t * 128 : (t + 1) * 128]
                out_ref[pl.ds(start + v * 8 + half * TILES + t, STEPS, stride=VARS * 8), :] = tile


def matrix_to_packed(raw_ref, out_ref, start=0):
    for i in range(VARS):
        for j in range(VARS):
            for half in range(2):
                for t in range(TILES):
                    tile = raw_ref[i, j, half * STEPS : (half + 1) * STEPS, t * 128 : (t + 1) * 128]
                    begin = start + (i * VARS + j) * 8 + half * TILES + t
                    out_ref[pl.ds(begin, STEPS, stride=SIZE * 8), :] = tile


def maps_kernel(
    state_ref, coupling_raw, back_raw,
    u_ref, last_ref, first_ref, lines_ref, maps_ref, up_ref,
    prefix_ref,
):
    sub, lane = iotas()
    top = sub < TILES
    field_to_packed(state_ref, u_ref)
    matrix_to_packed(coupling_raw, lines_ref, 0)
    matrix_to_packed(back_raw, lines_ref, MATRIX)

    def coupling(k):
        return rows(lines_ref, k * SIZE, SIZE)

    def back(k):
        return rows(lines_ref, STEPS * SIZE + k * SIZE, SIZE)

    def forward(k, p):
        p = [-x for x in matmul(coupling(k), p)]
        for n in range(SIZE):
            put(prefix_ref, k * SIZE + n, p[n])
        return p

    first = [-x for x in coupling(0)]
    for n in range(SIZE):
        put(prefix_ref, n, first[n])
    ahead = lax.fori_loop(1, STEPS, forward, first)

    def backward(step, carry):
        k = STEPS - 2 - step
        return minus(rows(prefix_ref, k * SIZE, SIZE), matmul(back(k), carry))

    mixed = lax.fori_loop(0, STEPS - 1, backward, ahead)

    def behind_step(step, carry):
        return [-x for x in matmul(back(STEPS - 2 - step), carry)]

    behind = lax.fori_loop(0, STEPS - 1, behind_step, [-x for x in back(STEPS - 1)])
    base = 2 * STEPS * SIZE
    for n in range(SIZE):
        put(lines_ref, base + n, ahead[n])
        put(lines_ref, base + SIZE + n, mixed[n])
        put(lines_ref, base + 2 * SIZE + n, behind[n])
    whole_ahead = matmul(swap(ahead), ahead)
    whole_behind = matmul(behind, swap(behind))
    for n in range(SIZE):
        put(maps_ref, n, halves_of(top, whole_ahead[n], whole_behind[n]))
    whole_mixed = plus(mixed, matmul(behind, matmul(swap(mixed), ahead)))
    for n in range(0, SIZE, 2):
        put(maps_ref, SIZE + n // 2, halves_of(top, whole_mixed[n], whole_mixed[min(n + 1, SIZE - 1)]))
    edge_lines(sub, lane, rows(u_ref, 0, STEPS * VARS), last_ref, first_ref)
    up_ref[: VARS * 8, :] = u_ref[(STEPS - 1) * VARS * 8 :, :]
    up_ref[VARS * 8 : (VARS + SIZE) * 8, :] = lines_ref[2 * MATRIX - SIZE * 8 : 2 * MATRIX, :]
    up_ref[(VARS + SIZE) * 8 :, :] = u_ref[: VARS * 8, :]


def cells_kernel(source_ref, flags_ref, pivot_raw, out_ref):
    field_to_packed(source_ref, out_ref, 0)
    for half in range(2):
        for t in range(TILES):
            flags = flags_ref[half * STEPS : (half + 1) * STEPS, t * 128 : (t + 1) * 128]
            out_ref[pl.ds(FIELD + half * TILES + t, STEPS, stride=8), :] = (1 - flags).astype(F32)
    matrix_to_packed(pivot_raw, out_ref, FIELD + STEPS * 8)


def time_kernel(weights, u_ref, wait_ref, later_ref, out_ref, *later_out):
    for v in range(VARS):
        fields = [row(u_ref, j * VARS + v) for j in range(INST)]
        for i in range(INST):
            put(out_ref, i * VARS + v, total(fields[j] * F32(weights[i, j]) for j in range(INST)))
    begin = 0
    for ref in later_out:
        ref[...] = later_ref[begin : begin + ref.shape[0], :]
        begin += ref.shape[0]


def stencil_kernel(u_ref, src_ref, below_ref, above_ref, left_ref, right_ref, out_ref):
    sub, lane = iotas()
    top = sub < TILES
    left_all = left_ref[...]
    right_all = right_ref[...]
    for k in range(STEPS):
        for v in range(VARS):
            n = k * VARS + v
            u = row(u_ref, n)
            if k == 0:
                below = pltpu.roll(jnp.where(top, row(u_ref, (STEPS - 1) * VARS + v), row(below_ref, v)), 4, 0)
            else:
                below = row(u_ref, n - VARS)
            if k == STEPS - 1:
                above = pltpu.roll(jnp.where(top, row(above_ref, v), row(u_ref, v)), 4, 0)
            else:
                above = row(u_ref, n + VARS)
            turned = pltpu.roll(u, 1, 1)
            edge = jnp.where(sub % TILES == 0, lane_roll(left_all, -n), pltpu.roll(turned, 1, 0))
            left = jnp.where(lane == 0, edge, turned)
            turned = pltpu.roll(u, 127, 1)
            edge = jnp.where(sub % TILES == TILES - 1, lane_roll(right_all, 127 - n), pltpu.roll(turned, 7, 0))
            right = jnp.where(lane == 127, edge, turned)
            value = row(src_ref, n) - 0.1 * above + 0.5 * below - 0.8 * u + 0.2 * (left + right)
            put(out_ref, n, value)


def local_kernel(base_ref, time_ref, cells_ref, lines_ref, source_ref, ends_ref, packed_ref):
    sub, lane = iotas()
    top = sub < TILES
    pivot_row = STEPS * VARS + STEPS

    def source_step(k, carry):
        keep = row(cells_ref, STEPS * VARS + k)
        rhs = [keep * (row(base_ref, k * VARS + v) + row(time_ref, k * VARS + v)) for v in range(VARS)]
        for v, value in enumerate(matvec(rows(cells_ref, pivot_row + k * SIZE, SIZE), rhs)):
            put(source_ref, k * VARS + v, value)
        return carry

    lax.fori_loop(0, STEPS, source_step, 0)
    y = rows(source_ref, 0, VARS)
    kept = [y]
    for k in range(1, STEPS):
        y = minus(rows(source_ref, k * VARS, VARS), matvec(rows(lines_ref, k * SIZE, SIZE), y))
        kept.append(y)
    end = y
    x = y
    for k in range(STEPS - 2, -1, -1):
        x = minus(kept[k], matvec(rows(lines_ref, (STEPS + k) * SIZE, SIZE), x))
    for v in range(VARS):
        put(ends_ref, v, end[v])
        put(ends_ref, VARS + v, x[v])
    base = 2 * STEPS * SIZE
    ahead = rows(lines_ref, base, SIZE)
    mixed = rows(lines_ref, base + SIZE, SIZE)
    behind = rows(lines_ref, base + 2 * SIZE, SIZE)
    whole_end = plus(swap(end), matvec(swap(ahead), end))
    inner = plus(swap(x), matvec(swap(mixed), end))
    whole_first = plus(x, matvec(behind, inner))
    for v in range(VARS):
        put(packed_ref, v, halves_of(top, whole_end[v], whole_first[v]))


def interface(top, place, ends_ref, maps_ref, entry_ref):
    zero = [jnp.zeros((8, 128), F32)] * VARS

    def pairs(d):
        return rows(ends_ref, d * VARS, VARS)

    def maps(d):
        return rows(maps_ref, d * MAP_BLOCKS, SIZE)

    def forward(d, e):
        for v in range(VARS):
            put(entry_ref, d * VARS + v, e[v])
        return plus(pairs(d), matvec(maps(d), e))

    last = lax.fori_loop(0, SEGMENTS - 1, forward, zero)
    for v in range(VARS):
        put(entry_ref, (SEGMENTS - 1) * VARS + v, last[v])

    def backward(step, f):
        d = SEGMENTS - 1 - step
        mixed = rows(maps_ref, d * MAP_BLOCKS + SIZE, (SIZE + 1) // 2)
        mixed = [mixed[n // 2] if n % 2 else pltpu.roll(mixed[n // 2], 4, 0) for n in range(SIZE)]
        entry = swap(rows(entry_ref, d * VARS, VARS))
        return plus(plus(pairs(d), matvec(mixed, entry)), matvec(maps(d), f))

    after = lax.fori_loop(0, SEGMENTS - 1 - place, backward, zero)
    entry = rows(entry_ref, place * VARS, VARS)
    return both(top, entry), both_low(top, after)


def finish_kernel(
    last, place_ref, gathered_ref, maps_ref, u_ref, source_ref, ends_ref, lines_ref, *rest
):
    if last:
        out_ref, new_ref, entry_ref = rest
    else:
        up_ref, above_ref, new_ref, last_ref, first_ref, new_below_ref, new_above_ref, entry_ref = rest
    sub, lane = iotas()
    top = sub < TILES
    entry, after = interface(top, place_ref[0], gathered_ref, maps_ref, entry_ref)
    base = 2 * STEPS * SIZE
    end = rows(ends_ref, 0, VARS)
    begin = rows(ends_ref, VARS, VARS)
    middle = plus(end, matvec(rows(lines_ref, base, SIZE), entry))
    start = pick(top, entry, swap(middle))
    follow = plus(
        plus(begin, matvec(rows(lines_ref, base + SIZE, SIZE), start)),
        matvec(rows(lines_ref, base + 2 * SIZE, SIZE), after),
    )
    finish = pick(top, swap(follow), after)
    y = start
    kept = []
    for k in range(STEPS):
        y = minus(rows(source_ref, k * VARS, VARS), matvec(rows(lines_ref, k * SIZE, SIZE), y))
        kept.append(y)
    x = finish
    for k in range(STEPS - 1, -1, -1):
        x = minus(kept[k], matvec(rows(lines_ref, (STEPS + k) * SIZE, SIZE), x))
        for v in range(VARS):
            put(new_ref, k * VARS + v, row(u_ref, k * VARS + v) + x[v])
    if last:
        for v in range(VARS):
            for half in range(2):
                for t in range(TILES):
                    tile = new_ref[pl.ds(v * 8 + half * TILES + t, STEPS, stride=VARS * 8), :]
                    out_ref[v, half * STEPS : (half + 1) * STEPS, t * 128 : (t + 1) * 128] = tile
    else:
        edge_lines(sub, lane, rows(new_ref, 0, STEPS * VARS), last_ref, first_ref)
        before = minus(entry, matvec(rows(up_ref, VARS, SIZE), swap(x)))
        for v in range(VARS):
            put(new_below_ref, v, row(up_ref, v) + before[v])
            put(new_above_ref, v, row(above_ref, v) + after[v])


def call(kernel, shapes, *args, scratch=(), flops=100_000, limit=8, place=None):
    outs = [jax.ShapeDtypeStruct(shape, F32) for shape in shapes]
    moved = 4 * (sum(math.prod(shape) for shape in shapes) + sum(a.size for a in args))
    specs = [pl.BlockSpec(memory_space=pltpu.VMEM)] * len(args)
    if place is not None:
        specs.insert(0, pl.BlockSpec(memory_space=pltpu.SMEM))
        args = (place,) + args
    return pl.pallas_call(
        kernel,
        out_shape=outs,
        in_specs=specs,
        scratch_shapes=[pltpu.VMEM(shape, F32) for shape in scratch],
        cost_estimate=pl.CostEstimate(flops=flops, bytes_accessed=moved, transcendentals=0),
        compiler_params=pltpu.CompilerParams(vmem_limit_bytes=limit * 1024 * 1024),
    )(*args)


def exchange(value, axis, count):
    shape = value.shape
    out = lax.all_to_all(value.reshape(count, shape[0] // count, 128), axis, 0, 0)
    return out.reshape(shape)


def moved(value, axis, step, wrap):
    count = lax.axis_size(axis)
    pairs = [(i, (i + step) % count) for i in range(count) if wrap or 0 <= i + step < count]
    return lax.ppermute(value, axis, pairs)


def body(state, source_terms, pivot_inverse, coupling, back_coupling, wall_flags):
    weights = np.float32(-0.5 * spectral())
    place = lax.axis_index("axial").astype(jnp.int32).reshape(1)
    edge = (8, 128)
    halo = (VARS * 8, 128)
    carried = ((VARS + SIZE) * 8, 128)
    u, last_line, first_line, lines, maps, halos = call(
        maps_kernel,
        [
            (FIELD, 128), edge, edge, (2 * MATRIX + 3 * SIZE * 8, 128), (MAP_BLOCKS * 8, 128),
            (carried[0] + halo[0], 128),
        ],
        state[0].transpose(1, 0, 2), coupling[0].transpose(1, 2, 0, 3), back_coupling[0].transpose(1, 2, 0, 3),
        scratch=[(MATRIX, 128)],
        flops=8_000_000,
        limit=16,
    )
    maps = lax.all_gather(maps, "axial", axis=0, tiled=True)
    (cells,) = call(
        cells_kernel,
        [(FIELD + STEPS * 8 + MATRIX, 128)],
        source_terms[0].transpose(1, 0, 2), wall_flags, pivot_inverse[0].transpose(1, 2, 0, 3),
    )
    for sweep in range(SWEEPS):
        spread = exchange(u, "inst", INST)
        left = moved(last_line, "span", 1, True)
        if sweep == 0:
            right = moved(first_line, "span", -1, True)
            term, up, above = call(
                lambda a, b, c, *refs: time_kernel(weights, a, b, c, *refs),
                [(FIELD, 128), carried, halo], spread, jnp.concatenate([left, right]), halos,
            )
            up = moved(up, "axial", 1, False)
            above = moved(above, "axial", -1, False)
            below = up[: VARS * 8]
        else:
            term, right = call(
                lambda *refs: time_kernel(weights, *refs), [(FIELD, 128), edge], spread, left, first_line
            )
            right = moved(right, "span", -1, True)
        time = exchange(term, "inst", INST)
        (base,) = call(stencil_kernel, [(FIELD, 128)], u, cells, below, above, left, right)
        source, ends, packed = call(
            local_kernel, [(FIELD, 128), (2 * VARS * 8, 128), (VARS * 8, 128)], base, time, cells, lines
        )
        gathered = lax.all_gather(packed, "axial", axis=0, tiled=True)
        last = sweep == SWEEPS - 1
        common = (gathered, maps, u, source, ends, lines)
        entries = (SEGMENTS * VARS * 8, 128)
        if last:
            (result,) = call(
                lambda *refs: finish_kernel(True, *refs), [(VARS, 2 * STEPS, TILES * 128)], *common,
                scratch=[(FIELD, 128), entries], place=place,
            )
        else:
            u, last_line, first_line, below, above = call(
                lambda *refs: finish_kernel(False, *refs), [(FIELD, 128), edge, edge, halo, halo],
                *common, up, above, scratch=[entries], place=place,
            )
    return result.transpose(1, 0, 2)[None]


def solution(mesh):
    return jax.shard_map(
        body,
        mesh=mesh,
        in_specs=(
            P("inst", "axial", None, "span"),
            P("inst", "axial", None, "span"),
            P("inst", "axial", None, None, "span"),
            P("inst", "axial", None, None, "span"),
            P("inst", "axial", None, None, "span"),
            P("axial", "span"),
        ),
        out_specs=P("inst", "axial", None, "span"),
        check_vma=False,
    )
```

time: 134 us -> 132 us (0.985)
  blocking collectives: 87.9 us -> 38.2 us
  starting transfers between devices: 27.3 us -> 48.4 us
  between operations: 0.3 us -> 13.5 us
  waiting for transfers between devices: 2.2 us -> 12.2 us
  Pallas kernels: 6.61 us -> 11.1 us
    all_to_all x6 -> x0, blocking collectives: 87.9 us -> none  [exchange(): lax.all_to_all(value.reshape(count, shape[0] // count, 128), axis, 0, 0)]
    all_gather x0 -> x2, blocking collectives: none -> 38.2 us  [body(): gathered = lax.all_gather(packed, 'axial', axis=0, tiled=True)]
    all_to_all x2 -> x4, starting transfers between devices: 6.76 us -> 26.3 us  [exchange(): lax.all_to_all(value.reshape(count, shape[0] // count, 128), axis, 0, 0)]
    all_to_all x2 -> x4, waiting for transfers between devices: 0.01 us -> 5.44 us  [exchange(): lax.all_to_all(value.reshape(count, shape[0] // count, 128), axis, 0, 0)]
    ppermute x6, waiting for transfers between devices: 2.19 us -> 6.75 us  [moved(): return lax.ppermute(value, axis, pairs)]
    pallas_call x12 -> x10, Pallas kernels: 6.61 us -> 11.1 us  [call(): pl.pallas_call(kernel, out_shape=outs, in_specs=specs, scratch_shapes=[pl...]
    ppermute x6, starting transfers between devices: 20.6 us -> 22.1 us  [moved(): return lax.ppermute(value, axis, pairs)]
    unnamed x39 -> x20, local copies, waits for them, and re-layouts: 6.73 us -> 7.65 us
  transfers between devices with their start and end apart: 8 -> 11, of which waited for: 2 -> 8; matrix products, arithmetic and copies ran while one was open for 1% -> 0% of each run, Pallas kernels for 2% -> 3%
where the time goes in v2:
time: 132 us; the launch traced here: 131 us
  starting transfers between devices  48.4 us (37%)
  blocking collectives  38.2 us (29%)
  between operations  13.5 us (10%)
  waiting for transfers between devices  12.2 us (9%)
  Pallas kernels  11.1 us (8%)
  local copies, waits for them, and re-layouts  7.65 us (6%)
    all_gather x2, blocking collectives, body(): gathered = lax.all_gather(packed, 'axial', axis=0, tiled=True)  38.2 us
    all_to_all x4, starting transfers between devices, exchange(): lax.all_to_all(value.reshape(count, shape[0] // count, 128), axis, 0, 0)  26.3 us
    ppermute x6, starting transfers between devices, moved(): return lax.ppermute(value, axis, pairs)  22.1 us
    pallas_call x10, Pallas kernels, call(): pl.pallas_call(kernel, out_shape=outs, in_specs=specs, scratch_shapes=[pl...  11.1 us
    unnamed x20, local copies, waits for them, and re-layouts  7.65 us
    ppermute x6, waiting for transfers between devices, moved(): return lax.ppermute(value, axis, pairs)  6.75 us
    all_to_all x4, waiting for transfers between devices, exchange(): lax.all_to_all(value.reshape(count, shape[0] // count, 128), axis, 0, 0)  5.44 us
  transfers between devices with their start and end apart: 11, of which 8 were waited for; matrix products, arithmetic and copies ran while one was open for 0% of the time, Pallas kernels for 3%

profile of v2, /device:TPU:1, one launch (start us, length us, event | category | flops | bytes accessed | tf_op | source)
XLA Modules:
  0.0 131.1 jit_solution(5550739462673999216)
XLA Ops:
  6.5 1.1 copy-done.2
  7.7 1.1 copy-done.3
  8.8 0.9 copy-done.7
  9.7 2.1 %shard_map.64 = (f32[320,128]{1,0:T(8,128)}, f32[8,128]{1,0:T(8,128)S(1)}, f32[8,128]{1,0:T(8,128)S(1)}, f32[3800,128]{1,0:T(8,128)S(1)}, f32[304,128]{1,0:T(8,128)}, /*index=5*/f32[280,128]{1,0:T(8,128)S(1)}) custom-call(f32[5,16,512]{2,1,0:T(8,128)S(1)} %bitcast.34, f32[5,5,16,512]{3,2,1,0:T(8,128)S(1)} %bitcast.27, f32[5,5,16,512]{3,2,1,0:T(8,128)S(1)} %bitcast.28), custom_call_target="tpu_custom_call" | custom-call | flops 8000000 | bytes 4218880 | tf_op jit(solution)/shard_map/pallas_call | solution.py:359
  11.9 10.9 %all-to-all-start = ((f32[8,40,128]{2,1,0:T(8,128)}), f32[8,40,128]{2,1,0:T(8,128)S(1)}, u32[]{:S(2)}, u32[]{:S(2)}) async-start(f32[8,40,128]{2,1,0:T(8,128)} %bitcast.11), calls=%async_computation | async-start | bytes 327680 | tf_op jit(solution)/shard_map/all_to_all | solution.py:371
  22.8 3.1 %collective-permute-start = (f32[8,128]{1,0:T(8,128)S(1)}, f32[8,128]{1,0:T(8,128)S(1)}, u32[]{:S(2)}, u32[]{:S(2)}) collective-permute-start(f32[8,128]{1,0:T(8,128)S(1)} %get-tuple-element.28), channel_id=1, source_target_pairs={{0,1},{1,2},{2,3},{3,0},{4,5},{5,6},{6,7},{7,4},{8,9},{9,10},{10,1... | collective-permute-start | bytes 12296 | tf_op jit(solution)/shard_map/ppermute | solution.py:378
  25.9 3.4 %collective-permute-start.1 = (f32[8,128]{1,0:T(8,128)S(1)}, f32[8,128]{1,0:T(8,128)S(1)}, u32[]{:S(2)}, u32[]{:S(2)}) collective-permute-start(f32[8,128]{1,0:T(8,128)S(1)} %get-tuple-element.29), channel_id=1, source_target_pairs={{0,3},{1,0},{2,1},{3,2},{4,7},{5,4},{6,5},{7,6},{8,11},{9,8},{10,9... | collective-permute-start | bytes 12296 | tf_op jit(solution)/shard_map/ppermute | solution.py:378
  29.3 1.2 collective-permute-done.1.right_ref
  30.9 0.8 shard_map.66
  31.7 6.0 %all-to-all-start.1 = ((f32[8,40,128]{2,1,0:T(8,128)}), f32[8,40,128]{2,1,0:T(8,128)S(1)}, u32[]{:S(2)}, u32[]{:S(2)}) async-start(f32[8,40,128]{2,1,0:T(8,128)} %bitcast.13), calls=%async_computation.1 | async-start | bytes 327680 | tf_op jit(solution)/shard_map/all_to_all | solution.py:371
  37.7 5.9 %collective-permute-start.2 = (f32[240,128]{1,0:T(8,128)}, f32[240,128]{1,0:T(8,128)S(1)}, u32[]{:S(2)}, u32[]{:S(2)}) collective-permute-start(f32[240,128]{1,0:T(8,128)} %get-tuple-element.31), channel_id=1, source_target_pairs={{0,4},{4,8},{8,12},{12,16},{16,20},{20,24},{24,28},{28,32},{32,36}... | collective-permute-start | bytes 368648 | tf_op jit(solution)/shard_map/ppermute | solution.py:378
  43.7 1.9 %collective-permute-start.3 = (f32[40,128]{1,0:T(8,128)S(1)}, f32[40,128]{1,0:T(8,128)S(1)}, u32[]{:S(2)}, u32[]{:S(2)}) collective-permute-start(f32[40,128]{1,0:T(8,128)S(1)} %get-tuple-element.32), channel_id=1, source_target_pairs={{4,0},{8,4},{12,8},{16,12},{20,16},{24,20},{28,24},{32,28},{36,32}... | collective-permute-start | bytes 61448 | tf_op jit(solution)/shard_map/ppermute | solution.py:378
  45.6 1.1 copy-done.4
  47.4 1.8 %collective-permute-done.3.above_ref.refs_8_ = f32[40,128]{1,0:T(8,128)S(1)} collective-permute-done((f32[40,128]{1,0:T(8,128)S(1)}, f32[40,128]{1,0:T(8,128)S(1)}, u32[]{:S(2)}, u32[]{:S(2)}) %collective-permute-start.3) | collective-permute-done | bytes 20512 | tf_op jit(solution)/shard_map/ppermute | solution.py:378
  49.2 1.2 shard_map.67.base_ref
  50.6 0.7 copy-done.5
  51.3 18.0 %all_gather.9.refs_1_ = f32[640,128]{1,0:T(8,128)S(1)} all-gather(f32[40,128]{1,0:T(8,128)S(1)} %get-tuple-element.35), channel_id=1, replica_groups=mesh['inst'=8,'axial'=16,'span'=4] {'axial'}, dimensions={0}, use_global_device_ids=true | all-gather | bytes 348160 | tf_op jit(solution)/shard_map/all_gather | solution.py:426
  69.3 1.7 %copy-done = f32[4864,128]{1,0:T(8,128)S(1)} copy-done((f32[4864,128]{1,0:T(8,128)S(1)}, f32[4864,128]{1,0:T(8,128)}, u32[]{:S(2)}) %copy-start) | copy-done | bytes 2490392
  71.0 0.9 copy-done.6
  71.9 2.3 %shard_map.69 = (f32[320,128]{1,0:T(8,128)}, f32[8,128]{1,0:T(8,128)S(1)}, f32[8,128]{1,0:T(8,128)S(1)}, f32[40,128]{1,0:T(8,128)S(1)}, f32[40,128]{1,0:T(8,128)S(1)}) custom-call(s32[1]{0:T(128)} %bitcast.refs_0_, f32[640,128]{1,0:T(8,128)S(1)} %all_gather.9.refs_1_, f32[4864,128]{1,0:T(8,128)S(1)} %copy-done, f32[320,128]{1,0:T(8,128)} %get-tuple-element.27.u_ref.refs_3_, ...), custom_call_target="tpu_custom_call" | custom-call | flops 100000 | bytes 5488640 | tf_op jit(solution)/shard_map/pallas_call | solution.py:359
  74.1 6.0 %all-to-all-start.2 = ((f32[8,40,128]{2,1,0:T(8,128)}), f32[8,40,128]{2,1,0:T(8,128)S(1)}, u32[]{:S(2)}, u32[]{:S(2)}) async-start(f32[8,40,128]{2,1,0:T(8,128)} %bitcast.15), calls=%async_computation.2 | async-start | bytes 327680 | tf_op jit(solution)/shard_map/all_to_all | solution.py:371
  80.1 3.2 %collective-permute-start.4 = (f32[8,128]{1,0:T(8,128)S(1)}, f32[8,128]{1,0:T(8,128)S(1)}, u32[]{:S(2)}, u32[]{:S(2)}) collective-permute-start(f32[8,128]{1,0:T(8,128)S(1)} %get-tuple-element.42), channel_id=1, source_target_pairs={{0,1},{1,2},{2,3},{3,0},{4,5},{5,6},{6,7},{7,4},{8,9},{9,10},{10,1... | collective-permute-start | bytes 12296 | tf_op jit(solution)/shard_map/ppermute | solution.py:378
  83.3 2.5 %collective-permute-done.4.refs_1_.left_ref = f32[8,128]{1,0:T(8,128)S(1)} collective-permute-done((f32[8,128]{1,0:T(8,128)S(1)}, f32[8,128]{1,0:T(8,128)S(1)}, u32[]{:S(2)}, u32[]{:S(2)}) %collective-permute-start.4) | collective-permute-done | bytes 4128 | tf_op jit(solution)/shard_map/ppermute | solution.py:378
  85.9 3.2 %all-to-all-done.2 = f32[8,40,128]{2,1,0:T(8,128)S(1)} async-done(((f32[8,40,128]{2,1,0:T(8,128)}), f32[8,40,128]{2,1,0:T(8,128)S(1)}, u32[]{:S(2)}, u32[]{:S(2)}) %all-to-all-start.2) | async-done | bytes 163872 | tf_op jit(solution)/shard_map/all_to_all | solution.py:371
  89.1 0.7 shard_map.70
  89.9 3.4 %all-to-all-start.3 = ((f32[8,40,128]{2,1,0:T(8,128)}), f32[8,40,128]{2,1,0:T(8,128)S(1)}, u32[]{:S(2)}, u32[]{:S(2)}) async-start(f32[8,40,128]{2,1,0:T(8,128)} %bitcast.17), calls=%async_computation.3 | async-start | bytes 327680 | tf_op jit(solution)/shard_map/all_to_all | solution.py:371
  93.3 4.6 %collective-permute-start.5 = (f32[8,128]{1,0:T(8,128)S(1)}, f32[8,128]{1,0:T(8,128)S(1)}, u32[]{:S(2)}, u32[]{:S(2)}) collective-permute-start(f32[8,128]{1,0:T(8,128)S(1)} %get-tuple-element.44), channel_id=1, source_target_pairs={{0,3},{1,0},{2,1},{3,2},{4,7},{5,4},{6,5},{7,6},{8,11},{9,8},{10,9... | collective-permute-start | bytes 12296 | tf_op jit(solution)/shard_map/ppermute | solution.py:378
  97.9 0.7 collective-permute-done.5.right_ref
  98.6 1.2 shard_map.71.base_ref
  99.8 1.8 %all-to-all-done.3 = f32[8,40,128]{2,1,0:T(8,128)S(1)} async-done(((f32[8,40,128]{2,1,0:T(8,128)}), f32[8,40,128]{2,1,0:T(8,128)S(1)}, u32[]{:S(2)}, u32[]{:S(2)}) %all-to-all-start.3) | async-done | bytes 163872 | tf_op jit(solution)/shard_map/all_to_all | solution.py:371
  101.8 20.2 %all_gather.11.refs_1_ = f32[640,128]{1,0:T(8,128)S(1)} all-gather(f32[40,128]{1,0:T(8,128)S(1)} %get-tuple-element.46), channel_id=1, replica_groups=mesh['inst'=8,'axial'=16,'span'=4] {'axial'}, dimensions={0}, use_global_device_ids=true | all-gather | bytes 348160 | tf_op jit(solution)/shard_map/all_gather | solution.py:426
  122.0 2.3 %shard_map.73 = f32[5,16,512]{2,1,0:T(8,128)} custom-call(s32[1]{0:T(128)} %bitcast.refs_0_, f32[640,128]{1,0:T(8,128)S(1)} %all_gather.11.refs_1_, f32[4864,128]{1,0:T(8,128)S(1)} %copy-done.1, f32[320,128]{1,0:T(8,128)} %get-tuple-element.39.u_ref.refs_3_, f32[320,128]{1,0:T(8,128)S(1)} %get-tuple-element.47.refs_4_, ...), custom_call_target="tpu_custom_call" | custom-call | flops 100000 | bytes 5296128 | tf_op jit(solution)/shard_map/pallas_call | solution.py:359
  (25 shorter events, 1.6 us)
Async XLA Ops:
  6.5 62.7 %all-gather.2.cloned.1.call-start = ((), (), s32[]{:S(2)}) async-start(), calls=%async_computation.4 | async-start | bytes 2646016 | tf_op jit(solution)/shard_map/all_gather | solution.py:398
  6.5 1.1 copy-start.2
  7.7 1.1 copy-start.3
  8.8 0.9 copy-start.7
  9.7 35.8 %copy-start.8 = (f32[1,16,5,512]{3,1,2,0:T(8,128)S(1)}, f32[1,16,5,512]{3,1,2,0:T(8,128)}, u32[]{:S(2)}) copy-start(f32[1,16,5,512]{3,1,2,0:T(8,128)} %param.7) | copy-start | bytes 491524
  9.7 35.8 %copy-start.9 = (s32[16,512]{1,0:T(8,128)S(1)}, s32[16,512]{1,0:T(8,128)}, u32[]{:S(2)}) copy-start(s32[16,512]{1,0:T(8,128)} %flags_ref.1) | copy-start | bytes 98308
  11.9 19.1 %all-to-all-start = ((f32[8,40,128]{2,1,0:T(8,128)}), f32[8,40,128]{2,1,0:T(8,128)S(1)}, u32[]{:S(2)}, u32[]{:S(2)}) async-start(f32[8,40,128]{2,1,0:T(8,128)} %bitcast.11), calls=%async_computation | async-start | bytes 327680 | tf_op jit(solution)/shard_map/all_to_all | solution.py:371
  22.8 6.5 %collective-permute-start = (f32[8,128]{1,0:T(8,128)S(1)}, f32[8,128]{1,0:T(8,128)S(1)}, u32[]{:S(2)}, u32[]{:S(2)}) collective-permute-start(f32[8,128]{1,0:T(8,128)S(1)} %get-tuple-element.28), channel_id=1, source_target_pairs={{0,1},{1,2},{2,3},{3,0},{4,5},{5,6},{6,7},{7,4},{8,9},{9,10},{10,1... | collective-permute-start | bytes 12296 | tf_op jit(solution)/shard_map/ppermute | solution.py:378
  25.9 4.6 %collective-permute-start.1 = (f32[8,128]{1,0:T(8,128)S(1)}, f32[8,128]{1,0:T(8,128)S(1)}, u32[]{:S(2)}, u32[]{:S(2)}) collective-permute-start(f32[8,128]{1,0:T(8,128)S(1)} %get-tuple-element.29), channel_id=1, source_target_pairs={{0,3},{1,0},{2,1},{3,2},{4,7},{5,4},{6,5},{7,6},{8,11},{9,8},{10,9... | collective-permute-start | bytes 12296 | tf_op jit(solution)/shard_map/ppermute | solution.py:378
  31.7 18.6 %all-to-all-start.1 = ((f32[8,40,128]{2,1,0:T(8,128)}), f32[8,40,128]{2,1,0:T(8,128)S(1)}, u32[]{:S(2)}, u32[]{:S(2)}) async-start(f32[8,40,128]{2,1,0:T(8,128)} %bitcast.13), calls=%async_computation.1 | async-start | bytes 327680 | tf_op jit(solution)/shard_map/all_to_all | solution.py:371
  37.7 9.7 %collective-permute-start.2 = (f32[240,128]{1,0:T(8,128)}, f32[240,128]{1,0:T(8,128)S(1)}, u32[]{:S(2)}, u32[]{:S(2)}) collective-permute-start(f32[240,128]{1,0:T(8,128)} %get-tuple-element.31), channel_id=1, source_target_pairs={{0,4},{4,8},{8,12},{12,16},{16,20},{20,24},{24,28},{28,32},{32,36}... | collective-permute-start | bytes 368648 | tf_op jit(solution)/shard_map/ppermute | solution.py:378
  43.7 5.5 %collective-permute-start.3 = (f32[40,128]{1,0:T(8,128)S(1)}, f32[40,128]{1,0:T(8,128)S(1)}, u32[]{:S(2)}, u32[]{:S(2)}) collective-permute-start(f32[40,128]{1,0:T(8,128)S(1)} %get-tuple-element.32), channel_id=1, source_target_pairs={{4,0},{8,4},{12,8},{16,12},{20,16},{24,20},{28,24},{32,28},{36,32}... | collective-permute-start | bytes 61448 | tf_op jit(solution)/shard_map/ppermute | solution.py:378
  45.6 1.2 copy-start.4
  50.6 0.7 copy-start.5
  69.3 1.7 %copy-start = (f32[4864,128]{1,0:T(8,128)S(1)}, f32[4864,128]{1,0:T(8,128)}, u32[]{:S(2)}) copy-start(f32[4864,128]{1,0:T(8,128)} %all-gather.2.cloned.1.call-done.refs_2_) | copy-start | bytes 7471108
  71.0 0.9 copy-start.6
  74.1 15.0 %all-to-all-start.2 = ((f32[8,40,128]{2,1,0:T(8,128)}), f32[8,40,128]{2,1,0:T(8,128)S(1)}, u32[]{:S(2)}, u32[]{:S(2)}) async-start(f32[8,40,128]{2,1,0:T(8,128)} %bitcast.15), calls=%async_computation.2 | async-start | bytes 327680 | tf_op jit(solution)/shard_map/all_to_all | solution.py:371
  80.1 5.7 %collective-permute-start.4 = (f32[8,128]{1,0:T(8,128)S(1)}, f32[8,128]{1,0:T(8,128)S(1)}, u32[]{:S(2)}, u32[]{:S(2)}) collective-permute-start(f32[8,128]{1,0:T(8,128)S(1)} %get-tuple-element.42), channel_id=1, source_target_pairs={{0,1},{1,2},{2,3},{3,0},{4,5},{5,6},{6,7},{7,4},{8,9},{9,10},{10,1... | collective-permute-start | bytes 12296 | tf_op jit(solution)/shard_map/ppermute | solution.py:378
  89.9 11.7 %all-to-all-start.3 = ((f32[8,40,128]{2,1,0:T(8,128)}), f32[8,40,128]{2,1,0:T(8,128)S(1)}, u32[]{:S(2)}, u32[]{:S(2)}) async-start(f32[8,40,128]{2,1,0:T(8,128)} %bitcast.17), calls=%async_computation.3 | async-start | bytes 327680 | tf_op jit(solution)/shard_map/all_to_all | solution.py:371
  93.3 5.4 %collective-permute-start.5 = (f32[8,128]{1,0:T(8,128)S(1)}, f32[8,128]{1,0:T(8,128)S(1)}, u32[]{:S(2)}, u32[]{:S(2)}) collective-permute-start(f32[8,128]{1,0:T(8,128)S(1)} %get-tuple-element.44), channel_id=1, source_target_pairs={{0,3},{1,0},{2,1},{3,2},{4,7},{5,4},{6,5},{7,6},{8,11},{9,8},{10,9... | collective-permute-start | bytes 12296 | tf_op jit(solution)/shard_map/ppermute | solution.py:378
  101.5 20.5 %copy-start.1 = (f32[4864,128]{1,0:T(8,128)S(1)}, f32[4864,128]{1,0:T(8,128)}, u32[]{:S(2)}) copy-start(f32[4864,128]{1,0:T(8,128)} %all-gather.2.cloned.1.call-done.refs_2_) | copy-start | bytes 7471108
Sparse Core Ops, SparseCore 0:
  12.0 48.4 all-gather.1

commit v3 on v2

--- a/solution.py
+++ b/solution.py
@@ -18,7 +18,9 @@
 FIELD = STEPS * VARS * 8
 MATRIX = STEPS * VARS * VARS * 8
 SIZE = VARS * VARS
-MAP_BLOCKS = SIZE + (SIZE + 1) // 2
+FULL_GROUPS = 24
+VEC_GROUPS = 4
+PACKED = 2 * MATRIX + 3 * SIZE * 8
 
 
 def spectral():
@@ -96,26 +98,29 @@
     return out
 
 
-def halves_of(top, a, b):
-    return jnp.where(top, a, pltpu.roll(b, 4, 0))
-
-
-def both(top, a):
-    return [jnp.where(top, x, pltpu.roll(x, 4, 0)) for x in a]
-
-
-def both_low(top, a):
-    return [jnp.where(top, pltpu.roll(x, 4, 0), x) for x in a]
-
-
-def edge_lines(sub, lane, u, last_ref, first_ref):
+def blocks4(block, parts):
+    out = parts[0]
+    for p in range(1, 4):
+        out = jnp.where(block == p, parts[p], out)
+    return out
+
+
+def pack_lines(out_ref, start, block, values, first, groups):
+    for g in range((len(values) + 3) // 4):
+        four = [values[min(4 * g + p, len(values) - 1)] for p in range(4)]
+        for q in range(4):
+            chunk = blocks4(block, [lane_roll(four[p], 32 * (p - q)) for p in range(4)])
+            out_ref[pl.ds(start + q * groups + first + g, 4, stride=4 * groups), :] = chunk[:4]
+
+
+def edge_lines(sub, lane, u, edges_ref):
     last = jnp.zeros((8, 128), F32)
     initial = jnp.zeros((8, 128), F32)
     for n in range(STEPS * VARS):
         last = jnp.where(lane == n, lane_roll(u[n], n - 127), last)
         initial = jnp.where(lane == n, lane_roll(u[n], n), initial)
-    last_ref[...] = pltpu.roll(last, 5, 0)
-    first_ref[...] = pltpu.roll(initial, 3, 0)
+    put(edges_ref, 0, pltpu.roll(last, 5, 0))
+    put(edges_ref, 1, pltpu.roll(initial, 3, 0))
 
 
 def field_to_packed(raw_ref, out_ref, start=0):
@@ -136,14 +141,15 @@
                     out_ref[pl.ds(begin, STEPS, stride=SIZE * 8), :] = tile
 
 
-def maps_kernel(
-    state_ref, coupling_raw, back_raw,
-    u_ref, last_ref, first_ref, lines_ref, maps_ref, up_ref,
-    prefix_ref,
-):
+def pack_kernel(state_ref, u_ref, edges_ref):
     sub, lane = iotas()
-    top = sub < TILES
     field_to_packed(state_ref, u_ref)
+    edge_lines(sub, lane, rows(u_ref, 0, STEPS * VARS), edges_ref)
+
+
+def maps_kernel(u_ref, coupling_raw, back_raw, lines_ref, up_ref, down_ref, prefix_ref):
+    sub, lane = iotas()
+    block = lane // 32
     matrix_to_packed(coupling_raw, lines_ref, 0)
     matrix_to_packed(back_raw, lines_ref, MATRIX)
 
@@ -179,17 +185,19 @@
         put(lines_ref, base + n, ahead[n])
         put(lines_ref, base + SIZE + n, mixed[n])
         put(lines_ref, base + 2 * SIZE + n, behind[n])
-    whole_ahead = matmul(swap(ahead), ahead)
-    whole_behind = matmul(behind, swap(behind))
+    whole = matmul(swap(ahead), ahead)
     for n in range(SIZE):
-        put(maps_ref, n, halves_of(top, whole_ahead[n], whole_behind[n]))
-    whole_mixed = plus(mixed, matmul(behind, matmul(swap(mixed), ahead)))
-    for n in range(0, SIZE, 2):
-        put(maps_ref, SIZE + n // 2, halves_of(top, whole_mixed[n], whole_mixed[min(n + 1, SIZE - 1)]))
-    edge_lines(sub, lane, rows(u_ref, 0, STEPS * VARS), last_ref, first_ref)
+        put(prefix_ref, n, whole[n])
+    whole = plus(mixed, matmul(behind, matmul(swap(mixed), ahead)))
+    for n in range(SIZE):
+        put(prefix_ref, SIZE + n, whole[n])
+    whole = matmul(behind, swap(behind))
+    for n in range(SIZE):
+        put(prefix_ref, 2 * SIZE + n, whole[n])
+    pack_lines(lines_ref, PACKED, block, rows(prefix_ref, 0, 3 * SIZE), VEC_GROUPS, FULL_GROUPS)
     up_ref[: VARS * 8, :] = u_ref[(STEPS - 1) * VARS * 8 :, :]
-    up_ref[VARS * 8 : (VARS + SIZE) * 8, :] = lines_ref[2 * MATRIX - SIZE * 8 : 2 * MATRIX, :]
-    up_ref[(VARS + SIZE) * 8 :, :] = u_ref[: VARS * 8, :]
+    up_ref[VARS * 8 :, :] = lines_ref[2 * MATRIX - SIZE * 8 : 2 * MATRIX, :]
+    down_ref[...] = u_ref[: VARS * 8, :]
 
 
 def cells_kernel(source_ref, flags_ref, pivot_raw, out_ref):
@@ -201,15 +209,15 @@
     matrix_to_packed(pivot_raw, out_ref, FIELD + STEPS * 8)
 
 
-def time_kernel(weights, u_ref, wait_ref, later_ref, out_ref, *later_out):
+def time_kernel(weights, u_ref, *rest):
     for v in range(VARS):
         fields = [row(u_ref, j * VARS + v) for j in range(INST)]
         for i in range(INST):
-            put(out_ref, i * VARS + v, total(fields[j] * F32(weights[i, j]) for j in range(INST)))
-    begin = 0
-    for ref in later_out:
-        ref[...] = later_ref[begin : begin + ref.shape[0], :]
-        begin += ref.shape[0]
+            put(rest[2], i * VARS + v, total(fields[j] * F32(weights[i, j]) for j in range(INST)))
+    if len(rest) > 3:
+        edges_ref, last_ref, first_ref = rest[3:]
+        last_ref[...] = row(edges_ref, 0)
+        first_ref[...] = row(edges_ref, 1)
 
 
 def stencil_kernel(u_ref, src_ref, below_ref, above_ref, left_ref, right_ref, out_ref):
@@ -239,9 +247,12 @@
             put(out_ref, n, value)
 
 
-def local_kernel(base_ref, time_ref, cells_ref, lines_ref, source_ref, ends_ref, packed_ref):
+def local_kernel(base_ref, time_ref, cells_ref, lines_ref, source_ref, packed_ref):
     sub, lane = iotas()
-    top = sub < TILES
+    block = lane // 32
+    groups = packed_ref.shape[0] // SEGMENTS
+    if groups == FULL_GROUPS:
+        packed_ref[...] = lines_ref[PACKED:, :]
     pivot_row = STEPS * VARS + STEPS
 
     def source_step(k, carry):
@@ -262,8 +273,8 @@
     for k in range(STEPS - 2, -1, -1):
         x = minus(kept[k], matvec(rows(lines_ref, (STEPS + k) * SIZE, SIZE), x))
     for v in range(VARS):
-        put(ends_ref, v, end[v])
-        put(ends_ref, VARS + v, x[v])
+        put(source_ref, STEPS * VARS + v, end[v])
+        put(source_ref, STEPS * VARS + VARS + v, x[v])
     base = 2 * STEPS * SIZE
     ahead = rows(lines_ref, base, SIZE)
     mixed = rows(lines_ref, base + SIZE, SIZE)
@@ -271,53 +282,88 @@
     whole_end = plus(swap(end), matvec(swap(ahead), end))
     inner = plus(swap(x), matvec(swap(mixed), end))
     whole_first = plus(x, matvec(behind, inner))
-    for v in range(VARS):
-        put(packed_ref, v, halves_of(top, whole_end[v], whole_first[v]))
-
-
-def interface(top, place, ends_ref, maps_ref, entry_ref):
+    values = whole_end + whole_first + [jnp.zeros((8, 128), F32)] * (4 * VEC_GROUPS - 2 * VARS)
+    pack_lines(packed_ref, 0, block, values, 0, groups)
+
+
+def shift_in(sub, values, entry):
+    return [jnp.where(sub == 0, e, pltpu.roll(x, 1, 0)) for x, e in zip(values, entry)]
+
+
+def shift_out(sub, values, entry):
+    return [jnp.where(sub == 7, e, pltpu.roll(x, 7, 0)) for x, e in zip(values, entry)]
+
+
+def reduced_kernel(first, recv_ref, maps_in_ref, out_ref, *rest):
+    sub, lane = iotas()
+    block = lane // 32
+    groups = FULL_GROUPS if first else VEC_GROUPS
+
+    def value(r, part):
+        stacked = recv_ref[pl.ds(part * 8 * groups + r // 4, 8, stride=groups), :]
+        return lane_roll(stacked, -32 * (r % 4))
+
+    if first:
+        maps_ref = rest[0]
+        for r in range(3 * SIZE):
+            for part in range(2):
+                put(maps_ref, part * 3 * SIZE + r, value(4 * VEC_GROUPS + r, part))
+    else:
+        maps_ref = maps_in_ref
     zero = [jnp.zeros((8, 128), F32)] * VARS
 
-    def pairs(d):
-        return rows(ends_ref, d * VARS, VARS)
-
-    def maps(d):
-        return rows(maps_ref, d * MAP_BLOCKS, SIZE)
-
-    def forward(d, e):
-        for v in range(VARS):
-            put(entry_ref, d * VARS + v, e[v])
-        return plus(pairs(d), matvec(maps(d), e))
-
-    last = lax.fori_loop(0, SEGMENTS - 1, forward, zero)
-    for v in range(VARS):
-        put(entry_ref, (SEGMENTS - 1) * VARS + v, last[v])
-
-    def backward(step, f):
-        d = SEGMENTS - 1 - step
-        mixed = rows(maps_ref, d * MAP_BLOCKS + SIZE, (SIZE + 1) // 2)
-        mixed = [mixed[n // 2] if n % 2 else pltpu.roll(mixed[n // 2], 4, 0) for n in range(SIZE)]
-        entry = swap(rows(entry_ref, d * VARS, VARS))
-        return plus(plus(pairs(d), matvec(mixed, entry)), matvec(maps(d), f))
-
-    after = lax.fori_loop(0, SEGMENTS - 1 - place, backward, zero)
-    entry = rows(entry_ref, place * VARS, VARS)
-    return both(top, entry), both_low(top, after)
-
-
-def finish_kernel(
-    last, place_ref, gathered_ref, maps_ref, u_ref, source_ref, ends_ref, lines_ref, *rest
-):
+    def solve(part, which, source, entry, shift):
+        maps = rows(maps_ref, part * 3 * SIZE + which * SIZE, SIZE)
+
+        def step(_, now):
+            return plus(source, matvec(maps, shift(sub, now, entry)))
+
+        out = lax.fori_loop(0, 7, step, plus(source, matvec(maps, shift(sub, zero, entry))))
+        return out, shift(sub, out, entry)
+
+    ends = [[value(r, part) for r in range(VARS)] for part in range(2)]
+    firsts = [[value(VARS + r, part) for r in range(VARS)] for part in range(2)]
+    out, low_entry = solve(0, 0, ends[0], zero, shift_in)
+    out, high_entry = solve(1, 0, ends[1], [pltpu.roll(x, 1, 0) for x in out], shift_in)
+    entries = [low_entry, high_entry]
+    drive = [
+        plus(firsts[part], matvec(rows(maps_ref, part * 3 * SIZE + SIZE, SIZE), entries[part])) for part in range(2)
+    ]
+    out, high_next = solve(1, 2, drive[1], zero, shift_out)
+    out, low_next = solve(0, 2, drive[0], [pltpu.roll(x, 7, 0) for x in out], shift_out)
+    nexts = [low_next, high_next]
+    for part in range(2):
+        values = entries[part] + nexts[part] + zero + zero[:1]
+        for g in range(VEC_GROUPS):
+            packed = blocks4(block, [lane_roll(values[4 * g + p], 32 * p) for p in range(4)])
+            out_ref[pl.ds(part * 8 * VEC_GROUPS + g, 8, stride=VEC_GROUPS), :] = packed
+
+
+def finish_kernel(last, recv_ref, u_ref, source_ref, lines_ref, *rest):
     if last:
-        out_ref, new_ref, entry_ref = rest
+        out_ref, new_ref = rest
     else:
-        up_ref, above_ref, new_ref, last_ref, first_ref, new_below_ref, new_above_ref, entry_ref = rest
+        up_ref, above_ref, new_ref, edges_ref, new_below_ref, new_above_ref = rest
     sub, lane = iotas()
+    block = lane // 32
     top = sub < TILES
-    entry, after = interface(top, place_ref[0], gathered_ref, maps_ref, entry_ref)
+    stacked = [
+        [
+            recv_ref[pl.ds(q * VEC_GROUPS + g, TILES, stride=4 * VEC_GROUPS), :]
+            for g in range((2 * VARS + 3) // 4)
+        ]
+        for q in range(4)
+    ]
+    stacked = [[jnp.concatenate([x, x], axis=0) for x in line] for line in stacked]
+
+    def value(r):
+        return blocks4(block, [lane_roll(stacked[q][r // 4], 32 * (q - r % 4)) for q in range(4)])
+
+    entry = [value(r) for r in range(VARS)]
+    after = [value(VARS + r) for r in range(VARS)]
     base = 2 * STEPS * SIZE
-    end = rows(ends_ref, 0, VARS)
-    begin = rows(ends_ref, VARS, VARS)
+    end = rows(source_ref, STEPS * VARS, VARS)
+    begin = rows(source_ref, STEPS * VARS + VARS, VARS)
     middle = plus(end, matvec(rows(lines_ref, base, SIZE), entry))
     start = pick(top, entry, swap(middle))
     follow = plus(
@@ -342,24 +388,19 @@
                     tile = new_ref[pl.ds(v * 8 + half * TILES + t, STEPS, stride=VARS * 8), :]
                     out_ref[v, half * STEPS : (half + 1) * STEPS, t * 128 : (t + 1) * 128] = tile
     else:
-        edge_lines(sub, lane, rows(new_ref, 0, STEPS * VARS), last_ref, first_ref)
+        edge_lines(sub, lane, rows(new_ref, 0, STEPS * VARS), edges_ref)
         before = minus(entry, matvec(rows(up_ref, VARS, SIZE), swap(x)))
         for v in range(VARS):
             put(new_below_ref, v, row(up_ref, v) + before[v])
             put(new_above_ref, v, row(above_ref, v) + after[v])
 
 
-def call(kernel, shapes, *args, scratch=(), flops=100_000, limit=8, place=None):
+def call(kernel, shapes, *args, scratch=(), flops=100_000, limit=8):
     outs = [jax.ShapeDtypeStruct(shape, F32) for shape in shapes]
     moved = 4 * (sum(math.prod(shape) for shape in shapes) + sum(a.size for a in args))
-    specs = [pl.BlockSpec(memory_space=pltpu.VMEM)] * len(args)
-    if place is not None:
-        specs.insert(0, pl.BlockSpec(memory_space=pltpu.SMEM))
-        args = (place,) + args
     return pl.pallas_call(
         kernel,
         out_shape=outs,
-        in_specs=specs,
         scratch_shapes=[pltpu.VMEM(shape, F32) for shape in scratch],
         cost_estimate=pl.CostEstimate(flops=flops, bytes_accessed=moved, transcendentals=0),
         compiler_params=pltpu.CompilerParams(vmem_limit_bytes=limit * 1024 * 1024),
@@ -380,62 +421,70 @@
 
 def body(state, source_terms, pivot_inverse, coupling, back_coupling, wall_flags):
     weights = np.float32(-0.5 * spectral())
-    place = lax.axis_index("axial").astype(jnp.int32).reshape(1)
     edge = (8, 128)
     halo = (VARS * 8, 128)
-    carried = ((VARS + SIZE) * 8, 128)
-    u, last_line, first_line, lines, maps, halos = call(
+    u, edges = call(pack_kernel, [(FIELD, 128), (16, 128)], state[0].transpose(1, 0, 2))
+    lines, up, above = call(
         maps_kernel,
-        [
-            (FIELD, 128), edge, edge, (2 * MATRIX + 3 * SIZE * 8, 128), (MAP_BLOCKS * 8, 128),
-            (carried[0] + halo[0], 128),
-        ],
-        state[0].transpose(1, 0, 2), coupling[0].transpose(1, 2, 0, 3), back_coupling[0].transpose(1, 2, 0, 3),
+        [(PACKED + SEGMENTS * FULL_GROUPS, 128), ((VARS + SIZE) * 8, 128), halo],
+        u, coupling[0].transpose(1, 2, 0, 3), back_coupling[0].transpose(1, 2, 0, 3),
         scratch=[(MATRIX, 128)],
         flops=8_000_000,
         limit=16,
     )
-    maps = lax.all_gather(maps, "axial", axis=0, tiled=True)
     (cells,) = call(
         cells_kernel,
         [(FIELD + STEPS * 8 + MATRIX, 128)],
         source_terms[0].transpose(1, 0, 2), wall_flags, pivot_inverse[0].transpose(1, 2, 0, 3),
     )
+    time_call = lambda *refs: time_kernel(weights, *refs)
     for sweep in range(SWEEPS):
+        first = sweep == 0
+        last = sweep == SWEEPS - 1
         spread = exchange(u, "inst", INST)
-        left = moved(last_line, "span", 1, True)
-        if sweep == 0:
-            right = moved(first_line, "span", -1, True)
-            term, up, above = call(
-                lambda a, b, c, *refs: time_kernel(weights, a, b, c, *refs),
-                [(FIELD, 128), carried, halo], spread, jnp.concatenate([left, right]), halos,
-            )
+        if first:
             up = moved(up, "axial", 1, False)
             above = moved(above, "axial", -1, False)
             below = up[: VARS * 8]
+            term, left, right = call(
+                lambda a, b, c, d, *outs: time_kernel(weights, a, b, c, outs[0], d, *outs[1:]),
+                [(FIELD, 128), edge, edge], spread, up, above, edges,
+            )
+            left = moved(left, "span", 1, True)
+            right = moved(right, "span", -1, True)
         else:
-            term, right = call(
-                lambda *refs: time_kernel(weights, *refs), [(FIELD, 128), edge], spread, left, first_line
-            )
-            right = moved(right, "span", -1, True)
+            left = moved(edges[:8], "span", 1, True)
+            right = moved(edges[8:], "span", -1, True)
+            (term,) = call(time_call, [(FIELD, 128)], spread, left, right)
         time = exchange(term, "inst", INST)
         (base,) = call(stencil_kernel, [(FIELD, 128)], u, cells, below, above, left, right)
-        source, ends, packed = call(
-            local_kernel, [(FIELD, 128), (2 * VARS * 8, 128), (VARS * 8, 128)], base, time, cells, lines
+        groups = FULL_GROUPS if first else VEC_GROUPS
+        source, packed = call(
+            local_kernel,
+            [(FIELD + 2 * VARS * 8, 128), (SEGMENTS * groups, 128)],
+            base, time, cells, lines,
         )
-        gathered = lax.all_gather(packed, "axial", axis=0, tiled=True)
-        last = sweep == SWEEPS - 1
-        common = (gathered, maps, u, source, ends, lines)
-        entries = (SEGMENTS * VARS * 8, 128)
+        recv = exchange(packed, "axial", SEGMENTS)
+        shapes = [(SEGMENTS * VEC_GROUPS, 128)]
+        if first:
+            shapes.append((6 * SIZE * 8, 128))
+        out = call(
+            lambda *refs, f=first: reduced_kernel(f, *((refs[0], None) + refs[1:] if f else refs)),
+            shapes, recv, *(() if first else (maps,)),
+        )
+        if first:
+            maps = out[1]
+        back_recv = exchange(out[0], "axial", SEGMENTS)
+        common = (back_recv, u, source, lines)
         if last:
             (result,) = call(
                 lambda *refs: finish_kernel(True, *refs), [(VARS, 2 * STEPS, TILES * 128)], *common,
-                scratch=[(FIELD, 128), entries], place=place,
+                scratch=[(FIELD, 128)],
             )
         else:
-            u, last_line, first_line, below, above = call(
-                lambda *refs: finish_kernel(False, *refs), [(FIELD, 128), edge, edge, halo, halo],
-                *common, up, above, scratch=[entries], place=place,
+            u, edges, below, above = call(
+                lambda *refs: finish_kernel(False, *refs), [(FIELD, 128), (16, 128), halo, halo],
+                *common, up, above,
             )
     return result.transpose(1, 0, 2)[None]
 

time: 132 us -> 136 us (1.030)
  blocking collectives: 38.2 us -> 52 us
  between operations: 13.5 us -> 0.2 us
  waiting for transfers between devices: 12.2 us -> 14.3 us
  local copies, waits for them, and re-layouts: 7.65 us -> 6.1 us
  Pallas kernels: 11.1 us -> 12.6 us
    all_to_all x0 -> x4, blocking collectives: none -> 52 us  [exchange(): lax.all_to_all(value.reshape(count, shape[0] // count, 128), axis, 0, 0)]
    all_gather x2 -> x0, blocking collectives: 38.2 us -> none  [body(): gathered = lax.all_gather(packed, 'axial', axis=0, tiled=True)]
    all_to_all x4, starting transfers between devices: 26.3 us -> 31.1 us  [exchange(): lax.all_to_all(value.reshape(count, shape[0] // count, 128), axis, 0, 0)]
    ppermute x6, starting transfers between devices: 22.1 us -> 18.5 us  [moved(): return lax.ppermute(value, axis, pairs)]
    all_to_all x4, waiting for transfers between devices: 5.44 us -> 7.23 us  [exchange(): lax.all_to_all(value.reshape(count, shape[0] // count, 128), axis, 0, 0)]
    pallas_call x10 -> x13, Pallas kernels: 11.1 us -> 12.6 us  [call(): pl.pallas_call(kernel, out_shape=outs, scratch_shapes=[pltpu.VMEM(shape,...]
    unnamed x20, local copies, waits for them, and re-layouts: 7.65 us -> 6.09 us
  transfers between devices with their start and end apart: 11 -> 10, of which waited for: 8 -> 3; matrix products, arithmetic and copies ran while one was open for 0% -> 0% of each run, Pallas kernels for 3% -> 4%
where the time goes in v3:
time: 136 us; the launch traced here: 135 us
  blocking collectives  52 us (38%)
  starting transfers between devices  49.6 us (36%)
  waiting for transfers between devices  14.3 us (11%)
  Pallas kernels  12.6 us (9%)
  local copies, waits for them, and re-layouts  6.1 us (4%)
    all_to_all x4, blocking collectives, exchange(): lax.all_to_all(value.reshape(count, shape[0] // count, 128), axis, 0, 0)  52 us
    all_to_all x4, starting transfers between devices, exchange(): lax.all_to_all(value.reshape(count, shape[0] // count, 128), axis, 0, 0)  31.1 us
    ppermute x6, starting transfers between devices, moved(): return lax.ppermute(value, axis, pairs)  18.5 us
    pallas_call x13, Pallas kernels, call(): pl.pallas_call(kernel, out_shape=outs, scratch_shapes=[pltpu.VMEM(shape,...  12.6 us
    all_to_all x4, waiting for transfers between devices, exchange(): lax.all_to_all(value.reshape(count, shape[0] // count, 128), axis, 0, 0)  7.23 us
    ppermute x6, waiting for transfers between devices, moved(): return lax.ppermute(value, axis, pairs)  7.1 us
    unnamed x20, local copies, waits for them, and re-layouts  6.09 us
  transfers between devices with their start and end apart: 10, of which 3 were waited for; matrix products, arithmetic and copies ran while one was open for 0% of the time, Pallas kernels for 4%

profile of v3, /device:TPU:1, one launch (start us, length us, event | category | flops | bytes accessed | tf_op | source)
XLA Modules:
  0.0 134.8 jit_solution(4817573807183437903)
XLA Ops:
  0.0 0.9 copy-done.7
  0.9 0.7 shard_map.64
  1.6 10.9 %all-to-all-start = ((f32[8,40,128]{2,1,0:T(8,128)}), f32[8,40,128]{2,1,0:T(8,128)S(1)}, u32[]{:S(2)}, u32[]{:S(2)}) async-start(f32[8,40,128]{2,1,0:T(8,128)} %bitcast.10), calls=%async_computation | async-start | bytes 327680 | tf_op jit(solution)/shard_map/all_to_all | solution.py:412
  12.5 1.1 copy-done
  13.7 1.1 copy-done.1
  14.8 2.4 %shard_map.66 = (f32[4184,128]{1,0:T(8,128)S(1)}, f32[240,128]{1,0:T(8,128)S(1)}, f32[40,128]{1,0:T(8,128)S(1)}) custom-call(f32[320,128]{1,0:T(8,128)} %get-tuple-element.23.u_ref.refs_1_, f32[5,5,16,512]{3,2,1,0:T(8,128)S(1)} %bitcast.34, f32[5,5,16,512]{3,2,1,0:T(8,128)S(1)} %bitcast.35), custom_call_target="tpu_custom_call" | custom-call | flops 8000000 | bytes 4087808 | tf_op jit(solution)/shard_map/pallas_call | solution.py:401
  17.2 4.0 %collective-permute-start = (f32[240,128]{1,0:T(8,128)S(1)}, f32[240,128]{1,0:T(8,128)S(1)}, u32[]{:S(2)}, u32[]{:S(2)}) collective-permute-start(f32[240,128]{1,0:T(8,128)S(1)} %get-tuple-element.24), channel_id=1, source_target_pairs={{0,4},{4,8},{8,12},{12,16},{16,20},{20,24},{24,28},{28,32},{32,36}... | collective-permute-start | bytes 368648 | tf_op jit(solution)/shard_map/ppermute | solution.py:419
  21.3 1.9 %collective-permute-start.1 = (f32[40,128]{1,0:T(8,128)S(1)}, f32[40,128]{1,0:T(8,128)S(1)}, u32[]{:S(2)}, u32[]{:S(2)}) collective-permute-start(f32[40,128]{1,0:T(8,128)S(1)} %get-tuple-element.25), channel_id=1, source_target_pairs={{4,0},{8,4},{12,8},{16,12},{20,16},{24,20},{28,24},{32,28},{36,32}... | collective-permute-start | bytes 61448 | tf_op jit(solution)/shard_map/ppermute | solution.py:419
  23.2 3.2 %collective-permute-done.1.c.above_ref.refs_5_ = f32[40,128]{1,0:T(8,128)S(1)} collective-permute-done((f32[40,128]{1,0:T(8,128)S(1)}, f32[40,128]{1,0:T(8,128)S(1)}, u32[]{:S(2)}, u32[]{:S(2)}) %collective-permute-start.1) | collective-permute-done | bytes 20512 | tf_op jit(solution)/shard_map/ppermute | solution.py:419
  26.4 0.7 shard_map.67
  27.1 6.9 %all-to-all-start.1 = ((f32[8,40,128]{2,1,0:T(8,128)}), f32[8,40,128]{2,1,0:T(8,128)S(1)}, u32[]{:S(2)}, u32[]{:S(2)}) async-start(f32[8,40,128]{2,1,0:T(8,128)} %bitcast.12), calls=%async_computation.1 | async-start | bytes 327680 | tf_op jit(solution)/shard_map/all_to_all | solution.py:412
  34.1 3.1 %collective-permute-start.2 = (f32[8,128]{1,0:T(8,128)S(1)}, f32[8,128]{1,0:T(8,128)S(1)}, u32[]{:S(2)}, u32[]{:S(2)}) collective-permute-start(f32[8,128]{1,0:T(8,128)S(1)} %get-tuple-element.27), channel_id=1, source_target_pairs={{0,1},{1,2},{2,3},{3,0},{4,5},{5,6},{6,7},{7,4},{8,9},{9,10},{10,1... | collective-permute-start | bytes 12296 | tf_op jit(solution)/shard_map/ppermute | solution.py:419
  37.2 3.4 %collective-permute-start.3 = (f32[8,128]{1,0:T(8,128)S(1)}, f32[8,128]{1,0:T(8,128)S(1)}, u32[]{:S(2)}, u32[]{:S(2)}) collective-permute-start(f32[8,128]{1,0:T(8,128)S(1)} %get-tuple-element.28), channel_id=1, source_target_pairs={{0,3},{1,0},{2,1},{3,2},{4,7},{5,4},{6,5},{7,6},{8,11},{9,8},{10,9... | collective-permute-start | bytes 12296 | tf_op jit(solution)/shard_map/ppermute | solution.py:419
  40.6 1.1 copy-done.2
  41.7 0.9 copy-done.8
  42.8 1.2 shard_map.68.base_ref
  44.4 18.1 %all_to_all.40 = f32[16,24,128]{2,1,0:T(8,128)S(1)} all-to-all(f32[16,24,128]{2,1,0:T(8,128)S(1)} %bitcast.42), channel_id=1, replica_groups=mesh['inst'=8,'axial'=16,'span'=4] {'axial'}, dimensions={0} | all-to-all | bytes 393216 | tf_op jit(solution)/shard_map/all_to_all | solution.py:412
  62.5 0.7 shard_map.70
  63.2 0.8 copy-done.3
  64.0 10.0 %all_to_all.41 = f32[16,4,128]{2,1,0:T(4,128)S(1)} all-to-all(f32[16,4,128]{2,1,0:T(4,128)S(1)} %bitcast.50), channel_id=1, replica_groups=mesh['inst'=8,'axial'=16,'span'=4] {'axial'}, dimensions={0} | all-to-all | bytes 65536 | tf_op jit(solution)/shard_map/all_to_all | solution.py:412
  74.0 1.8 %shard_map.71 = (f32[320,128]{1,0:T(8,128)}, f32[16,128]{1,0:T(8,128)S(1)}, f32[40,128]{1,0:T(8,128)S(1)}, f32[40,128]{1,0:T(8,128)S(1)}) custom-call(f32[64,128]{1,0:T(8,128)S(1)} %bitcast.45, f32[320,128]{1,0:T(8,128)} %get-tuple-element.23.u_ref.refs_1_, f32[400,128]{1,0:T(8,128)S(1)} %get-tuple-element.33.refs_2_, ...), custom_call_target="tpu_custom_call" | custom-call | flops 100000 | bytes 2899968 | tf_op jit(solution)/shard_map/pallas_call | solution.py:401
  75.9 6.9 %all-to-all-start.4 = ((f32[8,40,128]{2,1,0:T(8,128)}), f32[8,40,128]{2,1,0:T(8,128)S(1)}, u32[]{:S(2)}, u32[]{:S(2)}) async-start(f32[8,40,128]{2,1,0:T(8,128)} %bitcast.18), calls=%async_computation.4 | async-start | bytes 327680 | tf_op jit(solution)/shard_map/all_to_all | solution.py:412
  82.8 4.1 %collective-permute-start.5 = (f32[8,128]{1,0:T(8,128)S(1)}, f32[8,128]{1,0:T(8,128)S(1)}, u32[]{:S(2)}, u32[]{:S(2)}) collective-permute-start(f32[8,128]{1,0:T(8,128)S(1)} %get-tuple-element.41), channel_id=1, source_target_pairs={{0,3},{1,0},{2,1},{3,2},{4,7},{5,4},{6,5},{7,6},{8,11},{9,8},{10,9... | collective-permute-start | bytes 12296 | tf_op jit(solution)/shard_map/ppermute | solution.py:419
  86.9 1.9 %collective-permute-start.4 = (f32[8,128]{1,0:T(8,128)S(1)}, f32[8,128]{1,0:T(8,128)S(1)}, u32[]{:S(2)}, u32[]{:S(2)}) collective-permute-start(f32[8,128]{1,0:T(8,128)S(1)} %get-tuple-element.42), channel_id=1, source_target_pairs={{0,1},{1,2},{2,3},{3,0},{4,5},{5,6},{6,7},{7,4},{8,9},{9,10},{10,1... | collective-permute-start | bytes 12296 | tf_op jit(solution)/shard_map/ppermute | solution.py:419
  88.9 3.9 %collective-permute-done.4.left_ref.refs_1_ = f32[8,128]{1,0:T(8,128)S(1)} collective-permute-done((f32[8,128]{1,0:T(8,128)S(1)}, f32[8,128]{1,0:T(8,128)S(1)}, u32[]{:S(2)}, u32[]{:S(2)}) %collective-permute-start.4) | collective-permute-done | bytes 4128 | tf_op jit(solution)/shard_map/ppermute | solution.py:419
  92.8 0.7 shard_map.73
  93.5 6.3 %all-to-all-start.5 = ((f32[8,40,128]{2,1,0:T(8,128)}), f32[8,40,128]{2,1,0:T(8,128)S(1)}, u32[]{:S(2)}, u32[]{:S(2)}) async-start(f32[8,40,128]{2,1,0:T(8,128)} %bitcast.20), calls=%async_computation.5 | async-start | bytes 327680 | tf_op jit(solution)/shard_map/all_to_all | solution.py:412
  99.9 1.2 shard_map.72.base_ref
  101.0 7.2 %all-to-all-done.5 = f32[8,40,128]{2,1,0:T(8,128)S(1)} async-done(((f32[8,40,128]{2,1,0:T(8,128)}), f32[8,40,128]{2,1,0:T(8,128)S(1)}, u32[]{:S(2)}, u32[]{:S(2)}) %all-to-all-start.5) | async-done | bytes 163872 | tf_op jit(solution)/shard_map/all_to_all | solution.py:412
  108.6 13.6 %all_to_all.42 = f32[16,4,128]{2,1,0:T(4,128)S(1)} all-to-all(f32[16,4,128]{2,1,0:T(4,128)S(1)} %bitcast.49), channel_id=1, replica_groups=mesh['inst'=8,'axial'=16,'span'=4] {'axial'}, dimensions={0} | all-to-all | bytes 65536 | tf_op jit(solution)/shard_map/all_to_all | solution.py:412
  122.7 10.3 %all_to_all.43 = f32[16,4,128]{2,1,0:T(4,128)S(1)} all-to-all(f32[16,4,128]{2,1,0:T(4,128)S(1)} %bitcast.48), channel_id=1, replica_groups=mesh['inst'=8,'axial'=16,'span'=4] {'axial'}, dimensions={0} | all-to-all | bytes 65536 | tf_op jit(solution)/shard_map/all_to_all | solution.py:412
  133.0 1.8 %shard_map.76 = f32[5,16,512]{2,1,0:T(8,128)} custom-call(f32[64,128]{1,0:T(8,128)S(1)} %bitcast.46, f32[320,128]{1,0:T(8,128)} %get-tuple-element.34.u_ref.refs_1_, f32[400,128]{1,0:T(8,128)S(1)} %get-tuple-element.40.refs_2_, f32[4184,128]{1,0:T(8,128)S(1)} %get-tuple-element.30.lines_ref.refs_3_), custom_call_target="tpu_custom_call" | custom-call | flops 100000 | bytes 2707456 | tf_op jit(solution)/shard_map/pallas_call | solution.py:401
  (27 shorter events, 1.4 us)
Async XLA Ops:
  0.0 0.9 copy-start.7
  0.9 39.6 %copy-start.9 = (s32[16,512]{1,0:T(8,128)S(1)}, s32[16,512]{1,0:T(8,128)}, u32[]{:S(2)}) copy-start(s32[16,512]{1,0:T(8,128)} %flags_ref.1) | copy-start | bytes 98308
  1.6 24.7 %all-to-all-start = ((f32[8,40,128]{2,1,0:T(8,128)}), f32[8,40,128]{2,1,0:T(8,128)S(1)}, u32[]{:S(2)}, u32[]{:S(2)}) async-start(f32[8,40,128]{2,1,0:T(8,128)} %bitcast.10), calls=%async_computation | async-start | bytes 327680 | tf_op jit(solution)/shard_map/all_to_all | solution.py:412
  12.5 1.1 copy-start
  13.7 1.1 copy-start.1
  17.2 9.2 %collective-permute-start = (f32[240,128]{1,0:T(8,128)S(1)}, f32[240,128]{1,0:T(8,128)S(1)}, u32[]{:S(2)}, u32[]{:S(2)}) collective-permute-start(f32[240,128]{1,0:T(8,128)S(1)} %get-tuple-element.24), channel_id=1, source_target_pairs={{0,4},{4,8},{8,12},{12,16},{16,20},{20,24},{24,28},{28,32},{32,36}... | collective-permute-start | bytes 368648 | tf_op jit(solution)/shard_map/ppermute | solution.py:419
  21.3 5.1 %collective-permute-start.1 = (f32[40,128]{1,0:T(8,128)S(1)}, f32[40,128]{1,0:T(8,128)S(1)}, u32[]{:S(2)}, u32[]{:S(2)}) collective-permute-start(f32[40,128]{1,0:T(8,128)S(1)} %get-tuple-element.25), channel_id=1, source_target_pairs={{4,0},{8,4},{12,8},{16,12},{20,16},{24,20},{28,24},{32,28},{36,32}... | collective-permute-start | bytes 61448 | tf_op jit(solution)/shard_map/ppermute | solution.py:419
  26.4 16.5 %copy-start.5 = (f32[240,128]{1,0:T(8,128)}, f32[240,128]{1,0:T(8,128)S(1)}, u32[]{:S(2)}) copy-start(f32[240,128]{1,0:T(8,128)S(1)} %collective-permute-done.b.refs_4_) | copy-start | bytes 368644
  27.1 16.9 %all-to-all-start.1 = ((f32[8,40,128]{2,1,0:T(8,128)}), f32[8,40,128]{2,1,0:T(8,128)S(1)}, u32[]{:S(2)}, u32[]{:S(2)}) async-start(f32[8,40,128]{2,1,0:T(8,128)} %bitcast.12), calls=%async_computation.1 | async-start | bytes 327680 | tf_op jit(solution)/shard_map/all_to_all | solution.py:412
  34.1 8.8 %collective-permute-start.2 = (f32[8,128]{1,0:T(8,128)S(1)}, f32[8,128]{1,0:T(8,128)S(1)}, u32[]{:S(2)}, u32[]{:S(2)}) collective-permute-start(f32[8,128]{1,0:T(8,128)S(1)} %get-tuple-element.27), channel_id=1, source_target_pairs={{0,1},{1,2},{2,3},{3,0},{4,5},{5,6},{6,7},{7,4},{8,9},{9,10},{10,1... | collective-permute-start | bytes 12296 | tf_op jit(solution)/shard_map/ppermute | solution.py:419
  37.2 5.7 %collective-permute-start.3 = (f32[8,128]{1,0:T(8,128)S(1)}, f32[8,128]{1,0:T(8,128)S(1)}, u32[]{:S(2)}, u32[]{:S(2)}) collective-permute-start(f32[8,128]{1,0:T(8,128)S(1)} %get-tuple-element.28), channel_id=1, source_target_pairs={{0,3},{1,0},{2,1},{3,2},{4,7},{5,4},{6,5},{7,6},{8,11},{9,8},{10,9... | collective-permute-start | bytes 12296 | tf_op jit(solution)/shard_map/ppermute | solution.py:419
  40.6 1.1 copy-start.2
  41.7 0.9 copy-start.8
  44.0 30.0 %copy-start.6 = (f32[240,128]{1,0:T(8,128)S(1)}, f32[240,128]{1,0:T(8,128)}, u32[]{:S(2)}) copy-start(f32[240,128]{1,0:T(8,128)} %copy-done.5) | copy-start | bytes 368644
  63.2 0.8 copy-start.3
  75.9 16.9 %all-to-all-start.4 = ((f32[8,40,128]{2,1,0:T(8,128)}), f32[8,40,128]{2,1,0:T(8,128)S(1)}, u32[]{:S(2)}, u32[]{:S(2)}) async-start(f32[8,40,128]{2,1,0:T(8,128)} %bitcast.18), calls=%async_computation.4 | async-start | bytes 327680 | tf_op jit(solution)/shard_map/all_to_all | solution.py:412
  82.8 6.1 %collective-permute-start.5 = (f32[8,128]{1,0:T(8,128)S(1)}, f32[8,128]{1,0:T(8,128)S(1)}, u32[]{:S(2)}, u32[]{:S(2)}) collective-permute-start(f32[8,128]{1,0:T(8,128)S(1)} %get-tuple-element.41), channel_id=1, source_target_pairs={{0,3},{1,0},{2,1},{3,2},{4,7},{5,4},{6,5},{7,6},{8,11},{9,8},{10,9... | collective-permute-start | bytes 12296 | tf_op jit(solution)/shard_map/ppermute | solution.py:419
  86.9 5.9 %collective-permute-start.4 = (f32[8,128]{1,0:T(8,128)S(1)}, f32[8,128]{1,0:T(8,128)S(1)}, u32[]{:S(2)}, u32[]{:S(2)}) collective-permute-start(f32[8,128]{1,0:T(8,128)S(1)} %get-tuple-element.42), channel_id=1, source_target_pairs={{0,1},{1,2},{2,3},{3,0},{4,5},{5,6},{6,7},{7,4},{8,9},{9,10},{10,1... | collective-permute-start | bytes 12296 | tf_op jit(solution)/shard_map/ppermute | solution.py:419
  93.5 14.7 %all-to-all-start.5 = ((f32[8,40,128]{2,1,0:T(8,128)}), f32[8,40,128]{2,1,0:T(8,128)S(1)}, u32[]{:S(2)}, u32[]{:S(2)}) async-start(f32[8,40,128]{2,1,0:T(8,128)} %bitcast.20), calls=%async_computation.5 | async-start | bytes 327680 | tf_op jit(solution)/shard_map/all_to_all | solution.py:412
  108.3 13.9 %copy-start.4 = (f32[1200,128]{1,0:T(8,128)S(1)}, f32[1200,128]{1,0:T(8,128)}, u32[]{:S(2)}) copy-start(f32[1200,128]{1,0:T(8,128)} %copy-done.3) | copy-start | bytes 1843204

commit v4 on v3

--- a/solution.py
+++ b/solution.py
@@ -21,6 +21,10 @@
 FULL_GROUPS = 24
 VEC_GROUPS = 4
 PACKED = 2 * MATRIX + 3 * SIZE * 8
+CELLS = PACKED + SEGMENTS * FULL_GROUPS
+KEEP = CELLS + FIELD
+PIVOT = KEEP + STEPS * 8
+LINES = PIVOT + MATRIX
 
 
 def spectral():
@@ -141,16 +145,42 @@
                     out_ref[pl.ds(begin, STEPS, stride=SIZE * 8), :] = tile
 
 
-def pack_kernel(state_ref, u_ref, edges_ref):
+def fetch(source, target, sems, first):
+    copies = [pltpu.make_async_copy(source.at[i], target.at[i], sems.at[first + i]) for i in range(VARS)]
+    for copy in copies:
+        copy.start()
+    return copies
+
+
+def arrive(copies):
+    for copy in copies:
+        copy.wait()
+
+
+def pack_kernel(state_hbm, sent_ref, u_ref, edges_ref, state_ref, sems):
     sub, lane = iotas()
+    arrive(fetch(state_hbm, state_ref, sems, 0))
     field_to_packed(state_ref, u_ref)
+    sent_ref[...] = u_ref[...]
     edge_lines(sub, lane, rows(u_ref, 0, STEPS * VARS), edges_ref)
 
 
-def maps_kernel(u_ref, coupling_raw, back_raw, lines_ref, up_ref, down_ref, prefix_ref):
+def maps_kernel(
+    u_ref, coupling_hbm, back_hbm, pivot_hbm, source_hbm, flags_hbm,
+    lines_ref, halos_ref,
+    prefix_ref, coupling_raw, back_raw, pivot_raw, source_raw, flags_ref, sems,
+):
     sub, lane = iotas()
     block = lane // 32
+    flags_copy = pltpu.make_async_copy(flags_hbm, flags_ref, sems.at[4 * VARS])
+    coupling_copies = fetch(coupling_hbm, coupling_raw, sems, 0)
+    back_copies = fetch(back_hbm, back_raw, sems, VARS)
+    pivot_copies = fetch(pivot_hbm, pivot_raw, sems, 2 * VARS)
+    source_copies = fetch(source_hbm, source_raw, sems, 3 * VARS)
+    flags_copy.start()
+    arrive(coupling_copies)
     matrix_to_packed(coupling_raw, lines_ref, 0)
+    arrive(back_copies)
     matrix_to_packed(back_raw, lines_ref, MATRIX)
 
     def coupling(k):
@@ -195,32 +225,36 @@
     for n in range(SIZE):
         put(prefix_ref, 2 * SIZE + n, whole[n])
     pack_lines(lines_ref, PACKED, block, rows(prefix_ref, 0, 3 * SIZE), VEC_GROUPS, FULL_GROUPS)
-    up_ref[: VARS * 8, :] = u_ref[(STEPS - 1) * VARS * 8 :, :]
-    up_ref[VARS * 8 :, :] = lines_ref[2 * MATRIX - SIZE * 8 : 2 * MATRIX, :]
-    down_ref[...] = u_ref[: VARS * 8, :]
-
-
-def cells_kernel(source_ref, flags_ref, pivot_raw, out_ref):
-    field_to_packed(source_ref, out_ref, 0)
+    halos_ref[: VARS * 8, :] = u_ref[(STEPS - 1) * VARS * 8 :, :]
+    halos_ref[VARS * 8 : (VARS + SIZE) * 8, :] = lines_ref[2 * MATRIX - SIZE * 8 : 2 * MATRIX, :]
+    halos_ref[(VARS + SIZE) * 8 :, :] = u_ref[: VARS * 8, :]
+    arrive(pivot_copies)
+    matrix_to_packed(pivot_raw, lines_ref, PIVOT)
+    arrive(source_copies)
+    field_to_packed(source_raw, lines_ref, CELLS)
+    flags_copy.wait()
     for half in range(2):
         for t in range(TILES):
             flags = flags_ref[half * STEPS : (half + 1) * STEPS, t * 128 : (t + 1) * 128]
-            out_ref[pl.ds(FIELD + half * TILES + t, STEPS, stride=8), :] = (1 - flags).astype(F32)
-    matrix_to_packed(pivot_raw, out_ref, FIELD + STEPS * 8)
-
-
-def time_kernel(weights, u_ref, *rest):
+            lines_ref[pl.ds(KEEP + half * TILES + t, STEPS, stride=8), :] = (1 - flags).astype(F32)
+
+
+def time_kernel(weights, count, u_ref, *rest):
+    out_ref = rest[count]
     for v in range(VARS):
         fields = [row(u_ref, j * VARS + v) for j in range(INST)]
         for i in range(INST):
-            put(rest[2], i * VARS + v, total(fields[j] * F32(weights[i, j]) for j in range(INST)))
-    if len(rest) > 3:
-        edges_ref, last_ref, first_ref = rest[3:]
-        last_ref[...] = row(edges_ref, 0)
-        first_ref[...] = row(edges_ref, 1)
-
-
-def stencil_kernel(u_ref, src_ref, below_ref, above_ref, left_ref, right_ref, out_ref):
+            put(out_ref, i * VARS + v, total(fields[j] * F32(weights[i, j]) for j in range(INST)))
+    outs = list(rest[count + 1 :])
+    for ref in rest[:count]:
+        begin = 0
+        while begin < ref.shape[0]:
+            out = outs.pop(0)
+            out[...] = ref[begin : begin + out.shape[0], :]
+            begin += out.shape[0]
+
+
+def stencil_kernel(u_ref, lines_ref, below_ref, above_ref, left_ref, right_ref, out_ref):
     sub, lane = iotas()
     top = sub < TILES
     left_all = left_ref[...]
@@ -243,22 +277,21 @@
             turned = pltpu.roll(u, 127, 1)
             edge = jnp.where(sub % TILES == TILES - 1, lane_roll(right_all, 127 - n), pltpu.roll(turned, 7, 0))
             right = jnp.where(lane == 127, edge, turned)
-            value = row(src_ref, n) - 0.1 * above + 0.5 * below - 0.8 * u + 0.2 * (left + right)
+            value = row(lines_ref, CELLS // 8 + n) - 0.1 * above + 0.5 * below - 0.8 * u + 0.2 * (left + right)
             put(out_ref, n, value)
 
 
-def local_kernel(base_ref, time_ref, cells_ref, lines_ref, source_ref, packed_ref):
+def local_kernel(base_ref, time_ref, lines_ref, source_ref, packed_ref):
     sub, lane = iotas()
     block = lane // 32
     groups = packed_ref.shape[0] // SEGMENTS
     if groups == FULL_GROUPS:
-        packed_ref[...] = lines_ref[PACKED:, :]
-    pivot_row = STEPS * VARS + STEPS
+        packed_ref[...] = lines_ref[PACKED:CELLS, :]
 
     def source_step(k, carry):
-        keep = row(cells_ref, STEPS * VARS + k)
+        keep = row(lines_ref, KEEP // 8 + k)
         rhs = [keep * (row(base_ref, k * VARS + v) + row(time_ref, k * VARS + v)) for v in range(VARS)]
-        for v, value in enumerate(matvec(rows(cells_ref, pivot_row + k * SIZE, SIZE), rhs)):
+        for v, value in enumerate(matvec(rows(lines_ref, PIVOT // 8 + k * SIZE, SIZE), rhs)):
             put(source_ref, k * VARS + v, value)
         return carry
 
@@ -294,22 +327,22 @@
     return [jnp.where(sub == 7, e, pltpu.roll(x, 7, 0)) for x, e in zip(values, entry)]
 
 
-def reduced_kernel(first, recv_ref, maps_in_ref, out_ref, *rest):
+def reduced_kernel(first, recv_ref, *rest):
+    maps_recv_ref = recv_ref if first else rest[0]
+    out_ref, maps_ref = rest[-2:]
     sub, lane = iotas()
     block = lane // 32
-    groups = FULL_GROUPS if first else VEC_GROUPS
+
+    def stacked(ref, groups, r, part):
+        values = ref[pl.ds(part * 8 * groups + r // 4, 8, stride=groups), :]
+        return lane_roll(values, -32 * (r % 4))
 
     def value(r, part):
-        stacked = recv_ref[pl.ds(part * 8 * groups + r // 4, 8, stride=groups), :]
-        return lane_roll(stacked, -32 * (r % 4))
-
-    if first:
-        maps_ref = rest[0]
-        for r in range(3 * SIZE):
-            for part in range(2):
-                put(maps_ref, part * 3 * SIZE + r, value(4 * VEC_GROUPS + r, part))
-    else:
-        maps_ref = maps_in_ref
+        return stacked(recv_ref, FULL_GROUPS if first else VEC_GROUPS, r, part)
+
+    for r in range(3 * SIZE):
+        for part in range(2):
+            put(maps_ref, part * 3 * SIZE + r, stacked(maps_recv_ref, FULL_GROUPS, 4 * VEC_GROUPS + r, part))
     zero = [jnp.zeros((8, 128), F32)] * VARS
 
     def solve(part, which, source, entry, shift):
@@ -395,13 +428,16 @@
             put(new_above_ref, v, row(above_ref, v) + after[v])
 
 
-def call(kernel, shapes, *args, scratch=(), flops=100_000, limit=8):
+def call(kernel, shapes, *args, scratch=(), flops=100_000, limit=8, far=0):
     outs = [jax.ShapeDtypeStruct(shape, F32) for shape in shapes]
     moved = 4 * (sum(math.prod(shape) for shape in shapes) + sum(a.size for a in args))
+    near = len(args) - far
+    specs = [pl.BlockSpec(memory_space=pltpu.VMEM if n < near else pltpu.HBM) for n in range(len(args))]
     return pl.pallas_call(
         kernel,
         out_shape=outs,
-        scratch_shapes=[pltpu.VMEM(shape, F32) for shape in scratch],
+        in_specs=specs,
+        scratch_shapes=[pltpu.VMEM(item, F32) if isinstance(item, tuple) else item for item in scratch],
         cost_estimate=pl.CostEstimate(flops=flops, bytes_accessed=moved, transcendentals=0),
         compiler_params=pltpu.CompilerParams(vmem_limit_bytes=limit * 1024 * 1024),
     )(*args)
@@ -423,69 +459,72 @@
     weights = np.float32(-0.5 * spectral())
     edge = (8, 128)
     halo = (VARS * 8, 128)
-    u, edges = call(pack_kernel, [(FIELD, 128), (16, 128)], state[0].transpose(1, 0, 2))
-    lines, up, above = call(
+    up_shape = ((VARS + SIZE) * 8, 128)
+    raw_field = (VARS, 2 * STEPS, TILES * 128)
+    raw_matrix = (VARS,) + raw_field
+    sent, u, edges = call(
+        pack_kernel, [(FIELD, 128), (FIELD, 128), (16, 128)], state[0].transpose(1, 0, 2),
+        scratch=[raw_field, pltpu.SemaphoreType.DMA((VARS,))], far=1,
+    )
+    lines, halos = call(
         maps_kernel,
-        [(PACKED + SEGMENTS * FULL_GROUPS, 128), ((VARS + SIZE) * 8, 128), halo],
+        [(LINES, 128), (up_shape[0] + halo[0], 128)],
         u, coupling[0].transpose(1, 2, 0, 3), back_coupling[0].transpose(1, 2, 0, 3),
-        scratch=[(MATRIX, 128)],
+        pivot_inverse[0].transpose(1, 2, 0, 3), source_terms[0].transpose(1, 0, 2), wall_flags,
+        scratch=[
+            (MATRIX, 128), raw_matrix, raw_matrix, raw_matrix, raw_field,
+            pltpu.VMEM((2 * STEPS, TILES * 128), jnp.int32), pltpu.SemaphoreType.DMA((4 * VARS + 1,)),
+        ],
         flops=8_000_000,
         limit=16,
+        far=5,
     )
-    (cells,) = call(
-        cells_kernel,
-        [(FIELD + STEPS * 8 + MATRIX, 128)],
-        source_terms[0].transpose(1, 0, 2), wall_flags, pivot_inverse[0].transpose(1, 2, 0, 3),
-    )
-    time_call = lambda *refs: time_kernel(weights, *refs)
     for sweep in range(SWEEPS):
         first = sweep == 0
         last = sweep == SWEEPS - 1
-        spread = exchange(u, "inst", INST)
+        spread = exchange(sent, "inst", INST)
         if first:
+            term, left, right, up, above = call(
+                lambda *refs: time_kernel(weights, 2, *refs),
+                [(FIELD, 128), edge, edge, up_shape, halo], spread, edges, halos,
+            )
             up = moved(up, "axial", 1, False)
             above = moved(above, "axial", -1, False)
             below = up[: VARS * 8]
+        else:
             term, left, right = call(
-                lambda a, b, c, d, *outs: time_kernel(weights, a, b, c, outs[0], d, *outs[1:]),
-                [(FIELD, 128), edge, edge], spread, up, above, edges,
+                lambda *refs: time_kernel(weights, 1, *refs), [(FIELD, 128), edge, edge], spread, edges
             )
-            left = moved(left, "span", 1, True)
-            right = moved(right, "span", -1, True)
-        else:
-            left = moved(edges[:8], "span", 1, True)
-            right = moved(edges[8:], "span", -1, True)
-            (term,) = call(time_call, [(FIELD, 128)], spread, left, right)
+        left = moved(left, "span", 1, True)
+        right = moved(right, "span", -1, True)
         time = exchange(term, "inst", INST)
-        (base,) = call(stencil_kernel, [(FIELD, 128)], u, cells, below, above, left, right)
+        (base,) = call(stencil_kernel, [(FIELD, 128)], u, lines, below, above, left, right)
         groups = FULL_GROUPS if first else VEC_GROUPS
         source, packed = call(
             local_kernel,
             [(FIELD + 2 * VARS * 8, 128), (SEGMENTS * groups, 128)],
-            base, time, cells, lines,
+            base, time, lines,
         )
         recv = exchange(packed, "axial", SEGMENTS)
-        shapes = [(SEGMENTS * VEC_GROUPS, 128)]
         if first:
-            shapes.append((6 * SIZE * 8, 128))
-        out = call(
-            lambda *refs, f=first: reduced_kernel(f, *((refs[0], None) + refs[1:] if f else refs)),
-            shapes, recv, *(() if first else (maps,)),
+            maps_recv = recv
+        (solved,) = call(
+            lambda *refs, f=first: reduced_kernel(f, *refs),
+            [(SEGMENTS * VEC_GROUPS, 128)], recv, *(() if first else (maps_recv,)),
+            scratch=[(6 * SIZE * 8, 128)],
         )
-        if first:
-            maps = out[1]
-        back_recv = exchange(out[0], "axial", SEGMENTS)
+        back_recv = exchange(solved, "axial", SEGMENTS)
         common = (back_recv, u, source, lines)
         if last:
             (result,) = call(
-                lambda *refs: finish_kernel(True, *refs), [(VARS, 2 * STEPS, TILES * 128)], *common,
-                scratch=[(FIELD, 128)],
+                lambda *refs: finish_kernel(True, *refs), [raw_field], *common, scratch=[(FIELD, 128)],
             )
         else:
             u, edges, below, above = call(
                 lambda *refs: finish_kernel(False, *refs), [(FIELD, 128), (16, 128), halo, halo],
                 *common, up, above,
             )
+            sent = u
     return result.transpose(1, 0, 2)[None]
 
 

time: 136 us -> 141 us (1.037)
  blocking collectives: 52 us -> 69.1 us
  waiting for transfers between devices: 14.3 us -> 1.66 us
  local copies, waits for them, and re-layouts: 6.1 us -> 16.4 us
  starting transfers between devices: 49.6 us -> 41 us
    all_to_all x4 -> x5, blocking collectives: 52 us -> 69.1 us  [exchange(): lax.all_to_all(value.reshape(count, shape[0] // count, 128), axis, 0, 0)]
    unnamed x20 -> x48, local copies, waits for them, and re-layouts: 6.09 us -> 16.4 us
    all_to_all x4 -> x3, starting transfers between devices: 31.1 us -> 21.5 us  [exchange(): lax.all_to_all(value.reshape(count, shape[0] // count, 128), axis, 0, 0)]
    all_to_all x4 -> x3, waiting for transfers between devices: 7.23 us -> 0.01 us  [exchange(): lax.all_to_all(value.reshape(count, shape[0] // count, 128), axis, 0, 0)]
    ppermute x6, waiting for transfers between devices: 7.1 us -> 1.65 us  [moved(): return lax.ppermute(value, axis, pairs)]
    pallas_call x13 -> x12, Pallas kernels: 12.6 us -> 11.6 us  [call(): pl.pallas_call(kernel, out_shape=outs, in_specs=specs, scratch_shapes=[pl...]
  transfers between devices with their start and end apart: 10 -> 9, of which waited for: 3 -> 2; matrix products, arithmetic and copies ran while one was open for 0% -> 0% of each run, Pallas kernels for 4% -> 4%
where the time goes in v4:
time: 141 us; the launch traced here: 140 us
  blocking collectives  69.1 us (49%)
  starting transfers between devices  41 us (29%)
  local copies, waits for them, and re-layouts  16.4 us (12%)
  Pallas kernels  11.6 us (8%)
  waiting for transfers between devices  1.66 us (1%)
    all_to_all x5, blocking collectives, exchange(): lax.all_to_all(value.reshape(count, shape[0] // count, 128), axis, 0, 0)  69.1 us
    all_to_all x3, starting transfers between devices, exchange(): lax.all_to_all(value.reshape(count, shape[0] // count, 128), axis, 0, 0)  21.5 us
    ppermute x6, starting transfers between devices, moved(): return lax.ppermute(value, axis, pairs)  19.5 us
    unnamed x48, local copies, waits for them, and re-layouts  16.4 us
    pallas_call x12, Pallas kernels, call(): pl.pallas_call(kernel, out_shape=outs, in_specs=specs, scratch_shapes=[pl...  11.6 us
  transfers between devices with their start and end apart: 9, of which 2 were waited for; matrix products, arithmetic and copies ran while one was open for 0% of the time, Pallas kernels for 4%

profile of v4, /device:TPU:1, one launch (start us, length us, event | category | flops | bytes accessed | tf_op | source)
XLA Modules:
  0.0 140.0 jit_solution(17965539046962953056)
XLA Ops:
  0.0 0.9 copy-done.13
  0.9 1.0 shard_map.64
  1.9 10.9 %all-to-all-start = ((f32[8,40,128]{2,1,0:T(8,128)}), f32[8,40,128]{2,1,0:T(8,128)S(1)}, u32[]{:S(2)}, u32[]{:S(2)}) async-start(f32[8,40,128]{2,1,0:T(8,128)} %bitcast.10), calls=%async_computation | async-start | bytes 327680 | tf_op jit(solution)/shard_map/all_to_all | solution.py:448
  12.8 1.1 copy-done.3
  13.9 1.1 copy-done.4
  15.1 1.1 copy-done.5
  16.2 0.9 copy-done.12
  17.1 0.8 copy-done.18
  17.9 5.2 %shard_map.65 = (f32[6168,128]{1,0:T(8,128)S(1)}, f32[280,128]{1,0:T(8,128)S(1)}) custom-call(f32[320,128]{1,0:T(8,128)S(1)} %get-tuple-element.26.u_ref.refs_1_, f32[5,5,16,512]{3,2,1,0:T(8,128)S(1)} %bitcast.37, f32[5,5,16,512]{3,2,1,0:T(8,128)S(1)} %bitcast.38, f32[5,5,16,512]{3,2,1,0:T(8,128)S(1)} %bitcast.39, f32[5,16,512]{2,1,0:T(8,128)S(1)} %bitcast.44, ...), custom_call_target="tpu_custom_call" | custom-call | flops 8000000 | bytes 6119424 | tf_op jit(solution)/shard_map/pallas_call | solution.py:436
  23.8 0.9 copy-done.17
  26.6 6.6 %all-to-all-start.1 = ((f32[8,40,128]{2,1,0:T(8,128)}), f32[8,40,128]{2,1,0:T(8,128)S(1)}, u32[]{:S(2)}, u32[]{:S(2)}) async-start(f32[8,40,128]{2,1,0:T(8,128)} %bitcast.46), calls=%async_computation.1 | async-start | bytes 327680 | tf_op jit(solution)/shard_map/all_to_all | solution.py:448
  33.3 4.6 %collective-permute-start = (f32[240,128]{1,0:T(8,128)}, f32[240,128]{1,0:T(8,128)S(1)}, u32[]{:S(2)}, u32[]{:S(2)}) collective-permute-start(f32[240,128]{1,0:T(8,128)} %copy-done.23), channel_id=1, source_target_pairs={{0,4},{4,8},{8,12},{12,16},{16,20},{20,24},{24,28},{28,32},{32,36}... | collective-permute-start | bytes 368648 | tf_op jit(solution)/shard_map/ppermute | solution.py:455
  37.9 1.9 %collective-permute-start.1 = (f32[40,128]{1,0:T(8,128)}, f32[40,128]{1,0:T(8,128)S(1)}, u32[]{:S(2)}, u32[]{:S(2)}) collective-permute-start(f32[40,128]{1,0:T(8,128)} %get-tuple-element.32), channel_id=1, source_target_pairs={{4,0},{8,4},{12,8},{16,12},{20,16},{24,20},{28,24},{32,28},{36,32}... | collective-permute-start | bytes 61448 | tf_op jit(solution)/shard_map/ppermute | solution.py:455
  39.8 3.1 %collective-permute-start.2 = (f32[8,128]{1,0:T(8,128)S(1)}, f32[8,128]{1,0:T(8,128)S(1)}, u32[]{:S(2)}, u32[]{:S(2)}) collective-permute-start(f32[8,128]{1,0:T(8,128)S(1)} %get-tuple-element.33), channel_id=1, source_target_pairs={{0,1},{1,2},{2,3},{3,0},{4,5},{5,6},{6,7},{7,4},{8,9},{9,10},{10,1... | collective-permute-start | bytes 12296 | tf_op jit(solution)/shard_map/ppermute | solution.py:455
  42.9 3.4 %collective-permute-start.3 = (f32[8,128]{1,0:T(8,128)S(1)}, f32[8,128]{1,0:T(8,128)S(1)}, u32[]{:S(2)}, u32[]{:S(2)}) collective-permute-start(f32[8,128]{1,0:T(8,128)S(1)} %get-tuple-element.34), channel_id=1, source_target_pairs={{0,3},{1,0},{2,1},{3,2},{4,7},{5,4},{6,5},{7,6},{8,11},{9,8},{10,9... | collective-permute-start | bytes 12296 | tf_op jit(solution)/shard_map/ppermute | solution.py:455
  48.2 0.9 copy-done.9
  49.5 20.4 %all_to_all.40 = f32[16,24,128]{2,1,0:T(8,128)S(1)} all-to-all(f32[16,24,128]{2,1,0:T(8,128)S(1)} %bitcast.43), channel_id=1, replica_groups=mesh['inst'=8,'axial'=16,'span'=4] {'axial'}, dimensions={0} | all-to-all | bytes 393216 | tf_op jit(solution)/shard_map/all_to_all | solution.py:448
  69.9 0.7 shard_map.69
  70.6 10.1 %all_to_all.41 = f32[16,4,128]{2,1,0:T(4,128)S(1)} all-to-all(f32[16,4,128]{2,1,0:T(4,128)S(1)} %bitcast.50), channel_id=1, replica_groups=mesh['inst'=8,'axial'=16,'span'=4] {'axial'}, dimensions={0} | all-to-all | bytes 65536 | tf_op jit(solution)/shard_map/all_to_all | solution.py:448
  81.0 15.3 %all_to_all.42 = f32[8,40,128]{2,1,0:T(8,128)S(1)} all-to-all(f32[8,40,128]{2,1,0:T(8,128)S(1)} %bitcast.36), channel_id=1, replica_groups=mesh['inst'=8,'axial'=16,'span'=4] {'inst'}, dimensions={0} | all-to-all | bytes 327680 | tf_op jit(solution)/shard_map/all_to_all | solution.py:448
  97.7 4.0 %all-to-all-start.5 = ((f32[8,40,128]{2,1,0:T(8,128)}), f32[8,40,128]{2,1,0:T(8,128)}, u32[]{:S(2)}, u32[]{:S(2)}) async-start(f32[8,40,128]{2,1,0:T(8,128)} %bitcast.47), calls=%async_computation.5 | async-start | bytes 327680 | tf_op jit(solution)/shard_map/all_to_all | solution.py:448
  101.7 3.1 %collective-permute-start.4 = (f32[8,128]{1,0:T(8,128)S(1)}, f32[8,128]{1,0:T(8,128)S(1)}, u32[]{:S(2)}, u32[]{:S(2)}) collective-permute-start(f32[8,128]{1,0:T(8,128)S(1)} %get-tuple-element.42), channel_id=1, source_target_pairs={{0,1},{1,2},{2,3},{3,0},{4,5},{5,6},{6,7},{7,4},{8,9},{9,10},{10,1... | collective-permute-start | bytes 12296 | tf_op jit(solution)/shard_map/ppermute | solution.py:455
  104.9 3.4 %collective-permute-start.5 = (f32[8,128]{1,0:T(8,128)S(1)}, f32[8,128]{1,0:T(8,128)S(1)}, u32[]{:S(2)}, u32[]{:S(2)}) collective-permute-start(f32[8,128]{1,0:T(8,128)S(1)} %get-tuple-element.43), channel_id=1, source_target_pairs={{0,3},{1,0},{2,1},{3,2},{4,7},{5,4},{6,5},{7,6},{8,11},{9,8},{10,9... | collective-permute-start | bytes 12296 | tf_op jit(solution)/shard_map/ppermute | solution.py:455
  108.3 1.3 collective-permute-done.5.right_ref
  109.6 0.9 copy-done.1
  110.5 0.7 copy-done.20
  111.3 0.7 copy-done.22
  112.9 0.9 copy-done.7
  113.8 1.2 shard_map.73
  115.1 13.0 %all_to_all.43 = f32[16,4,128]{2,1,0:T(4,128)S(1)} all-to-all(f32[16,4,128]{2,1,0:T(4,128)S(1)} %bitcast.53), channel_id=1, replica_groups=mesh['inst'=8,'axial'=16,'span'=4] {'axial'}, dimensions={0} | all-to-all | bytes 65536 | tf_op jit(solution)/shard_map/all_to_all | solution.py:448
  128.8 10.3 %all_to_all.44 = f32[16,4,128]{2,1,0:T(4,128)S(1)} all-to-all(f32[16,4,128]{2,1,0:T(4,128)S(1)} %bitcast.52), channel_id=1, replica_groups=mesh['inst'=8,'axial'=16,'span'=4] {'axial'}, dimensions={0} | all-to-all | bytes 65536 | tf_op jit(solution)/shard_map/all_to_all | solution.py:448
  139.1 0.9 shard_map.75
  (52 shorter events, 8.1 us)
Async XLA Ops:
  0.0 0.9 copy-start.13
  1.9 21.9 %all-to-all-start = ((f32[8,40,128]{2,1,0:T(8,128)}), f32[8,40,128]{2,1,0:T(8,128)S(1)}, u32[]{:S(2)}, u32[]{:S(2)}) async-start(f32[8,40,128]{2,1,0:T(8,128)} %bitcast.10), calls=%async_computation | async-start | bytes 327680 | tf_op jit(solution)/shard_map/all_to_all | solution.py:448
  12.8 1.1 copy-start.3
  13.9 1.1 copy-start.4
  15.1 1.1 copy-start.5
  16.2 0.9 copy-start.12
  17.1 0.8 copy-start.18
  23.1 0.6 copy-start.16
  23.8 0.9 copy-start.17
  25.3 0.7 copy-start.14
  26.6 21.6 %all-to-all-start.1 = ((f32[8,40,128]{2,1,0:T(8,128)}), f32[8,40,128]{2,1,0:T(8,128)S(1)}, u32[]{:S(2)}, u32[]{:S(2)}) async-start(f32[8,40,128]{2,1,0:T(8,128)} %bitcast.46), calls=%async_computation.1 | async-start | bytes 327680 | tf_op jit(solution)/shard_map/all_to_all | solution.py:448
  33.3 13.0 %collective-permute-start = (f32[240,128]{1,0:T(8,128)}, f32[240,128]{1,0:T(8,128)S(1)}, u32[]{:S(2)}, u32[]{:S(2)}) collective-permute-start(f32[240,128]{1,0:T(8,128)} %copy-done.23), channel_id=1, source_target_pairs={{0,4},{4,8},{8,12},{12,16},{16,20},{20,24},{24,28},{28,32},{32,36}... | collective-permute-start | bytes 368648 | tf_op jit(solution)/shard_map/ppermute | solution.py:455
  37.9 9.4 %collective-permute-start.1 = (f32[40,128]{1,0:T(8,128)}, f32[40,128]{1,0:T(8,128)S(1)}, u32[]{:S(2)}, u32[]{:S(2)}) collective-permute-start(f32[40,128]{1,0:T(8,128)} %get-tuple-element.32), channel_id=1, source_target_pairs={{4,0},{8,4},{12,8},{16,12},{20,16},{24,20},{28,24},{32,28},{36,32}... | collective-permute-start | bytes 61448 | tf_op jit(solution)/shard_map/ppermute | solution.py:455
  39.8 7.2 %collective-permute-start.2 = (f32[8,128]{1,0:T(8,128)S(1)}, f32[8,128]{1,0:T(8,128)S(1)}, u32[]{:S(2)}, u32[]{:S(2)}) collective-permute-start(f32[8,128]{1,0:T(8,128)S(1)} %get-tuple-element.33), channel_id=1, source_target_pairs={{0,1},{1,2},{2,3},{3,0},{4,5},{5,6},{6,7},{7,4},{8,9},{9,10},{10,1... | collective-permute-start | bytes 12296 | tf_op jit(solution)/shard_map/ppermute | solution.py:455
  42.9 4.4 %collective-permute-start.3 = (f32[8,128]{1,0:T(8,128)S(1)}, f32[8,128]{1,0:T(8,128)S(1)}, u32[]{:S(2)}, u32[]{:S(2)}) collective-permute-start(f32[8,128]{1,0:T(8,128)S(1)} %get-tuple-element.34), channel_id=1, source_target_pairs={{0,3},{1,0},{2,1},{3,2},{4,7},{5,4},{6,5},{7,6},{8,11},{9,8},{10,9... | collective-permute-start | bytes 12296 | tf_op jit(solution)/shard_map/ppermute | solution.py:455
  46.3 0.7 copy-start.10
  47.5 0.7 copy-start.8
  48.2 0.9 copy-start.9
  49.1 31.5 %copy-start.11 = (f32[240,128]{1,0:T(8,128)S(1)}, f32[240,128]{1,0:T(8,128)}, u32[]{:S(2)}) copy-start(f32[240,128]{1,0:T(8,128)} %copy-done.10) | copy-start | bytes 368644
  81.0 16.1 %copy-start.19 = (f32[40,128]{1,0:T(8,128)}, f32[40,128]{1,0:T(8,128)S(1)}, u32[]{:S(2)}) copy-start(f32[40,128]{1,0:T(8,128)S(1)} %get-tuple-element.39.below_ref) | copy-start | bytes 61444
  81.0 16.7 %copy-start.21 = (f32[40,128]{1,0:T(8,128)}, f32[40,128]{1,0:T(8,128)S(1)}, u32[]{:S(2)}) copy-start(f32[40,128]{1,0:T(8,128)S(1)} %get-tuple-element.40.above_ref) | copy-start | bytes 61444
  96.3 0.7 copy-start
  97.0 0.7 copy-start.15
  97.7 15.2 %all-to-all-start.5 = ((f32[8,40,128]{2,1,0:T(8,128)}), f32[8,40,128]{2,1,0:T(8,128)}, u32[]{:S(2)}, u32[]{:S(2)}) async-start(f32[8,40,128]{2,1,0:T(8,128)} %bitcast.47), calls=%async_computation.5 | async-start | bytes 327680 | tf_op jit(solution)/shard_map/all_to_all | solution.py:448
  101.7 6.5 %collective-permute-start.4 = (f32[8,128]{1,0:T(8,128)S(1)}, f32[8,128]{1,0:T(8,128)S(1)}, u32[]{:S(2)}, u32[]{:S(2)}) collective-permute-start(f32[8,128]{1,0:T(8,128)S(1)} %get-tuple-element.42), channel_id=1, source_target_pairs={{0,1},{1,2},{2,3},{3,0},{4,5},{5,6},{6,7},{7,4},{8,9},{9,10},{10,1... | collective-permute-start | bytes 12296 | tf_op jit(solution)/shard_map/ppermute | solution.py:455
  104.9 4.8 %collective-permute-start.5 = (f32[8,128]{1,0:T(8,128)S(1)}, f32[8,128]{1,0:T(8,128)S(1)}, u32[]{:S(2)}, u32[]{:S(2)}) collective-permute-start(f32[8,128]{1,0:T(8,128)S(1)} %get-tuple-element.43), channel_id=1, source_target_pairs={{0,3},{1,0},{2,1},{3,2},{4,7},{5,4},{6,5},{7,6},{8,11},{9,8},{10,9... | collective-permute-start | bytes 12296 | tf_op jit(solution)/shard_map/ppermute | solution.py:455
  109.6 0.9 copy-start.1
  110.5 0.7 copy-start.20
  111.3 0.7 copy-start.22
  112.0 27.1 %copy-start.2 = (f32[320,128]{1,0:T(8,128)S(1)}, f32[320,128]{1,0:T(8,128)}, u32[]{:S(2)}) copy-start(f32[320,128]{1,0:T(8,128)} %copy-done) | copy-start | bytes 491524
  112.2 0.7 copy-start.6
  112.9 0.9 copy-start.7
  (1 other events, 0.6 us)

commit v5 on v4

--- a/solution.py
+++ b/solution.py
@@ -21,10 +21,9 @@
 FULL_GROUPS = 24
 VEC_GROUPS = 4
 PACKED = 2 * MATRIX + 3 * SIZE * 8
-CELLS = PACKED + SEGMENTS * FULL_GROUPS
-KEEP = CELLS + FIELD
-PIVOT = KEEP + STEPS * 8
-LINES = PIVOT + MATRIX
+PIVOT = PACKED
+CELLS = PIVOT + MATRIX
+LINES = CELLS + FIELD
 
 
 def spectral():
@@ -145,43 +144,50 @@
                     out_ref[pl.ds(begin, STEPS, stride=SIZE * 8), :] = tile
 
 
-def fetch(source, target, sems, first):
-    copies = [pltpu.make_async_copy(source.at[i], target.at[i], sems.at[first + i]) for i in range(VARS)]
-    for copy in copies:
-        copy.start()
-    return copies
-
-
-def arrive(copies):
-    for copy in copies:
-        copy.wait()
-
-
-def pack_kernel(state_hbm, sent_ref, u_ref, edges_ref, state_ref, sems):
+def pack_kernel(state_ref, u_ref, edges_ref):
     sub, lane = iotas()
-    arrive(fetch(state_hbm, state_ref, sems, 0))
     field_to_packed(state_ref, u_ref)
-    sent_ref[...] = u_ref[...]
     edge_lines(sub, lane, rows(u_ref, 0, STEPS * VARS), edges_ref)
 
 
+def time_term(weights, u_ref, out_ref):
+    for v in range(VARS):
+        fields = [row(u_ref, j * VARS + v) for j in range(INST)]
+        for i in range(INST):
+            put(out_ref, i * VARS + v, total(fields[j] * F32(weights[i, j]) for j in range(INST)))
+
+
+def time_kernel(weights, spread_ref, edges_ref, out_ref, last_ref, first_ref):
+    time_term(weights, spread_ref, out_ref)
+    last_ref[...] = row(edges_ref, 0)
+    first_ref[...] = row(edges_ref, 1)
+
+
 def maps_kernel(
-    u_ref, coupling_hbm, back_hbm, pivot_hbm, source_hbm, flags_hbm,
-    lines_ref, halos_ref,
-    prefix_ref, coupling_raw, back_raw, pivot_raw, source_raw, flags_ref, sems,
+    weights,
+    spread_ref, edges_ref, u_ref, coupling_raw, back_raw, pivot_raw, source_raw, flags_ref,
+    out_ref, last_ref, first_ref, up_ref, down_ref, lines_ref, packed_ref,
+    prefix_ref, keep_ref,
 ):
     sub, lane = iotas()
     block = lane // 32
-    flags_copy = pltpu.make_async_copy(flags_hbm, flags_ref, sems.at[4 * VARS])
-    coupling_copies = fetch(coupling_hbm, coupling_raw, sems, 0)
-    back_copies = fetch(back_hbm, back_raw, sems, VARS)
-    pivot_copies = fetch(pivot_hbm, pivot_raw, sems, 2 * VARS)
-    source_copies = fetch(source_hbm, source_raw, sems, 3 * VARS)
-    flags_copy.start()
-    arrive(coupling_copies)
+    time_kernel(weights, spread_ref, edges_ref, out_ref, last_ref, first_ref)
     matrix_to_packed(coupling_raw, lines_ref, 0)
-    arrive(back_copies)
     matrix_to_packed(back_raw, lines_ref, MATRIX)
+    matrix_to_packed(pivot_raw, lines_ref, PIVOT)
+    field_to_packed(source_raw, lines_ref, CELLS)
+    for half in range(2):
+        for t in range(TILES):
+            flags = flags_ref[half * STEPS : (half + 1) * STEPS, t * 128 : (t + 1) * 128]
+            keep_ref[pl.ds(half * TILES + t, STEPS, stride=8), :] = (1 - flags).astype(F32)
+
+    def mask(k, carry):
+        keep = row(keep_ref, k)
+        for n in range(SIZE):
+            put(lines_ref, PIVOT // 8 + k * SIZE + n, keep * row(lines_ref, PIVOT // 8 + k * SIZE + n))
+        return carry
+
+    lax.fori_loop(0, STEPS, mask, 0)
 
     def coupling(k):
         return rows(lines_ref, k * SIZE, SIZE)
@@ -224,38 +230,13 @@
     whole = matmul(behind, swap(behind))
     for n in range(SIZE):
         put(prefix_ref, 2 * SIZE + n, whole[n])
-    pack_lines(lines_ref, PACKED, block, rows(prefix_ref, 0, 3 * SIZE), VEC_GROUPS, FULL_GROUPS)
-    halos_ref[: VARS * 8, :] = u_ref[(STEPS - 1) * VARS * 8 :, :]
-    halos_ref[VARS * 8 : (VARS + SIZE) * 8, :] = lines_ref[2 * MATRIX - SIZE * 8 : 2 * MATRIX, :]
-    halos_ref[(VARS + SIZE) * 8 :, :] = u_ref[: VARS * 8, :]
-    arrive(pivot_copies)
-    matrix_to_packed(pivot_raw, lines_ref, PIVOT)
-    arrive(source_copies)
-    field_to_packed(source_raw, lines_ref, CELLS)
-    flags_copy.wait()
-    for half in range(2):
-        for t in range(TILES):
-            flags = flags_ref[half * STEPS : (half + 1) * STEPS, t * 128 : (t + 1) * 128]
-            lines_ref[pl.ds(KEEP + half * TILES + t, STEPS, stride=8), :] = (1 - flags).astype(F32)
-
-
-def time_kernel(weights, count, u_ref, *rest):
-    out_ref = rest[count]
-    for v in range(VARS):
-        fields = [row(u_ref, j * VARS + v) for j in range(INST)]
-        for i in range(INST):
-            put(out_ref, i * VARS + v, total(fields[j] * F32(weights[i, j]) for j in range(INST)))
-    outs = list(rest[count + 1 :])
-    for ref in rest[:count]:
-        begin = 0
-        while begin < ref.shape[0]:
-            out = outs.pop(0)
-            out[...] = ref[begin : begin + out.shape[0], :]
-            begin += out.shape[0]
-
-
-def stencil_kernel(u_ref, lines_ref, below_ref, above_ref, left_ref, right_ref, out_ref):
-    sub, lane = iotas()
+    pack_lines(packed_ref, 0, block, rows(prefix_ref, 0, 3 * SIZE), VEC_GROUPS, FULL_GROUPS)
+    up_ref[: VARS * 8, :] = u_ref[(STEPS - 1) * VARS * 8 :, :]
+    up_ref[VARS * 8 :, :] = lines_ref[2 * MATRIX - SIZE * 8 : 2 * MATRIX, :]
+    down_ref[...] = u_ref[: VARS * 8, :]
+
+
+def stencil(sub, lane, u_ref, lines_ref, below_ref, above_ref, left_ref, right_ref, time_ref, out_ref):
     top = sub < TILES
     left_all = left_ref[...]
     right_all = right_ref[...]
@@ -278,19 +259,23 @@
             edge = jnp.where(sub % TILES == TILES - 1, lane_roll(right_all, 127 - n), pltpu.roll(turned, 7, 0))
             right = jnp.where(lane == 127, edge, turned)
             value = row(lines_ref, CELLS // 8 + n) - 0.1 * above + 0.5 * below - 0.8 * u + 0.2 * (left + right)
-            put(out_ref, n, value)
-
-
-def local_kernel(base_ref, time_ref, lines_ref, source_ref, packed_ref):
+            put(out_ref, n, value + row(time_ref, n))
+
+
+def local_kernel(
+    time_ref, u_ref, lines_ref, below_ref, above_ref, left_ref, right_ref, *rest
+):
+    source_ref, packed_ref, rhs_ref = rest[-3:]
     sub, lane = iotas()
     block = lane // 32
-    groups = packed_ref.shape[0] // SEGMENTS
-    if groups == FULL_GROUPS:
-        packed_ref[...] = lines_ref[PACKED:CELLS, :]
+    groups = VEC_GROUPS
+    if len(rest) > 3:
+        groups = FULL_GROUPS
+        packed_ref[...] = rest[0][...]
+    stencil(sub, lane, u_ref, lines_ref, below_ref, above_ref, left_ref, right_ref, time_ref, rhs_ref)
 
     def source_step(k, carry):
-        keep = row(lines_ref, KEEP // 8 + k)
-        rhs = [keep * (row(base_ref, k * VARS + v) + row(time_ref, k * VARS + v)) for v in range(VARS)]
+        rhs = rows(rhs_ref, k * VARS, VARS)
         for v, value in enumerate(matvec(rows(lines_ref, PIVOT // 8 + k * SIZE, SIZE), rhs)):
             put(source_ref, k * VARS + v, value)
         return carry
@@ -428,16 +413,13 @@
             put(new_above_ref, v, row(above_ref, v) + after[v])
 
 
-def call(kernel, shapes, *args, scratch=(), flops=100_000, limit=8, far=0):
+def call(kernel, shapes, *args, scratch=(), flops=100_000, limit=8):
     outs = [jax.ShapeDtypeStruct(shape, F32) for shape in shapes]
     moved = 4 * (sum(math.prod(shape) for shape in shapes) + sum(a.size for a in args))
-    near = len(args) - far
-    specs = [pl.BlockSpec(memory_space=pltpu.VMEM if n < near else pltpu.HBM) for n in range(len(args))]
     return pl.pallas_call(
         kernel,
         out_shape=outs,
-        in_specs=specs,
-        scratch_shapes=[pltpu.VMEM(item, F32) if isinstance(item, tuple) else item for item in scratch],
+        scratch_shapes=[pltpu.VMEM(shape, F32) for shape in scratch],
         cost_estimate=pl.CostEstimate(flops=flops, bytes_accessed=moved, transcendentals=0),
         compiler_params=pltpu.CompilerParams(vmem_limit_bytes=limit * 1024 * 1024),
     )(*args)
@@ -459,51 +441,42 @@
     weights = np.float32(-0.5 * spectral())
     edge = (8, 128)
     halo = (VARS * 8, 128)
-    up_shape = ((VARS + SIZE) * 8, 128)
     raw_field = (VARS, 2 * STEPS, TILES * 128)
-    raw_matrix = (VARS,) + raw_field
-    sent, u, edges = call(
-        pack_kernel, [(FIELD, 128), (FIELD, 128), (16, 128)], state[0].transpose(1, 0, 2),
-        scratch=[raw_field, pltpu.SemaphoreType.DMA((VARS,))], far=1,
-    )
-    lines, halos = call(
-        maps_kernel,
-        [(LINES, 128), (up_shape[0] + halo[0], 128)],
-        u, coupling[0].transpose(1, 2, 0, 3), back_coupling[0].transpose(1, 2, 0, 3),
-        pivot_inverse[0].transpose(1, 2, 0, 3), source_terms[0].transpose(1, 0, 2), wall_flags,
-        scratch=[
-            (MATRIX, 128), raw_matrix, raw_matrix, raw_matrix, raw_field,
-            pltpu.VMEM((2 * STEPS, TILES * 128), jnp.int32), pltpu.SemaphoreType.DMA((4 * VARS + 1,)),
-        ],
-        flops=8_000_000,
-        limit=16,
-        far=5,
-    )
+    u, edges = call(pack_kernel, [(FIELD, 128), (16, 128)], state[0].transpose(1, 0, 2))
     for sweep in range(SWEEPS):
         first = sweep == 0
         last = sweep == SWEEPS - 1
-        spread = exchange(sent, "inst", INST)
+        spread = exchange(u, "inst", INST)
         if first:
-            term, left, right, up, above = call(
-                lambda *refs: time_kernel(weights, 2, *refs),
-                [(FIELD, 128), edge, edge, up_shape, halo], spread, edges, halos,
+            term, left, right, up, above, lines, packed_maps = call(
+                lambda *refs: maps_kernel(weights, *refs),
+                [
+                    (FIELD, 128), edge, edge, ((VARS + SIZE) * 8, 128), halo, (LINES, 128),
+                    (SEGMENTS * FULL_GROUPS, 128),
+                ],
+                spread, edges, u,
+                coupling[0].transpose(1, 2, 0, 3), back_coupling[0].transpose(1, 2, 0, 3),
+                pivot_inverse[0].transpose(1, 2, 0, 3), source_terms[0].transpose(1, 0, 2), wall_flags,
+                scratch=[(MATRIX, 128), (STEPS * 8, 128)],
+                flops=8_000_000,
+                limit=12,
             )
             up = moved(up, "axial", 1, False)
             above = moved(above, "axial", -1, False)
             below = up[: VARS * 8]
         else:
             term, left, right = call(
-                lambda *refs: time_kernel(weights, 1, *refs), [(FIELD, 128), edge, edge], spread, edges
+                lambda *refs: time_kernel(weights, *refs), [(FIELD, 128), edge, edge], spread, edges
             )
         left = moved(left, "span", 1, True)
         right = moved(right, "span", -1, True)
         time = exchange(term, "inst", INST)
-        (base,) = call(stencil_kernel, [(FIELD, 128)], u, lines, below, above, left, right)
         groups = FULL_GROUPS if first else VEC_GROUPS
         source, packed = call(
             local_kernel,
             [(FIELD + 2 * VARS * 8, 128), (SEGMENTS * groups, 128)],
-            base, time, lines,
+            time, u, lines, below, above, left, right, *((packed_maps,) if first else ()),
+            scratch=[(FIELD, 128)],
         )
         recv = exchange(packed, "axial", SEGMENTS)
         if first:
@@ -524,7 +497,6 @@
                 lambda *refs: finish_kernel(False, *refs), [(FIELD, 128), (16, 128), halo, halo],
                 *common, up, above,
             )
-            sent = u
     return result.transpose(1, 0, 2)[None]
 
 

time: 141 us -> 133 us (0.943)
  blocking collectives: 69.1 us -> 87.8 us
  starting transfers between devices: 41 us -> 27.3 us
  local copies, waits for them, and re-layouts: 16.4 us -> 8.65 us
  Pallas kernels: 11.6 us -> 5.77 us
    all_to_all x5 -> x6, blocking collectives: 69.1 us -> 87.8 us  [exchange(): lax.all_to_all(value.reshape(count, shape[0] // count, 128), axis, 0, 0)]
    all_to_all x3 -> x2, starting transfers between devices: 21.5 us -> 6.76 us  [exchange(): lax.all_to_all(value.reshape(count, shape[0] // count, 128), axis, 0, 0)]
    unnamed x48 -> x22, local copies, waits for them, and re-layouts: 16.4 us -> 8.64 us
    pallas_call x12 -> x9, Pallas kernels: 11.6 us -> 5.77 us  [call(): pl.pallas_call(kernel, out_shape=outs, scratch_shapes=[pltpu.VMEM(shape,...]
  transfers between devices with their start and end apart: 9 -> 8, of which waited for: 2 -> 3; matrix products, arithmetic and copies ran while one was open for 0% -> 0% of each run, Pallas kernels for 4% -> 0%
where the time goes in v5:
time: 133 us; the launch traced here: 132 us
  blocking collectives  87.8 us (66%)
  starting transfers between devices  27.3 us (21%)
  local copies, waits for them, and re-layouts  8.65 us (7%)
  Pallas kernels  5.77 us (4%)
  waiting for transfers between devices  2.06 us (2%)
    all_to_all x6, blocking collectives, exchange(): lax.all_to_all(value.reshape(count, shape[0] // count, 128), axis, 0, 0)  87.8 us
    ppermute x6, starting transfers between devices, moved(): return lax.ppermute(value, axis, pairs)  20.6 us
    unnamed x22, local copies, waits for them, and re-layouts  8.64 us
    all_to_all x2, starting transfers between devices, exchange(): lax.all_to_all(value.reshape(count, shape[0] // count, 128), axis, 0, 0)  6.76 us
    pallas_call x9, Pallas kernels, call(): pl.pallas_call(kernel, out_shape=outs, scratch_shapes=[pltpu.VMEM(shape,...  5.77 us
  transfers between devices with their start and end apart: 8, of which 3 were waited for; matrix products, arithmetic and copies ran while one was open for 0% of the time, Pallas kernels for 0%

profile of v5, /device:TPU:1, one launch (start us, length us, event | category | flops | bytes accessed | tf_op | source)
XLA Modules:
  0.0 131.8 jit_solution(1310195162416749231)
XLA Ops:
  0.0 0.9 copy-done.6
  1.1 18.8 %all_to_all.40 = f32[8,40,128]{2,1,0:T(8,128)S(1)} all-to-all(f32[8,40,128]{2,1,0:T(8,128)S(1)} %bitcast.34), channel_id=1, replica_groups=mesh['inst'=8,'axial'=16,'span'=4] {'inst'}, dimensions={0} | all-to-all | bytes 327680 | tf_op jit(solution)/shard_map/all_to_all | solution.py:430
  19.9 1.1 copy-done
  21.1 1.1 copy-done.1
  22.2 1.1 copy-done.2
  23.3 0.9 copy-done.5
  24.3 0.8 copy-done.9
  25.0 1.8 %shard_map.65 = (f32[320,128]{1,0:T(8,128)S(1)}, f32[8,128]{1,0:T(8,128)S(1)}, f32[8,128]{1,0:T(8,128)S(1)}, f32[240,128]{1,0:T(8,128)S(1)}, f32[40,128]{1,0:T(8...) custom-call(f32[320,128]{1,0:T(8,128)S(1)} %bitcast.42, f32[16,128]{1,0:T(8,128)S(1)} %get-tuple-element.26.refs_1_, ...), custom_call_target="tpu_custom_call" | custom-call | flops 8000000 | bytes 6430720 | tf_op jit(solution)/shard_map/pallas_call | solution.py:419
  26.8 0.7 copy-done.7
  27.5 0.7 copy-done.10
  28.1 3.4 %all-to-all-start.1 = ((f32[8,40,128]{2,1,0:T(8,128)}), f32[8,40,128]{2,1,0:T(8,128)S(1)}, u32[]{:S(2)}, u32[]{:S(2)}) async-start(f32[8,40,128]{2,1,0:T(8,128)} %bitcast.48), calls=%async_computation.1 | async-start | bytes 327680 | tf_op jit(solution)/shard_map/all_to_all | solution.py:430
  31.5 5.7 %collective-permute-start = (f32[240,128]{1,0:T(8,128)}, f32[240,128]{1,0:T(8,128)S(1)}, u32[]{:S(2)}, u32[]{:S(2)}) collective-permute-start(f32[240,128]{1,0:T(8,128)} %copy-done.10), channel_id=1, source_target_pairs={{0,4},{4,8},{8,12},{12,16},{16,20},{20,24},{24,28},{28,32},{32,36}... | collective-permute-start | bytes 368648 | tf_op jit(solution)/shard_map/ppermute | solution.py:437
  37.2 1.9 %collective-permute-start.1 = (f32[40,128]{1,0:T(8,128)S(1)}, f32[40,128]{1,0:T(8,128)S(1)}, u32[]{:S(2)}, u32[]{:S(2)}) collective-permute-start(f32[40,128]{1,0:T(8,128)S(1)} %get-tuple-element.30), channel_id=1, source_target_pairs={{4,0},{8,4},{12,8},{16,12},{20,16},{24,20},{28,24},{32,28},{36,32}... | collective-permute-start | bytes 61448 | tf_op jit(solution)/shard_map/ppermute | solution.py:437
  39.1 3.1 %collective-permute-start.2 = (f32[8,128]{1,0:T(8,128)S(1)}, f32[8,128]{1,0:T(8,128)S(1)}, u32[]{:S(2)}, u32[]{:S(2)}) collective-permute-start(f32[8,128]{1,0:T(8,128)S(1)} %get-tuple-element.31), channel_id=1, source_target_pairs={{0,1},{1,2},{2,3},{3,0},{4,5},{5,6},{6,7},{7,4},{8,9},{9,10},{10,1... | collective-permute-start | bytes 12296 | tf_op jit(solution)/shard_map/ppermute | solution.py:437
  42.2 3.4 %collective-permute-start.3 = (f32[8,128]{1,0:T(8,128)S(1)}, f32[8,128]{1,0:T(8,128)S(1)}, u32[]{:S(2)}, u32[]{:S(2)}) collective-permute-start(f32[8,128]{1,0:T(8,128)S(1)} %get-tuple-element.32), channel_id=1, source_target_pairs={{0,3},{1,0},{2,1},{3,2},{4,7},{5,4},{6,5},{7,6},{8,11},{9,8},{10,9... | collective-permute-start | bytes 12296 | tf_op jit(solution)/shard_map/ppermute | solution.py:437
  45.7 0.6 copy-done.3
  46.6 0.6 shard_map.66
  47.2 20.4 %all_to_all.41 = f32[16,24,128]{2,1,0:T(8,128)S(1)} all-to-all(f32[16,24,128]{2,1,0:T(8,128)S(1)} %bitcast.45), channel_id=1, replica_groups=mesh['inst'=8,'axial'=16,'span'=4] {'axial'}, dimensions={0} | all-to-all | bytes 393216 | tf_op jit(solution)/shard_map/all_to_all | solution.py:430
  67.6 0.7 shard_map.67
  68.3 10.1 %all_to_all.42 = f32[16,4,128]{2,1,0:T(4,128)S(1)} all-to-all(f32[16,4,128]{2,1,0:T(4,128)S(1)} %bitcast.52), channel_id=1, replica_groups=mesh['inst'=8,'axial'=16,'span'=4] {'axial'}, dimensions={0} | all-to-all | bytes 65536 | tf_op jit(solution)/shard_map/all_to_all | solution.py:430
  78.7 15.2 %all_to_all.43 = f32[8,40,128]{2,1,0:T(8,128)S(1)} all-to-all(f32[8,40,128]{2,1,0:T(8,128)S(1)} %bitcast.37), channel_id=1, replica_groups=mesh['inst'=8,'axial'=16,'span'=4] {'inst'}, dimensions={0} | all-to-all | bytes 327680 | tf_op jit(solution)/shard_map/all_to_all | solution.py:430
  94.0 0.7 copy-done.8
  94.7 3.4 %all-to-all-start.5 = ((f32[8,40,128]{2,1,0:T(8,128)}), f32[8,40,128]{2,1,0:T(8,128)S(1)}, u32[]{:S(2)}, u32[]{:S(2)}) async-start(f32[8,40,128]{2,1,0:T(8,128)} %bitcast.49), calls=%async_computation.5 | async-start | bytes 327680 | tf_op jit(solution)/shard_map/all_to_all | solution.py:430
  98.0 3.1 %collective-permute-start.4 = (f32[8,128]{1,0:T(8,128)S(1)}, f32[8,128]{1,0:T(8,128)S(1)}, u32[]{:S(2)}, u32[]{:S(2)}) collective-permute-start(f32[8,128]{1,0:T(8,128)S(1)} %get-tuple-element.41), channel_id=1, source_target_pairs={{0,1},{1,2},{2,3},{3,0},{4,5},{5,6},{6,7},{7,4},{8,9},{9,10},{10,1... | collective-permute-start | bytes 12296 | tf_op jit(solution)/shard_map/ppermute | solution.py:437
  101.2 3.4 %collective-permute-start.5 = (f32[8,128]{1,0:T(8,128)S(1)}, f32[8,128]{1,0:T(8,128)S(1)}, u32[]{:S(2)}, u32[]{:S(2)}) collective-permute-start(f32[8,128]{1,0:T(8,128)S(1)} %get-tuple-element.42), channel_id=1, source_target_pairs={{0,3},{1,0},{2,1},{3,2},{4,7},{5,4},{6,5},{7,6},{8,11},{9,8},{10,9... | collective-permute-start | bytes 12296 | tf_op jit(solution)/shard_map/ppermute | solution.py:437
  104.6 1.2 collective-permute-done.5.right_ref
  105.8 0.5 all-to-all-done.5
  106.3 0.6 shard_map.70
  106.9 13.1 %all_to_all.44 = f32[16,4,128]{2,1,0:T(4,128)S(1)} all-to-all(f32[16,4,128]{2,1,0:T(4,128)S(1)} %bitcast.55), channel_id=1, replica_groups=mesh['inst'=8,'axial'=16,'span'=4] {'axial'}, dimensions={0} | all-to-all | bytes 65536 | tf_op jit(solution)/shard_map/all_to_all | solution.py:430
  120.0 0.7 shard_map.71
  120.7 10.3 %all_to_all.45 = f32[16,4,128]{2,1,0:T(4,128)S(1)} all-to-all(f32[16,4,128]{2,1,0:T(4,128)S(1)} %bitcast.54), channel_id=1, replica_groups=mesh['inst'=8,'axial'=16,'span'=4] {'axial'}, dimensions={0} | all-to-all | bytes 65536 | tf_op jit(solution)/shard_map/all_to_all | solution.py:430
  130.9 0.9 shard_map.72
  (22 shorter events, 0.9 us)
Async XLA Ops:
  0.0 0.9 copy-start.6
  19.9 1.1 copy-start
  21.1 1.1 copy-start.1
  22.2 1.1 copy-start.2
  23.3 0.9 copy-start.5
  24.3 0.8 copy-start.9
  26.8 0.7 copy-start.7
  27.5 0.7 copy-start.10
  28.1 18.5 %all-to-all-start.1 = ((f32[8,40,128]{2,1,0:T(8,128)}), f32[8,40,128]{2,1,0:T(8,128)S(1)}, u32[]{:S(2)}, u32[]{:S(2)}) async-start(f32[8,40,128]{2,1,0:T(8,128)} %bitcast.48), calls=%async_computation.1 | async-start | bytes 327680 | tf_op jit(solution)/shard_map/all_to_all | solution.py:430
  31.5 14.1 %collective-permute-start = (f32[240,128]{1,0:T(8,128)}, f32[240,128]{1,0:T(8,128)S(1)}, u32[]{:S(2)}, u32[]{:S(2)}) collective-permute-start(f32[240,128]{1,0:T(8,128)} %copy-done.10), channel_id=1, source_target_pairs={{0,4},{4,8},{8,12},{12,16},{16,20},{20,24},{24,28},{28,32},{32,36}... | collective-permute-start | bytes 368648 | tf_op jit(solution)/shard_map/ppermute | solution.py:437
  37.2 9.4 %collective-permute-start.1 = (f32[40,128]{1,0:T(8,128)S(1)}, f32[40,128]{1,0:T(8,128)S(1)}, u32[]{:S(2)}, u32[]{:S(2)}) collective-permute-start(f32[40,128]{1,0:T(8,128)S(1)} %get-tuple-element.30), channel_id=1, source_target_pairs={{4,0},{8,4},{12,8},{16,12},{20,16},{24,20},{28,24},{32,28},{36,32}... | collective-permute-start | bytes 61448 | tf_op jit(solution)/shard_map/ppermute | solution.py:437
  39.1 7.2 %collective-permute-start.2 = (f32[8,128]{1,0:T(8,128)S(1)}, f32[8,128]{1,0:T(8,128)S(1)}, u32[]{:S(2)}, u32[]{:S(2)}) collective-permute-start(f32[8,128]{1,0:T(8,128)S(1)} %get-tuple-element.31), channel_id=1, source_target_pairs={{0,1},{1,2},{2,3},{3,0},{4,5},{5,6},{6,7},{7,4},{8,9},{9,10},{10,1... | collective-permute-start | bytes 12296 | tf_op jit(solution)/shard_map/ppermute | solution.py:437
  42.2 4.4 %collective-permute-start.3 = (f32[8,128]{1,0:T(8,128)S(1)}, f32[8,128]{1,0:T(8,128)S(1)}, u32[]{:S(2)}, u32[]{:S(2)}) collective-permute-start(f32[8,128]{1,0:T(8,128)S(1)} %get-tuple-element.32), channel_id=1, source_target_pairs={{0,3},{1,0},{2,1},{3,2},{4,7},{5,4},{6,5},{7,6},{8,11},{9,8},{10,9... | collective-permute-start | bytes 12296 | tf_op jit(solution)/shard_map/ppermute | solution.py:437
  45.6 0.7 copy-start.3
  46.6 31.7 %copy-start.4 = (f32[240,128]{1,0:T(8,128)S(1)}, f32[240,128]{1,0:T(8,128)}, u32[]{:S(2)}) copy-start(f32[240,128]{1,0:T(8,128)} %copy-done.3) | copy-start | bytes 368644
  94.0 0.7 copy-start.8
  94.7 11.7 %all-to-all-start.5 = ((f32[8,40,128]{2,1,0:T(8,128)}), f32[8,40,128]{2,1,0:T(8,128)S(1)}, u32[]{:S(2)}, u32[]{:S(2)}) async-start(f32[8,40,128]{2,1,0:T(8,128)} %bitcast.49), calls=%async_computation.5 | async-start | bytes 327680 | tf_op jit(solution)/shard_map/all_to_all | solution.py:430
  98.0 6.5 %collective-permute-start.4 = (f32[8,128]{1,0:T(8,128)S(1)}, f32[8,128]{1,0:T(8,128)S(1)}, u32[]{:S(2)}, u32[]{:S(2)}) collective-permute-start(f32[8,128]{1,0:T(8,128)S(1)} %get-tuple-element.41), channel_id=1, source_target_pairs={{0,1},{1,2},{2,3},{3,0},{4,5},{5,6},{6,7},{7,4},{8,9},{9,10},{10,1... | collective-permute-start | bytes 12296 | tf_op jit(solution)/shard_map/ppermute | solution.py:437
  101.2 4.6 %collective-permute-start.5 = (f32[8,128]{1,0:T(8,128)S(1)}, f32[8,128]{1,0:T(8,128)S(1)}, u32[]{:S(2)}, u32[]{:S(2)}) collective-permute-start(f32[8,128]{1,0:T(8,128)S(1)} %get-tuple-element.42), channel_id=1, source_target_pairs={{0,3},{1,0},{2,1},{3,2},{4,7},{5,4},{6,5},{7,6},{8,11},{9,8},{10,9... | collective-permute-start | bytes 12296 | tf_op jit(solution)/shard_map/ppermute | solution.py:437

commit v6 on v4

--- a/solution.py
+++ b/solution.py
@@ -21,10 +21,12 @@
 FULL_GROUPS = 24
 VEC_GROUPS = 4
 PACKED = 2 * MATRIX + 3 * SIZE * 8
-CELLS = PACKED + SEGMENTS * FULL_GROUPS
-KEEP = CELLS + FIELD
-PIVOT = KEEP + STEPS * 8
-LINES = PIVOT + MATRIX
+PIVOT = PACKED
+CELLS = PIVOT + MATRIX
+LINES = CELLS + FIELD
+UP = VARS * 8 + (SIZE + 1) // 2 * 8
+BELOW = STEPS * VARS
+ABOVE = BELOW + VARS
 
 
 def spectral():
@@ -165,23 +167,56 @@
     edge_lines(sub, lane, rows(u_ref, 0, STEPS * VARS), edges_ref)
 
 
+def time_kernel(weights, spread_ref, edges_ref, *rest):
+    halos_ref = rest[0] if len(rest) > 3 else None
+    out_ref, last_ref, first_ref = rest[-5:-2] if len(rest) > 3 else rest
+    for v in range(VARS):
+        fields = [row(spread_ref, j * VARS + v) for j in range(INST)]
+        for i in range(INST):
+            put(out_ref, i * VARS + v, total(fields[j] * F32(weights[i, j]) for j in range(INST)))
+    last_ref[...] = row(edges_ref, 0)
+    first_ref[...] = row(edges_ref, 1)
+    if halos_ref is not None:
+        up_ref, down_ref = rest[-2:]
+        up_ref[...] = halos_ref[:UP, :]
+        down_ref[...] = halos_ref[UP:, :]
+
+
 def maps_kernel(
     u_ref, coupling_hbm, back_hbm, pivot_hbm, source_hbm, flags_hbm,
-    lines_ref, halos_ref,
-    prefix_ref, coupling_raw, back_raw, pivot_raw, source_raw, flags_ref, sems,
+    halos_ref, lines_ref, packed_ref,
+    prefix_ref, keep_ref, coupling_raw, back_raw, pivot_raw, source_raw, flags_ref, sems,
 ):
     sub, lane = iotas()
     block = lane // 32
-    flags_copy = pltpu.make_async_copy(flags_hbm, flags_ref, sems.at[4 * VARS])
     coupling_copies = fetch(coupling_hbm, coupling_raw, sems, 0)
     back_copies = fetch(back_hbm, back_raw, sems, VARS)
     pivot_copies = fetch(pivot_hbm, pivot_raw, sems, 2 * VARS)
     source_copies = fetch(source_hbm, source_raw, sems, 3 * VARS)
+    flags_copy = pltpu.make_async_copy(flags_hbm, flags_ref, sems.at[4 * VARS])
     flags_copy.start()
+    top = sub < TILES
     arrive(coupling_copies)
     matrix_to_packed(coupling_raw, lines_ref, 0)
     arrive(back_copies)
     matrix_to_packed(back_raw, lines_ref, MATRIX)
+    arrive(pivot_copies)
+    matrix_to_packed(pivot_raw, lines_ref, PIVOT)
+    arrive(source_copies)
+    field_to_packed(source_raw, lines_ref, CELLS)
+    flags_copy.wait()
+    for half in range(2):
+        for t in range(TILES):
+            flags = flags_ref[half * STEPS : (half + 1) * STEPS, t * 128 : (t + 1) * 128]
+            keep_ref[pl.ds(half * TILES + t, STEPS, stride=8), :] = (1 - flags).astype(F32)
+
+    def mask(k, carry):
+        keep = row(keep_ref, k)
+        for n in range(SIZE):
+            put(lines_ref, PIVOT // 8 + k * SIZE + n, keep * row(lines_ref, PIVOT // 8 + k * SIZE + n))
+        return carry
+
+    lax.fori_loop(0, STEPS, mask, 0)
 
     def coupling(k):
         return rows(lines_ref, k * SIZE, SIZE)
@@ -224,38 +259,18 @@
     whole = matmul(behind, swap(behind))
     for n in range(SIZE):
         put(prefix_ref, 2 * SIZE + n, whole[n])
-    pack_lines(lines_ref, PACKED, block, rows(prefix_ref, 0, 3 * SIZE), VEC_GROUPS, FULL_GROUPS)
+    pack_lines(packed_ref, 0, block, rows(prefix_ref, 0, 3 * SIZE), VEC_GROUPS, FULL_GROUPS)
     halos_ref[: VARS * 8, :] = u_ref[(STEPS - 1) * VARS * 8 :, :]
-    halos_ref[VARS * 8 : (VARS + SIZE) * 8, :] = lines_ref[2 * MATRIX - SIZE * 8 : 2 * MATRIX, :]
-    halos_ref[(VARS + SIZE) * 8 :, :] = u_ref[: VARS * 8, :]
-    arrive(pivot_copies)
-    matrix_to_packed(pivot_raw, lines_ref, PIVOT)
-    arrive(source_copies)
-    field_to_packed(source_raw, lines_ref, CELLS)
-    flags_copy.wait()
-    for half in range(2):
-        for t in range(TILES):
-            flags = flags_ref[half * STEPS : (half + 1) * STEPS, t * 128 : (t + 1) * 128]
-            lines_ref[pl.ds(KEEP + half * TILES + t, STEPS, stride=8), :] = (1 - flags).astype(F32)
-
-
-def time_kernel(weights, count, u_ref, *rest):
-    out_ref = rest[count]
-    for v in range(VARS):
-        fields = [row(u_ref, j * VARS + v) for j in range(INST)]
-        for i in range(INST):
-            put(out_ref, i * VARS + v, total(fields[j] * F32(weights[i, j]) for j in range(INST)))
-    outs = list(rest[count + 1 :])
-    for ref in rest[:count]:
-        begin = 0
-        while begin < ref.shape[0]:
-            out = outs.pop(0)
-            out[...] = ref[begin : begin + out.shape[0], :]
-            begin += out.shape[0]
-
-
-def stencil_kernel(u_ref, lines_ref, below_ref, above_ref, left_ref, right_ref, out_ref):
-    sub, lane = iotas()
+    last = back(STEPS - 1)
+    for n in range(0, SIZE, 2):
+        pair = jnp.where(top, pltpu.roll(last[n], 4, 0), last[min(n + 1, SIZE - 1)])
+        put(halos_ref, VARS + n // 2, pair)
+    halos_ref[UP:, :] = u_ref[: VARS * 8, :]
+
+
+def stencil(
+    sub, lane, u_ref, lines_ref, below_ref, below_at, above_ref, above_at, left_ref, right_ref, time_ref, out_ref
+):
     top = sub < TILES
     left_all = left_ref[...]
     right_all = right_ref[...]
@@ -264,11 +279,11 @@
             n = k * VARS + v
             u = row(u_ref, n)
             if k == 0:
-                below = pltpu.roll(jnp.where(top, row(u_ref, (STEPS - 1) * VARS + v), row(below_ref, v)), 4, 0)
+                below = pltpu.roll(jnp.where(top, row(u_ref, (STEPS - 1) * VARS + v), row(below_ref, below_at + v)), 4, 0)
             else:
                 below = row(u_ref, n - VARS)
             if k == STEPS - 1:
-                above = pltpu.roll(jnp.where(top, row(above_ref, v), row(u_ref, v)), 4, 0)
+                above = pltpu.roll(jnp.where(top, row(above_ref, above_at + v), row(u_ref, v)), 4, 0)
             else:
                 above = row(u_ref, n + VARS)
             turned = pltpu.roll(u, 1, 1)
@@ -278,19 +293,27 @@
             edge = jnp.where(sub % TILES == TILES - 1, lane_roll(right_all, 127 - n), pltpu.roll(turned, 7, 0))
             right = jnp.where(lane == 127, edge, turned)
             value = row(lines_ref, CELLS // 8 + n) - 0.1 * above + 0.5 * below - 0.8 * u + 0.2 * (left + right)
-            put(out_ref, n, value)
-
-
-def local_kernel(base_ref, time_ref, lines_ref, source_ref, packed_ref):
+            put(out_ref, n, value + row(time_ref, n))
+
+
+def local_kernel(time_ref, u_ref, lines_ref, left_ref, right_ref, *rest):
     sub, lane = iotas()
     block = lane // 32
-    groups = packed_ref.shape[0] // SEGMENTS
-    if groups == FULL_GROUPS:
-        packed_ref[...] = lines_ref[PACKED:CELLS, :]
+    if len(rest) > 3:
+        below_ref, above_ref, maps_hbm, source_ref, packed_ref, rhs_ref, sem = rest
+        below_at, above_at, groups = 0, 0, FULL_GROUPS
+        maps_copy = pltpu.make_async_copy(maps_hbm, packed_ref, sem)
+        maps_copy.start()
+    else:
+        source_ref, packed_ref, rhs_ref = rest
+        below_ref = above_ref = u_ref
+        below_at, above_at, groups = BELOW, ABOVE, VEC_GROUPS
+    stencil(
+        sub, lane, u_ref, lines_ref, below_ref, below_at, above_ref, above_at, left_ref, right_ref, time_ref, rhs_ref
+    )
 
     def source_step(k, carry):
-        keep = row(lines_ref, KEEP // 8 + k)
-        rhs = [keep * (row(base_ref, k * VARS + v) + row(time_ref, k * VARS + v)) for v in range(VARS)]
+        rhs = rows(rhs_ref, k * VARS, VARS)
         for v, value in enumerate(matvec(rows(lines_ref, PIVOT // 8 + k * SIZE, SIZE), rhs)):
             put(source_ref, k * VARS + v, value)
         return carry
@@ -316,6 +339,8 @@
     inner = plus(swap(x), matvec(swap(mixed), end))
     whole_first = plus(x, matvec(behind, inner))
     values = whole_end + whole_first + [jnp.zeros((8, 128), F32)] * (4 * VEC_GROUPS - 2 * VARS)
+    if groups == FULL_GROUPS:
+        maps_copy.wait()
     pack_lines(packed_ref, 0, block, values, 0, groups)
 
 
@@ -376,7 +401,7 @@
     if last:
         out_ref, new_ref = rest
     else:
-        up_ref, above_ref, new_ref, edges_ref, new_below_ref, new_above_ref = rest
+        up_ref, above_ref, sent_ref, edges_ref, new_ref = rest
     sub, lane = iotas()
     block = lane // 32
     top = sub < TILES
@@ -422,21 +447,26 @@
                     out_ref[v, half * STEPS : (half + 1) * STEPS, t * 128 : (t + 1) * 128] = tile
     else:
         edge_lines(sub, lane, rows(new_ref, 0, STEPS * VARS), edges_ref)
-        before = minus(entry, matvec(rows(up_ref, VARS, SIZE), swap(x)))
+        pairs = rows(up_ref, VARS, (SIZE + 1) // 2)
+        blocks = [pairs[n // 2] if n % 2 else pltpu.roll(pairs[n // 2], 4, 0) for n in range(SIZE)]
+        before = minus(entry, matvec(blocks, swap(x)))
         for v in range(VARS):
-            put(new_below_ref, v, row(up_ref, v) + before[v])
-            put(new_above_ref, v, row(above_ref, v) + after[v])
-
-
-def call(kernel, shapes, *args, scratch=(), flops=100_000, limit=8, far=0):
-    outs = [jax.ShapeDtypeStruct(shape, F32) for shape in shapes]
+            put(new_ref, BELOW + v, row(up_ref, v) + before[v])
+            put(new_ref, ABOVE + v, row(above_ref, v) + after[v])
+        sent_ref[...] = new_ref[:FIELD, :]
+
+
+def call(kernel, shapes, *args, scratch=(), flops=100_000, limit=8, far=0, sent=()):
+    outs = [pltpu.HBM(shape, F32) if n in sent else jax.ShapeDtypeStruct(shape, F32) for n, shape in enumerate(shapes)]
     moved = 4 * (sum(math.prod(shape) for shape in shapes) + sum(a.size for a in args))
     near = len(args) - far
     specs = [pl.BlockSpec(memory_space=pltpu.VMEM if n < near else pltpu.HBM) for n in range(len(args))]
+    args = args[:near] + tuple(pltpu.with_memory_space_constraint(a, pltpu.HBM) for a in args[near:])
     return pl.pallas_call(
         kernel,
         out_shape=outs,
         in_specs=specs,
+        out_specs=[pl.BlockSpec(memory_space=pltpu.VMEM)] * len(outs),
         scratch_shapes=[pltpu.VMEM(item, F32) if isinstance(item, tuple) else item for item in scratch],
         cost_estimate=pl.CostEstimate(flops=flops, bytes_accessed=moved, transcendentals=0),
         compiler_params=pltpu.CompilerParams(vmem_limit_bytes=limit * 1024 * 1024),
@@ -459,51 +489,47 @@
     weights = np.float32(-0.5 * spectral())
     edge = (8, 128)
     halo = (VARS * 8, 128)
-    up_shape = ((VARS + SIZE) * 8, 128)
     raw_field = (VARS, 2 * STEPS, TILES * 128)
     raw_matrix = (VARS,) + raw_field
     sent, u, edges = call(
         pack_kernel, [(FIELD, 128), (FIELD, 128), (16, 128)], state[0].transpose(1, 0, 2),
         scratch=[raw_field, pltpu.SemaphoreType.DMA((VARS,))], far=1,
     )
-    lines, halos = call(
+    halos, lines, packed_maps = call(
         maps_kernel,
-        [(LINES, 128), (up_shape[0] + halo[0], 128)],
+        [(UP + halo[0], 128), (LINES, 128), (SEGMENTS * FULL_GROUPS, 128)],
         u, coupling[0].transpose(1, 2, 0, 3), back_coupling[0].transpose(1, 2, 0, 3),
         pivot_inverse[0].transpose(1, 2, 0, 3), source_terms[0].transpose(1, 0, 2), wall_flags,
         scratch=[
-            (MATRIX, 128), raw_matrix, raw_matrix, raw_matrix, raw_field,
+            (MATRIX, 128), (STEPS * 8, 128), raw_matrix, raw_matrix, raw_matrix, raw_field,
             pltpu.VMEM((2 * STEPS, TILES * 128), jnp.int32), pltpu.SemaphoreType.DMA((4 * VARS + 1,)),
         ],
         flops=8_000_000,
         limit=16,
         far=5,
+        sent=(2,),
     )
     for sweep in range(SWEEPS):
         first = sweep == 0
         last = sweep == SWEEPS - 1
         spread = exchange(sent, "inst", INST)
+        term, left, right, *ends = call(
+            lambda *refs: time_kernel(weights, *refs),
+            [(FIELD, 128), edge, edge] + ([(UP, 128), halo] if first else []),
+            spread, edges, *((halos,) if first else ()), sent=(0,),
+        )
         if first:
-            term, left, right, up, above = call(
-                lambda *refs: time_kernel(weights, 2, *refs),
-                [(FIELD, 128), edge, edge, up_shape, halo], spread, edges, halos,
-            )
-            up = moved(up, "axial", 1, False)
-            above = moved(above, "axial", -1, False)
-            below = up[: VARS * 8]
-        else:
-            term, left, right = call(
-                lambda *refs: time_kernel(weights, 1, *refs), [(FIELD, 128), edge, edge], spread, edges
-            )
+            up = moved(ends[0], "axial", 1, False)
+            above = moved(ends[1], "axial", -1, False)
         left = moved(left, "span", 1, True)
         right = moved(right, "span", -1, True)
         time = exchange(term, "inst", INST)
-        (base,) = call(stencil_kernel, [(FIELD, 128)], u, lines, below, above, left, right)
         groups = FULL_GROUPS if first else VEC_GROUPS
         source, packed = call(
             local_kernel,
             [(FIELD + 2 * VARS * 8, 128), (SEGMENTS * groups, 128)],
-            base, time, lines,
+            time, u, lines, left, right, *((up, above, packed_maps) if first else ()),
+            scratch=[(FIELD, 128)] + ([pltpu.SemaphoreType.DMA] if first else []), far=1 if first else 0,
         )
         recv = exchange(packed, "axial", SEGMENTS)
         if first:
@@ -520,11 +546,10 @@
                 lambda *refs: finish_kernel(True, *refs), [raw_field], *common, scratch=[(FIELD, 128)],
             )
         else:
-            u, edges, below, above = call(
-                lambda *refs: finish_kernel(False, *refs), [(FIELD, 128), (16, 128), halo, halo],
+            sent, edges, u = call(
+                lambda *refs: finish_kernel(False, *refs), [(FIELD, 128), (16, 128), (FIELD + 2 * halo[0], 128)],
                 *common, up, above,
             )
-            sent = u
     return result.transpose(1, 0, 2)[None]
 
 

time: 141 us -> 127 us (0.901)
  local copies, waits for them, and re-layouts: 16.4 us -> 0.89 us
  waiting for transfers between devices: 1.66 us -> 6.81 us
  starting transfers between devices: 41 us -> 38.2 us
    unnamed x48 -> x4, local copies, waits for them, and re-layouts: 16.4 us -> 0.89 us
    all_to_all x3, waiting for transfers between devices: 0.01 us -> 4.6 us  [exchange(): lax.all_to_all(value.reshape(count, shape[0] // count, 128), axis, 0, 0)]
    all_to_all x3, starting transfers between devices: 21.5 us -> 17.6 us  [exchange(): lax.all_to_all(value.reshape(count, shape[0] // count, 128), axis, 0, 0)]
    pallas_call x12 -> x10, Pallas kernels: 11.6 us -> 11.3 us  [call(): pl.pallas_call(kernel, out_shape=outs, in_specs=specs, out_specs=[pl.Bloc...]
  transfers between devices with their start and end apart: 9 -> 9, of which waited for: 2 -> 4; matrix products, arithmetic and copies ran while one was open for 0% -> 0% of each run, Pallas kernels for 4% -> 3%
where the time goes in v6:
time: 127 us; the launch traced here: 126 us
  blocking collectives  69 us (54%)
  starting transfers between devices  38.2 us (30%)
  Pallas kernels  11.3 us (9%)
  waiting for transfers between devices  6.81 us (5%)
    all_to_all x5, blocking collectives, exchange(): lax.all_to_all(value.reshape(count, shape[0] // count, 128), axis, 0, 0)  69 us
    ppermute x6, starting transfers between devices, moved(): return lax.ppermute(value, axis, pairs)  20.6 us
    all_to_all x3, starting transfers between devices, exchange(): lax.all_to_all(value.reshape(count, shape[0] // count, 128), axis, 0, 0)  17.6 us
    pallas_call x10, Pallas kernels, call(): pl.pallas_call(kernel, out_shape=outs, in_specs=specs, out_specs=[pl.Bloc...  11.3 us
    all_to_all x3, waiting for transfers between devices, exchange(): lax.all_to_all(value.reshape(count, shape[0] // count, 128), axis, 0, 0)  4.6 us
  transfers between devices with their start and end apart: 9, of which 4 were waited for; matrix products, arithmetic and copies ran while one was open for 0% of the time, Pallas kernels for 3%

profile of v6, /device:TPU:1, one launch (start us, length us, event | category | flops | bytes accessed | tf_op | source)
XLA Modules:
  0.0 126.5 jit_solution(13129015130058138904)
XLA Ops:
  0.0 1.6 %shard_map.64 = (f32[320,128]{1,0:T(8,128)}, f32[320,128]{1,0:T(8,128)S(1)}, f32[16,128]{1,0:T(8,128)S(1)}) custom-call(f32[5,16,512]{2,1,0:T(8,128)} %bitcast.52), custom_call_target="tpu_custom_call" | custom-call | flops 100000 | bytes 499712 | tf_op jit(solution)/shard_map/pallas_call | solution.py:465
  1.6 10.9 %all-to-all-start = ((f32[8,40,128]{2,1,0:T(8,128)}), f32[8,40,128]{2,1,0:T(8,128)S(1)}, u32[]{:S(2)}, u32[]{:S(2)}) async-start(f32[8,40,128]{2,1,0:T(8,128)} %bitcast.2), calls=%async_computation | async-start | bytes 327680 | tf_op jit(solution)/shard_map/all_to_all | solution.py:478
  12.5 4.1 %shard_map.65 = (f32[184,128]{1,0:T(8,128)S(1)}, f32[5720,128]{1,0:T(8,128)S(1)}, f32[384,128]{1,0:T(8,128)}) custom-call(f32[320,128]{1,0:T(8,128)S(1)} %get-tuple-element.28.u_ref.refs_1_, f32[5,5,16,512]{3,2,1,0:T(8,128)} %bitcast.48, f32[5,5,16,512]{3,2,1,0:T(8,128)} %bitcast.49, f32[5,5,16,512]{3,2,1,0:T(8,128)} %bitcast.50, f32[5,16,512]{2,1,0:T(8,128)} %bitcast.51, ...), custom_call_target="tpu_custom_call" | custom-call | flops 8000000 | bytes 6037504 | tf_op jit(solution)/shard_map/pallas_call | solution.py:465
  16.5 4.1 %all-to-all-done = f32[8,40,128]{2,1,0:T(8,128)S(1)} async-done(((f32[8,40,128]{2,1,0:T(8,128)}), f32[8,40,128]{2,1,0:T(8,128)S(1)}, u32[]{:S(2)}, u32[]{:S(2)}) %all-to-all-start) | async-done | bytes 163872 | tf_op jit(solution)/shard_map/all_to_all | solution.py:478
  20.6 0.7 shard_map.66
  21.4 3.4 %all-to-all-start.1 = ((f32[8,40,128]{2,1,0:T(8,128)}), f32[8,40,128]{2,1,0:T(8,128)S(1)}, u32[]{:S(2)}, u32[]{:S(2)}) async-start(f32[8,40,128]{2,1,0:T(8,128)} %bitcast.53), calls=%async_computation.1 | async-start | bytes 327680 | tf_op jit(solution)/shard_map/all_to_all | solution.py:478
  24.8 5.7 %collective-permute-start.2 = (f32[144,128]{1,0:T(8,128)S(1)}, f32[144,128]{1,0:T(8,128)S(1)}, u32[]{:S(2)}, u32[]{:S(2)}) collective-permute-start(f32[144,128]{1,0:T(8,128)S(1)} %get-tuple-element.34), channel_id=1, source_target_pairs={{0,4},{4,8},{8,12},{12,16},{16,20},{20,24},{24,28},{28,32},{32,36}... | collective-permute-start | bytes 221192 | tf_op jit(solution)/shard_map/ppermute | solution.py:485
  30.4 1.9 %collective-permute-start.3 = (f32[40,128]{1,0:T(8,128)S(1)}, f32[40,128]{1,0:T(8,128)S(1)}, u32[]{:S(2)}, u32[]{:S(2)}) collective-permute-start(f32[40,128]{1,0:T(8,128)S(1)} %get-tuple-element.35), channel_id=1, source_target_pairs={{4,0},{8,4},{12,8},{16,12},{20,16},{24,20},{28,24},{32,28},{36,32}... | collective-permute-start | bytes 61448 | tf_op jit(solution)/shard_map/ppermute | solution.py:485
  32.4 3.1 %collective-permute-start = (f32[8,128]{1,0:T(8,128)S(1)}, f32[8,128]{1,0:T(8,128)S(1)}, u32[]{:S(2)}, u32[]{:S(2)}) collective-permute-start(f32[8,128]{1,0:T(8,128)S(1)} %get-tuple-element.32), channel_id=1, source_target_pairs={{0,1},{1,2},{2,3},{3,0},{4,5},{5,6},{6,7},{7,4},{8,9},{9,10},{10,1... | collective-permute-start | bytes 12296 | tf_op jit(solution)/shard_map/ppermute | solution.py:485
  35.5 3.4 %collective-permute-start.1 = (f32[8,128]{1,0:T(8,128)S(1)}, f32[8,128]{1,0:T(8,128)S(1)}, u32[]{:S(2)}, u32[]{:S(2)}) collective-permute-start(f32[8,128]{1,0:T(8,128)S(1)} %get-tuple-element.33), channel_id=1, source_target_pairs={{0,3},{1,0},{2,1},{3,2},{4,7},{5,4},{6,5},{7,6},{8,11},{9,8},{10,9... | collective-permute-start | bytes 12296 | tf_op jit(solution)/shard_map/ppermute | solution.py:485
  38.9 0.0 collective-permute-done.left_ref
  38.9 1.0 collective-permute-done.1.right_ref
  39.8 0.0 collective-permute-done.3.rest_1_.refs_5_
  39.8 0.0 collective-permute-done.2.rest_0_.refs_4_
  39.9 1.1 shard_map.67
  40.9 20.4 %all_to_all.40 = f32[16,24,128]{2,1,0:T(8,128)S(1)} all-to-all(f32[16,24,128]{2,1,0:T(8,128)S(1)} %bitcast.40), channel_id=1, replica_groups=mesh['inst'=8,'axial'=16,'span'=4] {'axial'}, dimensions={0} | all-to-all | bytes 393216 | tf_op jit(solution)/shard_map/all_to_all | solution.py:478
  61.4 0.7 shard_map.68
  62.0 10.1 %all_to_all.41 = f32[16,4,128]{2,1,0:T(4,128)S(1)} all-to-all(f32[16,4,128]{2,1,0:T(4,128)S(1)} %bitcast.43), channel_id=1, replica_groups=mesh['inst'=8,'axial'=16,'span'=4] {'axial'}, dimensions={0} | all-to-all | bytes 65536 | tf_op jit(solution)/shard_map/all_to_all | solution.py:478
  72.1 0.9 copy-done.1
  73.0 0.3 shard_map.69
  73.3 15.2 %all_to_all.42 = f32[8,40,128]{2,1,0:T(8,128)S(1)} all-to-all(f32[8,40,128]{2,1,0:T(8,128)S(1)} %bitcast.41), channel_id=1, replica_groups=mesh['inst'=8,'axial'=16,'span'=4] {'inst'}, dimensions={0} | all-to-all | bytes 327680 | tf_op jit(solution)/shard_map/all_to_all | solution.py:478
  88.5 0.7 shard_map.70
  89.3 3.4 %all-to-all-start.5 = ((f32[8,40,128]{2,1,0:T(8,128)}), f32[8,40,128]{2,1,0:T(8,128)S(1)}, u32[]{:S(2)}, u32[]{:S(2)}) async-start(f32[8,40,128]{2,1,0:T(8,128)} %bitcast.54), calls=%async_computation.5 | async-start | bytes 327680 | tf_op jit(solution)/shard_map/all_to_all | solution.py:478
  92.7 3.1 %collective-permute-start.4 = (f32[8,128]{1,0:T(8,128)S(1)}, f32[8,128]{1,0:T(8,128)S(1)}, u32[]{:S(2)}, u32[]{:S(2)}) collective-permute-start(f32[8,128]{1,0:T(8,128)S(1)} %get-tuple-element.43), channel_id=1, source_target_pairs={{0,1},{1,2},{2,3},{3,0},{4,5},{5,6},{6,7},{7,4},{8,9},{9,10},{10,1... | collective-permute-start | bytes 12296 | tf_op jit(solution)/shard_map/ppermute | solution.py:485
  95.8 3.4 %collective-permute-start.5 = (f32[8,128]{1,0:T(8,128)S(1)}, f32[8,128]{1,0:T(8,128)S(1)}, u32[]{:S(2)}, u32[]{:S(2)}) collective-permute-start(f32[8,128]{1,0:T(8,128)S(1)} %get-tuple-element.44), channel_id=1, source_target_pairs={{0,3},{1,0},{2,1},{3,2},{4,7},{5,4},{6,5},{7,6},{8,11},{9,8},{10,9... | collective-permute-start | bytes 12296 | tf_op jit(solution)/shard_map/ppermute | solution.py:485
  99.2 1.2 collective-permute-done.5.right_ref
  100.4 0.5 all-to-all-done.5
  101.0 0.6 shard_map.71
  101.5 13.1 %all_to_all.43 = f32[16,4,128]{2,1,0:T(4,128)S(1)} all-to-all(f32[16,4,128]{2,1,0:T(4,128)S(1)} %bitcast.47), channel_id=1, replica_groups=mesh['inst'=8,'axial'=16,'span'=4] {'axial'}, dimensions={0} | all-to-all | bytes 65536 | tf_op jit(solution)/shard_map/all_to_all | solution.py:478
  114.6 0.7 shard_map.72
  115.3 10.3 %all_to_all.44 = f32[16,4,128]{2,1,0:T(4,128)S(1)} all-to-all(f32[16,4,128]{2,1,0:T(4,128)S(1)} %bitcast.45), channel_id=1, replica_groups=mesh['inst'=8,'axial'=16,'span'=4] {'axial'}, dimensions={0} | all-to-all | bytes 65536 | tf_op jit(solution)/shard_map/all_to_all | solution.py:478
  125.5 0.9 shard_map.73
  (5 shorter events, 0.0 us)
Async XLA Ops:
  1.6 19.0 %all-to-all-start = ((f32[8,40,128]{2,1,0:T(8,128)}), f32[8,40,128]{2,1,0:T(8,128)S(1)}, u32[]{:S(2)}, u32[]{:S(2)}) async-start(f32[8,40,128]{2,1,0:T(8,128)} %bitcast.2), calls=%async_computation | async-start | bytes 327680 | tf_op jit(solution)/shard_map/all_to_all | solution.py:478
  21.4 18.5 %all-to-all-start.1 = ((f32[8,40,128]{2,1,0:T(8,128)}), f32[8,40,128]{2,1,0:T(8,128)S(1)}, u32[]{:S(2)}, u32[]{:S(2)}) async-start(f32[8,40,128]{2,1,0:T(8,128)} %bitcast.53), calls=%async_computation.1 | async-start | bytes 327680 | tf_op jit(solution)/shard_map/all_to_all | solution.py:478
  24.8 15.1 %collective-permute-start.2 = (f32[144,128]{1,0:T(8,128)S(1)}, f32[144,128]{1,0:T(8,128)S(1)}, u32[]{:S(2)}, u32[]{:S(2)}) collective-permute-start(f32[144,128]{1,0:T(8,128)S(1)} %get-tuple-element.34), channel_id=1, source_target_pairs={{0,4},{4,8},{8,12},{12,16},{16,20},{20,24},{24,28},{28,32},{32,36}... | collective-permute-start | bytes 221192 | tf_op jit(solution)/shard_map/ppermute | solution.py:485
  30.4 9.4 %collective-permute-start.3 = (f32[40,128]{1,0:T(8,128)S(1)}, f32[40,128]{1,0:T(8,128)S(1)}, u32[]{:S(2)}, u32[]{:S(2)}) collective-permute-start(f32[40,128]{1,0:T(8,128)S(1)} %get-tuple-element.35), channel_id=1, source_target_pairs={{4,0},{8,4},{12,8},{16,12},{20,16},{24,20},{28,24},{32,28},{36,32}... | collective-permute-start | bytes 61448 | tf_op jit(solution)/shard_map/ppermute | solution.py:485
  32.4 6.5 %collective-permute-start = (f32[8,128]{1,0:T(8,128)S(1)}, f32[8,128]{1,0:T(8,128)S(1)}, u32[]{:S(2)}, u32[]{:S(2)}) collective-permute-start(f32[8,128]{1,0:T(8,128)S(1)} %get-tuple-element.32), channel_id=1, source_target_pairs={{0,1},{1,2},{2,3},{3,0},{4,5},{5,6},{6,7},{7,4},{8,9},{9,10},{10,1... | collective-permute-start | bytes 12296 | tf_op jit(solution)/shard_map/ppermute | solution.py:485
  35.5 4.4 %collective-permute-start.1 = (f32[8,128]{1,0:T(8,128)S(1)}, f32[8,128]{1,0:T(8,128)S(1)}, u32[]{:S(2)}, u32[]{:S(2)}) collective-permute-start(f32[8,128]{1,0:T(8,128)S(1)} %get-tuple-element.33), channel_id=1, source_target_pairs={{0,3},{1,0},{2,1},{3,2},{4,7},{5,4},{6,5},{7,6},{8,11},{9,8},{10,9... | collective-permute-start | bytes 12296 | tf_op jit(solution)/shard_map/ppermute | solution.py:485
  39.8 32.3 %copy-start = (f32[144,128]{1,0:T(8,128)}, f32[144,128]{1,0:T(8,128)S(1)}, u32[]{:S(2)}) copy-start(f32[144,128]{1,0:T(8,128)S(1)} %collective-permute-done.2.rest_0_.refs_4_) | copy-start | bytes 221188
  72.1 0.9 copy-start.1
  89.3 11.7 %all-to-all-start.5 = ((f32[8,40,128]{2,1,0:T(8,128)}), f32[8,40,128]{2,1,0:T(8,128)S(1)}, u32[]{:S(2)}, u32[]{:S(2)}) async-start(f32[8,40,128]{2,1,0:T(8,128)} %bitcast.54), calls=%async_computation.5 | async-start | bytes 327680 | tf_op jit(solution)/shard_map/all_to_all | solution.py:478
  92.7 6.5 %collective-permute-start.4 = (f32[8,128]{1,0:T(8,128)S(1)}, f32[8,128]{1,0:T(8,128)S(1)}, u32[]{:S(2)}, u32[]{:S(2)}) collective-permute-start(f32[8,128]{1,0:T(8,128)S(1)} %get-tuple-element.43), channel_id=1, source_target_pairs={{0,1},{1,2},{2,3},{3,0},{4,5},{5,6},{6,7},{7,4},{8,9},{9,10},{10,1... | collective-permute-start | bytes 12296 | tf_op jit(solution)/shard_map/ppermute | solution.py:485
  95.8 4.6 %collective-permute-start.5 = (f32[8,128]{1,0:T(8,128)S(1)}, f32[8,128]{1,0:T(8,128)S(1)}, u32[]{:S(2)}, u32[]{:S(2)}) collective-permute-start(f32[8,128]{1,0:T(8,128)S(1)} %get-tuple-element.44), channel_id=1, source_target_pairs={{0,3},{1,0},{2,1},{3,2},{4,7},{5,4},{6,5},{7,6},{8,11},{9,8},{10,9... | collective-permute-start | bytes 12296 | tf_op jit(solution)/shard_map/ppermute | solution.py:485

commit v7 on v6

--- a/solution.py
+++ b/solution.py
@@ -119,14 +119,14 @@
             out_ref[pl.ds(start + q * groups + first + g, 4, stride=4 * groups), :] = chunk[:4]
 
 
-def edge_lines(sub, lane, u, edges_ref):
+def edge_lines(sub, lane, u, last_ref, first_ref):
     last = jnp.zeros((8, 128), F32)
     initial = jnp.zeros((8, 128), F32)
     for n in range(STEPS * VARS):
         last = jnp.where(lane == n, lane_roll(u[n], n - 127), last)
         initial = jnp.where(lane == n, lane_roll(u[n], n), initial)
-    put(edges_ref, 0, pltpu.roll(last, 5, 0))
-    put(edges_ref, 1, pltpu.roll(initial, 3, 0))
+    last_ref[...] = pltpu.roll(last, 5, 0)
+    first_ref[...] = pltpu.roll(initial, 3, 0)
 
 
 def field_to_packed(raw_ref, out_ref, start=0):
@@ -159,33 +159,30 @@
         copy.wait()
 
 
-def pack_kernel(state_hbm, sent_ref, u_ref, edges_ref, state_ref, sems):
-    sub, lane = iotas()
-    arrive(fetch(state_hbm, state_ref, sems, 0))
-    field_to_packed(state_ref, u_ref)
-    sent_ref[...] = u_ref[...]
-    edge_lines(sub, lane, rows(u_ref, 0, STEPS * VARS), edges_ref)
-
-
-def time_kernel(weights, spread_ref, edges_ref, *rest):
-    halos_ref = rest[0] if len(rest) > 3 else None
-    out_ref, last_ref, first_ref = rest[-5:-2] if len(rest) > 3 else rest
+def time_term(weights, spread_ref, out_ref):
     for v in range(VARS):
         fields = [row(spread_ref, j * VARS + v) for j in range(INST)]
         for i in range(INST):
             put(out_ref, i * VARS + v, total(fields[j] * F32(weights[i, j]) for j in range(INST)))
+
+
+def time_kernel(weights, spread_ref, edges_ref, halos_ref, out_ref, last_ref, first_ref, up_ref, down_ref):
+    time_term(weights, spread_ref, out_ref)
     last_ref[...] = row(edges_ref, 0)
     first_ref[...] = row(edges_ref, 1)
-    if halos_ref is not None:
-        up_ref, down_ref = rest[-2:]
-        up_ref[...] = halos_ref[:UP, :]
-        down_ref[...] = halos_ref[UP:, :]
+    up_ref[...] = halos_ref[:UP, :]
+    down_ref[...] = halos_ref[UP:, :]
+
+
+def late_time_kernel(weights, spread_ref, left_ref, line_ref, out_ref, first_ref):
+    time_term(weights, spread_ref, out_ref)
+    first_ref[...] = line_ref[...]
 
 
 def maps_kernel(
-    u_ref, coupling_hbm, back_hbm, pivot_hbm, source_hbm, flags_hbm,
-    halos_ref, lines_ref, packed_ref,
-    prefix_ref, keep_ref, coupling_raw, back_raw, pivot_raw, source_raw, flags_ref, sems,
+    state_hbm, coupling_hbm, back_hbm, pivot_hbm, source_hbm, flags_hbm,
+    u_ref, edges_ref, halos_ref, lines_ref, packed_ref,
+    prefix_ref, keep_ref, state_raw, coupling_raw, back_raw, pivot_raw, source_raw, flags_ref, sems,
 ):
     sub, lane = iotas()
     block = lane // 32
@@ -193,7 +190,8 @@
     back_copies = fetch(back_hbm, back_raw, sems, VARS)
     pivot_copies = fetch(pivot_hbm, pivot_raw, sems, 2 * VARS)
     source_copies = fetch(source_hbm, source_raw, sems, 3 * VARS)
-    flags_copy = pltpu.make_async_copy(flags_hbm, flags_ref, sems.at[4 * VARS])
+    state_copies = fetch(state_hbm, state_raw, sems, 4 * VARS)
+    flags_copy = pltpu.make_async_copy(flags_hbm, flags_ref, sems.at[5 * VARS])
     flags_copy.start()
     top = sub < TILES
     arrive(coupling_copies)
@@ -204,6 +202,9 @@
     matrix_to_packed(pivot_raw, lines_ref, PIVOT)
     arrive(source_copies)
     field_to_packed(source_raw, lines_ref, CELLS)
+    arrive(state_copies)
+    field_to_packed(state_raw, u_ref)
+    edge_lines(sub, lane, rows(u_ref, 0, STEPS * VARS), edges_ref.at[:8], edges_ref.at[8:])
     flags_copy.wait()
     for half in range(2):
         for t in range(TILES):
@@ -304,6 +305,10 @@
         below_at, above_at, groups = 0, 0, FULL_GROUPS
         maps_copy = pltpu.make_async_copy(maps_hbm, packed_ref, sem)
         maps_copy.start()
+        for n in range(STEPS * VARS):
+            v, tile = n // 8, n % 8
+            rhs_ref[pl.ds(v * 8 + tile, STEPS, stride=VARS * 8), :] = row(time_ref, n)
+        time_ref = rhs_ref
     else:
         source_ref, packed_ref, rhs_ref = rest
         below_ref = above_ref = u_ref
@@ -401,7 +406,9 @@
     if last:
         out_ref, new_ref = rest
     else:
-        up_ref, above_ref, sent_ref, edges_ref, new_ref = rest
+        above_ref, up_hbm, sent_ref, last_ref, first_ref, new_ref, up_ref, sem = rest
+        up_copy = pltpu.make_async_copy(up_hbm, up_ref, sem)
+        up_copy.start()
     sub, lane = iotas()
     block = lane // 32
     top = sub < TILES
@@ -446,7 +453,8 @@
                     tile = new_ref[pl.ds(v * 8 + half * TILES + t, STEPS, stride=VARS * 8), :]
                     out_ref[v, half * STEPS : (half + 1) * STEPS, t * 128 : (t + 1) * 128] = tile
     else:
-        edge_lines(sub, lane, rows(new_ref, 0, STEPS * VARS), edges_ref)
+        edge_lines(sub, lane, rows(new_ref, 0, STEPS * VARS), last_ref, first_ref)
+        up_copy.wait()
         pairs = rows(up_ref, VARS, (SIZE + 1) // 2)
         blocks = [pairs[n // 2] if n % 2 else pltpu.roll(pairs[n // 2], 4, 0) for n in range(SIZE)]
         before = minus(entry, matvec(blocks, swap(x)))
@@ -491,37 +499,40 @@
     halo = (VARS * 8, 128)
     raw_field = (VARS, 2 * STEPS, TILES * 128)
     raw_matrix = (VARS,) + raw_field
-    sent, u, edges = call(
-        pack_kernel, [(FIELD, 128), (FIELD, 128), (16, 128)], state[0].transpose(1, 0, 2),
-        scratch=[raw_field, pltpu.SemaphoreType.DMA((VARS,))], far=1,
-    )
-    halos, lines, packed_maps = call(
+    cells_first = state[0].transpose(1, 0, 2)
+    sent = cells_first.reshape(VARS, 2, STEPS, TILES, 128).transpose(0, 1, 3, 2, 4).reshape(FIELD, 128)
+    u, edges, halos, lines, packed_maps = call(
         maps_kernel,
-        [(UP + halo[0], 128), (LINES, 128), (SEGMENTS * FULL_GROUPS, 128)],
-        u, coupling[0].transpose(1, 2, 0, 3), back_coupling[0].transpose(1, 2, 0, 3),
+        [(FIELD, 128), (16, 128), (UP + halo[0], 128), (LINES, 128), (SEGMENTS * FULL_GROUPS, 128)],
+        cells_first, coupling[0].transpose(1, 2, 0, 3), back_coupling[0].transpose(1, 2, 0, 3),
         pivot_inverse[0].transpose(1, 2, 0, 3), source_terms[0].transpose(1, 0, 2), wall_flags,
         scratch=[
-            (MATRIX, 128), (STEPS * 8, 128), raw_matrix, raw_matrix, raw_matrix, raw_field,
-            pltpu.VMEM((2 * STEPS, TILES * 128), jnp.int32), pltpu.SemaphoreType.DMA((4 * VARS + 1,)),
+            (MATRIX, 128), (STEPS * 8, 128), raw_field, raw_matrix, raw_matrix, raw_matrix, raw_field,
+            pltpu.VMEM((2 * STEPS, TILES * 128), jnp.int32), pltpu.SemaphoreType.DMA((5 * VARS + 1,)),
         ],
         flops=8_000_000,
         limit=16,
-        far=5,
-        sent=(2,),
+        far=6,
+        sent=(4,),
     )
     for sweep in range(SWEEPS):
         first = sweep == 0
         last = sweep == SWEEPS - 1
         spread = exchange(sent, "inst", INST)
-        term, left, right, *ends = call(
-            lambda *refs: time_kernel(weights, *refs),
-            [(FIELD, 128), edge, edge] + ([(UP, 128), halo] if first else []),
-            spread, edges, *((halos,) if first else ()), sent=(0,),
-        )
         if first:
-            up = moved(ends[0], "axial", 1, False)
-            above = moved(ends[1], "axial", -1, False)
-        left = moved(left, "span", 1, True)
+            term, left, right, up, above = call(
+                lambda *refs: time_kernel(weights, *refs),
+                [(FIELD, 128), edge, edge, (UP, 128), halo], spread, edges, halos, sent=(0,),
+            )
+            up = moved(up, "axial", 1, False)
+            above = moved(above, "axial", -1, False)
+            left = moved(left, "span", 1, True)
+        else:
+            left = moved(last_line, "span", 1, True)
+            term, right = call(
+                lambda *refs: late_time_kernel(weights, *refs), [(FIELD, 128), edge], spread, left, first_line,
+                sent=(0,),
+            )
         right = moved(right, "span", -1, True)
         time = exchange(term, "inst", INST)
         groups = FULL_GROUPS if first else VEC_GROUPS
@@ -546,9 +557,9 @@
                 lambda *refs: finish_kernel(True, *refs), [raw_field], *common, scratch=[(FIELD, 128)],
             )
         else:
-            sent, edges, u = call(
-                lambda *refs: finish_kernel(False, *refs), [(FIELD, 128), (16, 128), (FIELD + 2 * halo[0], 128)],
-                *common, up, above,
+            sent, last_line, first_line, u = call(
+                lambda *refs: finish_kernel(False, *refs), [(FIELD, 128), edge, edge, (FIELD + 2 * halo[0], 128)],
+                *common, above, up, scratch=[(UP, 128), pltpu.SemaphoreType.DMA], far=1, sent=(0,),
             )
     return result.transpose(1, 0, 2)[None]
 

time: 127 us -> 127 us (level)
  blocking collectives: 69 us -> 54 us
  starting transfers between devices: 38.2 us -> 46.3 us
  waiting for transfers between devices: 6.81 us -> 14.3 us
    all_to_all x5 -> x4, blocking collectives: 69 us -> 54 us  [exchange(): lax.all_to_all(value.reshape(count, shape[0] // count, 128), axis, 0, 0)]
    all_to_all x3 -> x4, starting transfers between devices: 17.6 us -> 24.7 us  [exchange(): lax.all_to_all(value.reshape(count, shape[0] // count, 128), axis, 0, 0)]
    all_to_all x3 -> x4, waiting for transfers between devices: 4.6 us -> 10.2 us  [exchange(): lax.all_to_all(value.reshape(count, shape[0] // count, 128), axis, 0, 0)]
    ppermute x6, waiting for transfers between devices: 2.21 us -> 4.15 us  [moved(): return lax.ppermute(value, axis, pairs)]
    pallas_call x10 -> x9, Pallas kernels: 11.3 us -> 11.5 us  [call(): pl.pallas_call(kernel, out_shape=outs, in_specs=specs, out_specs=[pl.Bloc...]
  transfers between devices with their start and end apart: 9 -> 10, of which waited for: 4 -> 6; matrix products, arithmetic and copies ran while one was open for 0% -> 0% of each run, Pallas kernels for 3% -> 3%
where the time goes in v7:
time: 127 us; the launch traced here: 126 us
  blocking collectives  54 us (43%)
  starting transfers between devices  46.3 us (36%)
  waiting for transfers between devices  14.3 us (11%)
  Pallas kernels  11.5 us (9%)
    all_to_all x4, blocking collectives, exchange(): lax.all_to_all(value.reshape(count, shape[0] // count, 128), axis, 0, 0)  54 us
    all_to_all x4, starting transfers between devices, exchange(): lax.all_to_all(value.reshape(count, shape[0] // count, 128), axis, 0, 0)  24.7 us
    ppermute x6, starting transfers between devices, moved(): return lax.ppermute(value, axis, pairs)  21.5 us
    pallas_call x9, Pallas kernels, call(): pl.pallas_call(kernel, out_shape=outs, in_specs=specs, out_specs=[pl.Bloc...  11.5 us
    all_to_all x4, waiting for transfers between devices, exchange(): lax.all_to_all(value.reshape(count, shape[0] // count, 128), axis, 0, 0)  10.2 us
    ppermute x6, waiting for transfers between devices, moved(): return lax.ppermute(value, axis, pairs)  4.15 us
  transfers between devices with their start and end apart: 10, of which 6 were waited for; matrix products, arithmetic and copies ran while one was open for 0% of the time, Pallas kernels for 3%

profile of v7, /device:TPU:1, one launch (start us, length us, event | category | flops | bytes accessed | tf_op | source)
XLA Modules:
  0.0 126.3 jit_solution(7907776696104949648)
XLA Ops:
  0.0 10.9 %all-to-all-start = ((f32[8,40,128]{2,1,0:T(8,128)}), f32[8,40,128]{2,1,0:T(8,128)S(1)}, u32[]{:S(2)}, u32[]{:S(2)}) async-start(f32[8,40,128]{2,1,0:T(8,128)} %bitcast.55), calls=%async_computation | async-start | bytes 327680 | tf_op jit(solution)/shard_map/all_to_all | solution.py:486
  10.9 4.3 %shard_map.64 = (f32[320,128]{1,0:T(8,128)S(1)}, f32[16,128]{1,0:T(8,128)S(1)}, f32[184,128]{1,0:T(8,128)S(1)}, f32[5720,128]{1,0:T(8,128)S(1)}, f32[384,128]{1,0:T(8,128)}) custom-call(f32[5,16,512]{2,1,0:T(8,128)} %bitcast.56, f32[5,5,16,512]{3,2,1,0:T(8,128)} %bitcast.52, f32[5,5,16,512]{3,2,1,0:T(8,128)} %bitcast.53, f32[5,5,16,512]{3,2,1,0:T(8,128)} %bitcast.54, ...), custom_call_target="tpu_custom_call" | custom-call | flops 8000000 | bytes 6209536 | tf_op jit(solution)/shard_map/pallas_call | solution.py:473
  15.2 3.9 %all-to-all-done = f32[8,40,128]{2,1,0:T(8,128)S(1)} async-done(((f32[8,40,128]{2,1,0:T(8,128)}), f32[8,40,128]{2,1,0:T(8,128)S(1)}, u32[]{:S(2)}, u32[]{:S(2)}) %all-to-all-start) | async-done | bytes 163872 | tf_op jit(solution)/shard_map/all_to_all | solution.py:486
  19.0 0.7 shard_map.65
  19.8 3.4 %all-to-all-start.1 = ((f32[8,40,128]{2,1,0:T(8,128)}), f32[8,40,128]{2,1,0:T(8,128)S(1)}, u32[]{:S(2)}, u32[]{:S(2)}) async-start(f32[8,40,128]{2,1,0:T(8,128)} %bitcast.58), calls=%async_computation.1 | async-start | bytes 327680 | tf_op jit(solution)/shard_map/all_to_all | solution.py:486
  23.2 5.7 %collective-permute-start.2 = (f32[144,128]{1,0:T(8,128)S(1)}, f32[144,128]{1,0:T(8,128)S(1)}, u32[]{:S(2)}, u32[]{:S(2)}) collective-permute-start(f32[144,128]{1,0:T(8,128)S(1)} %get-tuple-element.32), channel_id=1, source_target_pairs={{0,4},{4,8},{8,12},{12,16},{16,20},{20,24},{24,28},{28,32},{32,36}... | collective-permute-start | bytes 221192 | tf_op jit(solution)/shard_map/ppermute | solution.py:493
  28.8 1.9 %collective-permute-start.3 = (f32[40,128]{1,0:T(8,128)S(1)}, f32[40,128]{1,0:T(8,128)S(1)}, u32[]{:S(2)}, u32[]{:S(2)}) collective-permute-start(f32[40,128]{1,0:T(8,128)S(1)} %get-tuple-element.33), channel_id=1, source_target_pairs={{4,0},{8,4},{12,8},{16,12},{20,16},{24,20},{28,24},{32,28},{36,32}... | collective-permute-start | bytes 61448 | tf_op jit(solution)/shard_map/ppermute | solution.py:493
  30.8 3.1 %collective-permute-start = (f32[8,128]{1,0:T(8,128)S(1)}, f32[8,128]{1,0:T(8,128)S(1)}, u32[]{:S(2)}, u32[]{:S(2)}) collective-permute-start(f32[8,128]{1,0:T(8,128)S(1)} %get-tuple-element.30), channel_id=1, source_target_pairs={{0,1},{1,2},{2,3},{3,0},{4,5},{5,6},{6,7},{7,4},{8,9},{9,10},{10,1... | collective-permute-start | bytes 12296 | tf_op jit(solution)/shard_map/ppermute | solution.py:493
  33.9 3.4 %collective-permute-start.1 = (f32[8,128]{1,0:T(8,128)S(1)}, f32[8,128]{1,0:T(8,128)S(1)}, u32[]{:S(2)}, u32[]{:S(2)}) collective-permute-start(f32[8,128]{1,0:T(8,128)S(1)} %get-tuple-element.31), channel_id=1, source_target_pairs={{0,3},{1,0},{2,1},{3,2},{4,7},{5,4},{6,5},{7,6},{8,11},{9,8},{10,9... | collective-permute-start | bytes 12296 | tf_op jit(solution)/shard_map/ppermute | solution.py:493
  37.3 0.0 collective-permute-done.left_ref
  37.3 1.0 collective-permute-done.1.right_ref
  38.2 0.0 collective-permute-done.3.rest_1_.refs_4_
  38.2 0.0 collective-permute-done.2.rest_0_.refs_5_
  38.3 1.1 shard_map.66
  39.4 20.4 %all_to_all.40 = f32[16,24,128]{2,1,0:T(8,128)S(1)} all-to-all(f32[16,24,128]{2,1,0:T(8,128)S(1)} %bitcast.45), channel_id=1, replica_groups=mesh['inst'=8,'axial'=16,'span'=4] {'axial'}, dimensions={0} | all-to-all | bytes 393216 | tf_op jit(solution)/shard_map/all_to_all | solution.py:486
  59.8 0.7 shard_map.67
  60.5 10.1 %all_to_all.41 = f32[16,4,128]{2,1,0:T(4,128)S(1)} all-to-all(f32[16,4,128]{2,1,0:T(4,128)S(1)} %bitcast.47), channel_id=1, replica_groups=mesh['inst'=8,'axial'=16,'span'=4] {'axial'}, dimensions={0} | all-to-all | bytes 65536 | tf_op jit(solution)/shard_map/all_to_all | solution.py:486
  70.6 1.8 %shard_map.68 = (f32[320,128]{1,0:T(8,128)}, f32[8,128]{1,0:T(8,128)S(1)}, f32[8,128]{1,0:T(8,128)S(1)}, f32[400,128]{1,0:T(8,128)S(1)}) custom-call(f32[64,128]{1,0:T(8,128)S(1)} %bitcast.50, f32[320,128]{1,0:T(8,128)S(1)} %get-tuple-element.28.u_ref.refs_1_, f32[400,128]{1,0:T(8,128)S(1)} %get-tuple-element.36.refs_2_, ...), custom_call_target="tpu_custom_call" | custom-call | flops 100000 | bytes 3801088 | tf_op jit(solution)/shard_map/pallas_call | solution.py:473
  72.4 6.8 %all-to-all-start.4 = ((f32[8,40,128]{2,1,0:T(8,128)}), f32[8,40,128]{2,1,0:T(8,128)S(1)}, u32[]{:S(2)}, u32[]{:S(2)}) async-start(f32[8,40,128]{2,1,0:T(8,128)} %bitcast.59), calls=%async_computation.4 | async-start | bytes 327680 | tf_op jit(solution)/shard_map/all_to_all | solution.py:486
  79.2 3.1 %collective-permute-start.4 = (f32[8,128]{1,0:T(8,128)S(1)}, f32[8,128]{1,0:T(8,128)S(1)}, u32[]{:S(2)}, u32[]{:S(2)}) collective-permute-start(f32[8,128]{1,0:T(8,128)S(1)} %get-tuple-element.38), channel_id=1, source_target_pairs={{0,1},{1,2},{2,3},{3,0},{4,5},{5,6},{6,7},{7,4},{8,9},{9,10},{10,1... | collective-permute-start | bytes 12296 | tf_op jit(solution)/shard_map/ppermute | solution.py:493
  82.4 2.4 %collective-permute-done.4.refs_1_.left_ref = f32[8,128]{1,0:T(8,128)S(1)} collective-permute-done((f32[8,128]{1,0:T(8,128)S(1)}, f32[8,128]{1,0:T(8,128)S(1)}, u32[]{:S(2)}, u32[]{:S(2)}) %collective-permute-start.4) | collective-permute-done | bytes 4128 | tf_op jit(solution)/shard_map/ppermute | solution.py:493
  84.8 3.0 %all-to-all-done.4 = f32[8,40,128]{2,1,0:T(8,128)S(1)} async-done(((f32[8,40,128]{2,1,0:T(8,128)}), f32[8,40,128]{2,1,0:T(8,128)S(1)}, u32[]{:S(2)}, u32[]{:S(2)}) %all-to-all-start.4) | async-done | bytes 163872 | tf_op jit(solution)/shard_map/all_to_all | solution.py:486
  87.8 0.7 shard_map.69
  88.6 3.6 %all-to-all-start.5 = ((f32[8,40,128]{2,1,0:T(8,128)}), f32[8,40,128]{2,1,0:T(8,128)S(1)}, u32[]{:S(2)}, u32[]{:S(2)}) async-start(f32[8,40,128]{2,1,0:T(8,128)} %bitcast.60), calls=%async_computation.5 | async-start | bytes 327680 | tf_op jit(solution)/shard_map/all_to_all | solution.py:486
  92.2 4.3 %collective-permute-start.5 = (f32[8,128]{1,0:T(8,128)S(1)}, f32[8,128]{1,0:T(8,128)S(1)}, u32[]{:S(2)}, u32[]{:S(2)}) collective-permute-start(f32[8,128]{1,0:T(8,128)S(1)} %get-tuple-element.42), channel_id=1, source_target_pairs={{0,3},{1,0},{2,1},{3,2},{4,7},{5,4},{6,5},{7,6},{8,11},{9,8},{10,9... | collective-permute-start | bytes 12296 | tf_op jit(solution)/shard_map/ppermute | solution.py:493
  96.5 0.7 collective-permute-done.5.right_ref
  97.3 3.3 %all-to-all-done.5 = f32[8,40,128]{2,1,0:T(8,128)S(1)} async-done(((f32[8,40,128]{2,1,0:T(8,128)}), f32[8,40,128]{2,1,0:T(8,128)S(1)}, u32[]{:S(2)}, u32[]{:S(2)}) %all-to-all-start.5) | async-done | bytes 163872 | tf_op jit(solution)/shard_map/all_to_all | solution.py:486
  100.6 0.6 shard_map.70
  101.2 13.3 %all_to_all.42 = f32[16,4,128]{2,1,0:T(4,128)S(1)} all-to-all(f32[16,4,128]{2,1,0:T(4,128)S(1)} %bitcast.51), channel_id=1, replica_groups=mesh['inst'=8,'axial'=16,'span'=4] {'axial'}, dimensions={0} | all-to-all | bytes 65536 | tf_op jit(solution)/shard_map/all_to_all | solution.py:486
  114.4 0.7 shard_map.71
  115.1 10.3 %all_to_all.43 = f32[16,4,128]{2,1,0:T(4,128)S(1)} all-to-all(f32[16,4,128]{2,1,0:T(4,128)S(1)} %bitcast.49), channel_id=1, replica_groups=mesh['inst'=8,'axial'=16,'span'=4] {'axial'}, dimensions={0} | all-to-all | bytes 65536 | tf_op jit(solution)/shard_map/all_to_all | solution.py:486
  125.4 0.9 shard_map.72
  (3 shorter events, 0.0 us)
Async XLA Ops:
  0.0 19.0 %all-to-all-start = ((f32[8,40,128]{2,1,0:T(8,128)}), f32[8,40,128]{2,1,0:T(8,128)S(1)}, u32[]{:S(2)}, u32[]{:S(2)}) async-start(f32[8,40,128]{2,1,0:T(8,128)} %bitcast.55), calls=%async_computation | async-start | bytes 327680 | tf_op jit(solution)/shard_map/all_to_all | solution.py:486
  19.8 18.5 %all-to-all-start.1 = ((f32[8,40,128]{2,1,0:T(8,128)}), f32[8,40,128]{2,1,0:T(8,128)S(1)}, u32[]{:S(2)}, u32[]{:S(2)}) async-start(f32[8,40,128]{2,1,0:T(8,128)} %bitcast.58), calls=%async_computation.1 | async-start | bytes 327680 | tf_op jit(solution)/shard_map/all_to_all | solution.py:486
  23.2 15.1 %collective-permute-start.2 = (f32[144,128]{1,0:T(8,128)S(1)}, f32[144,128]{1,0:T(8,128)S(1)}, u32[]{:S(2)}, u32[]{:S(2)}) collective-permute-start(f32[144,128]{1,0:T(8,128)S(1)} %get-tuple-element.32), channel_id=1, source_target_pairs={{0,4},{4,8},{8,12},{12,16},{16,20},{20,24},{24,28},{28,32},{32,36}... | collective-permute-start | bytes 221192 | tf_op jit(solution)/shard_map/ppermute | solution.py:493
  28.8 9.4 %collective-permute-start.3 = (f32[40,128]{1,0:T(8,128)S(1)}, f32[40,128]{1,0:T(8,128)S(1)}, u32[]{:S(2)}, u32[]{:S(2)}) collective-permute-start(f32[40,128]{1,0:T(8,128)S(1)} %get-tuple-element.33), channel_id=1, source_target_pairs={{4,0},{8,4},{12,8},{16,12},{20,16},{24,20},{28,24},{32,28},{36,32}... | collective-permute-start | bytes 61448 | tf_op jit(solution)/shard_map/ppermute | solution.py:493
  30.8 6.5 %collective-permute-start = (f32[8,128]{1,0:T(8,128)S(1)}, f32[8,128]{1,0:T(8,128)S(1)}, u32[]{:S(2)}, u32[]{:S(2)}) collective-permute-start(f32[8,128]{1,0:T(8,128)S(1)} %get-tuple-element.30), channel_id=1, source_target_pairs={{0,1},{1,2},{2,3},{3,0},{4,5},{5,6},{6,7},{7,4},{8,9},{9,10},{10,1... | collective-permute-start | bytes 12296 | tf_op jit(solution)/shard_map/ppermute | solution.py:493
  33.9 4.4 %collective-permute-start.1 = (f32[8,128]{1,0:T(8,128)S(1)}, f32[8,128]{1,0:T(8,128)S(1)}, u32[]{:S(2)}, u32[]{:S(2)}) collective-permute-start(f32[8,128]{1,0:T(8,128)S(1)} %get-tuple-element.31), channel_id=1, source_target_pairs={{0,3},{1,0},{2,1},{3,2},{4,7},{5,4},{6,5},{7,6},{8,11},{9,8},{10,9... | collective-permute-start | bytes 12296 | tf_op jit(solution)/shard_map/ppermute | solution.py:493
  38.2 1.2 copy-start
  72.4 15.4 %all-to-all-start.4 = ((f32[8,40,128]{2,1,0:T(8,128)}), f32[8,40,128]{2,1,0:T(8,128)S(1)}, u32[]{:S(2)}, u32[]{:S(2)}) async-start(f32[8,40,128]{2,1,0:T(8,128)} %bitcast.59), calls=%async_computation.4 | async-start | bytes 327680 | tf_op jit(solution)/shard_map/all_to_all | solution.py:486
  79.2 5.6 %collective-permute-start.4 = (f32[8,128]{1,0:T(8,128)S(1)}, f32[8,128]{1,0:T(8,128)S(1)}, u32[]{:S(2)}, u32[]{:S(2)}) collective-permute-start(f32[8,128]{1,0:T(8,128)S(1)} %get-tuple-element.38), channel_id=1, source_target_pairs={{0,1},{1,2},{2,3},{3,0},{4,5},{5,6},{6,7},{7,4},{8,9},{9,10},{10,1... | collective-permute-start | bytes 12296 | tf_op jit(solution)/shard_map/ppermute | solution.py:493
  88.6 12.0 %all-to-all-start.5 = ((f32[8,40,128]{2,1,0:T(8,128)}), f32[8,40,128]{2,1,0:T(8,128)S(1)}, u32[]{:S(2)}, u32[]{:S(2)}) async-start(f32[8,40,128]{2,1,0:T(8,128)} %bitcast.60), calls=%async_computation.5 | async-start | bytes 327680 | tf_op jit(solution)/shard_map/all_to_all | solution.py:486
  92.2 5.1 %collective-permute-start.5 = (f32[8,128]{1,0:T(8,128)S(1)}, f32[8,128]{1,0:T(8,128)S(1)}, u32[]{:S(2)}, u32[]{:S(2)}) collective-permute-start(f32[8,128]{1,0:T(8,128)S(1)} %get-tuple-element.42), channel_id=1, source_target_pairs={{0,3},{1,0},{2,1},{3,2},{4,7},{5,4},{6,5},{7,6},{8,11},{9,8},{10,9... | collective-permute-start | bytes 12296 | tf_op jit(solution)/shard_map/ppermute | solution.py:493

commit v8 on v7

--- a/solution.py
+++ b/solution.py
@@ -27,6 +27,7 @@
 UP = VARS * 8 + (SIZE + 1) // 2 * 8
 BELOW = STEPS * VARS
 ABOVE = BELOW + VARS
+KEPT = STEPS * VARS + 2 * VARS
 
 
 def spectral():
@@ -159,30 +160,51 @@
         copy.wait()
 
 
-def time_term(weights, spread_ref, out_ref):
-    for v in range(VARS):
-        fields = [row(spread_ref, j * VARS + v) for j in range(INST)]
-        for i in range(INST):
-            put(out_ref, i * VARS + v, total(fields[j] * F32(weights[i, j]) for j in range(INST)))
-
-
-def time_kernel(weights, spread_ref, edges_ref, halos_ref, out_ref, last_ref, first_ref, up_ref, down_ref):
-    time_term(weights, spread_ref, out_ref)
-    last_ref[...] = row(edges_ref, 0)
-    first_ref[...] = row(edges_ref, 1)
+def pack_kernel(state_hbm, u_ref, last_ref, first_ref, state_ref, sems):
+    sub, lane = iotas()
+    arrive(fetch(state_hbm, state_ref, sems, 0))
+    field_to_packed(state_ref, u_ref)
+    edge_lines(sub, lane, rows(u_ref, 0, STEPS * VARS), last_ref, first_ref)
+
+
+def piece_out(stage_ref, out_hbm, sems, index, count):
+    piece = pl.ds(index * count, count)
+    copy = pltpu.make_async_copy(stage_ref.at[piece], out_hbm.at[piece], sems.at[index])
+    copy.start()
+    return copy
+
+
+def time_term(weights, spread_ref, out_hbm, stage_ref, sems):
+    copies = []
+    for i in range(INST):
+        for v in range(VARS):
+            terms = [row(spread_ref, j * VARS + v) * F32(weights[i, j]) for j in range(INST)]
+            put(stage_ref, i * VARS + v, total(terms))
+        copies.append(piece_out(stage_ref, out_hbm, sems, i, VARS * 8))
+    return copies
+
+
+def time_kernel(
+    weights, spread_ref, left_ref, line_ref, halos_ref,
+    out_hbm, first_ref, up_ref, down_ref, stage_ref, sems,
+):
+    copies = time_term(weights, spread_ref, out_hbm, stage_ref, sems)
+    first_ref[...] = line_ref[...]
     up_ref[...] = halos_ref[:UP, :]
     down_ref[...] = halos_ref[UP:, :]
-
-
-def late_time_kernel(weights, spread_ref, left_ref, line_ref, out_ref, first_ref):
-    time_term(weights, spread_ref, out_ref)
+    arrive(copies)
+
+
+def late_time_kernel(weights, spread_ref, left_ref, line_ref, out_hbm, first_ref, stage_ref, sems):
+    copies = time_term(weights, spread_ref, out_hbm, stage_ref, sems)
     first_ref[...] = line_ref[...]
+    arrive(copies)
 
 
 def maps_kernel(
-    state_hbm, coupling_hbm, back_hbm, pivot_hbm, source_hbm, flags_hbm,
-    u_ref, edges_ref, halos_ref, lines_ref, packed_ref,
-    prefix_ref, keep_ref, state_raw, coupling_raw, back_raw, pivot_raw, source_raw, flags_ref, sems,
+    u_ref, coupling_hbm, back_hbm, pivot_hbm, source_hbm, flags_hbm,
+    halos_ref, lines_ref, packed_hbm,
+    prefix_ref, keep_ref, coupling_raw, back_raw, pivot_raw, source_raw, flags_ref, packed_ref, sems,
 ):
     sub, lane = iotas()
     block = lane // 32
@@ -190,35 +212,13 @@
     back_copies = fetch(back_hbm, back_raw, sems, VARS)
     pivot_copies = fetch(pivot_hbm, pivot_raw, sems, 2 * VARS)
     source_copies = fetch(source_hbm, source_raw, sems, 3 * VARS)
-    state_copies = fetch(state_hbm, state_raw, sems, 4 * VARS)
-    flags_copy = pltpu.make_async_copy(flags_hbm, flags_ref, sems.at[5 * VARS])
+    flags_copy = pltpu.make_async_copy(flags_hbm, flags_ref, sems.at[4 * VARS])
     flags_copy.start()
     top = sub < TILES
     arrive(coupling_copies)
     matrix_to_packed(coupling_raw, lines_ref, 0)
     arrive(back_copies)
     matrix_to_packed(back_raw, lines_ref, MATRIX)
-    arrive(pivot_copies)
-    matrix_to_packed(pivot_raw, lines_ref, PIVOT)
-    arrive(source_copies)
-    field_to_packed(source_raw, lines_ref, CELLS)
-    arrive(state_copies)
-    field_to_packed(state_raw, u_ref)
-    edge_lines(sub, lane, rows(u_ref, 0, STEPS * VARS), edges_ref.at[:8], edges_ref.at[8:])
-    flags_copy.wait()
-    for half in range(2):
-        for t in range(TILES):
-            flags = flags_ref[half * STEPS : (half + 1) * STEPS, t * 128 : (t + 1) * 128]
-            keep_ref[pl.ds(half * TILES + t, STEPS, stride=8), :] = (1 - flags).astype(F32)
-
-    def mask(k, carry):
-        keep = row(keep_ref, k)
-        for n in range(SIZE):
-            put(lines_ref, PIVOT // 8 + k * SIZE + n, keep * row(lines_ref, PIVOT // 8 + k * SIZE + n))
-        return carry
-
-    lax.fori_loop(0, STEPS, mask, 0)
-
     def coupling(k):
         return rows(lines_ref, k * SIZE, SIZE)
 
@@ -261,12 +261,32 @@
     for n in range(SIZE):
         put(prefix_ref, 2 * SIZE + n, whole[n])
     pack_lines(packed_ref, 0, block, rows(prefix_ref, 0, 3 * SIZE), VEC_GROUPS, FULL_GROUPS)
+    packed_copy = pltpu.make_async_copy(packed_ref, packed_hbm, sems.at[4 * VARS + 1])
+    packed_copy.start()
+    arrive(pivot_copies)
+    matrix_to_packed(pivot_raw, lines_ref, PIVOT)
+    arrive(source_copies)
+    field_to_packed(source_raw, lines_ref, CELLS)
+    flags_copy.wait()
+    for half in range(2):
+        for t in range(TILES):
+            flags = flags_ref[half * STEPS : (half + 1) * STEPS, t * 128 : (t + 1) * 128]
+            keep_ref[pl.ds(half * TILES + t, STEPS, stride=8), :] = (1 - flags).astype(F32)
+
+    def mask(k, carry):
+        keep = row(keep_ref, k)
+        for n in range(SIZE):
+            put(lines_ref, PIVOT // 8 + k * SIZE + n, keep * row(lines_ref, PIVOT // 8 + k * SIZE + n))
+        return carry
+
+    lax.fori_loop(0, STEPS, mask, 0)
     halos_ref[: VARS * 8, :] = u_ref[(STEPS - 1) * VARS * 8 :, :]
     last = back(STEPS - 1)
     for n in range(0, SIZE, 2):
         pair = jnp.where(top, pltpu.roll(last[n], 4, 0), last[min(n + 1, SIZE - 1)])
         put(halos_ref, VARS + n // 2, pair)
     halos_ref[UP:, :] = u_ref[: VARS * 8, :]
+    packed_copy.wait()
 
 
 def stencil(
@@ -301,10 +321,11 @@
     sub, lane = iotas()
     block = lane // 32
     if len(rest) > 3:
-        below_ref, above_ref, maps_hbm, source_ref, packed_ref, rhs_ref, sem = rest
+        below_ref, above_ref, maps_hbm, source_ref, packed_ref, rhs_ref, sems = rest
         below_at, above_at, groups = 0, 0, FULL_GROUPS
-        maps_copy = pltpu.make_async_copy(maps_hbm, packed_ref, sem)
-        maps_copy.start()
+        maps_copies = [piece_out(maps_hbm, packed_ref, sems, n, SEGMENTS * FULL_GROUPS // 4) for n in range(4)]
+        source_ref[KEPT * 8 : KEPT * 8 + UP, :] = below_ref[...]
+        source_ref[KEPT * 8 + UP :, :] = above_ref[...]
         for n in range(STEPS * VARS):
             v, tile = n // 8, n % 8
             rhs_ref[pl.ds(v * 8 + tile, STEPS, stride=VARS * 8), :] = row(time_ref, n)
@@ -345,7 +366,7 @@
     whole_first = plus(x, matvec(behind, inner))
     values = whole_end + whole_first + [jnp.zeros((8, 128), F32)] * (4 * VEC_GROUPS - 2 * VARS)
     if groups == FULL_GROUPS:
-        maps_copy.wait()
+        arrive(maps_copies)
     pack_lines(packed_ref, 0, block, values, 0, groups)
 
 
@@ -404,11 +425,10 @@
 
 def finish_kernel(last, recv_ref, u_ref, source_ref, lines_ref, *rest):
     if last:
-        out_ref, new_ref = rest
+        out_hbm, new_ref, out_ref, sems = rest
     else:
-        above_ref, up_hbm, sent_ref, last_ref, first_ref, new_ref, up_ref, sem = rest
-        up_copy = pltpu.make_async_copy(up_hbm, up_ref, sem)
-        up_copy.start()
+        sent_hbm, last_ref, first_ref, new_ref, sems = rest
+    copies = []
     sub, lane = iotas()
     block = lane // 32
     top = sub < TILES
@@ -446,22 +466,25 @@
         x = minus(kept[k], matvec(rows(lines_ref, (STEPS + k) * SIZE, SIZE), x))
         for v in range(VARS):
             put(new_ref, k * VARS + v, row(u_ref, k * VARS + v) + x[v])
+        if not last:
+            copies.append(piece_out(new_ref, sent_hbm, sems, k, VARS * 8))
     if last:
         for v in range(VARS):
             for half in range(2):
                 for t in range(TILES):
                     tile = new_ref[pl.ds(v * 8 + half * TILES + t, STEPS, stride=VARS * 8), :]
                     out_ref[v, half * STEPS : (half + 1) * STEPS, t * 128 : (t + 1) * 128] = tile
+            copies.append(pltpu.make_async_copy(out_ref.at[v], out_hbm.at[v], sems.at[v]))
+            copies[-1].start()
     else:
         edge_lines(sub, lane, rows(new_ref, 0, STEPS * VARS), last_ref, first_ref)
-        up_copy.wait()
-        pairs = rows(up_ref, VARS, (SIZE + 1) // 2)
+        pairs = rows(source_ref, KEPT + VARS, (SIZE + 1) // 2)
         blocks = [pairs[n // 2] if n % 2 else pltpu.roll(pairs[n // 2], 4, 0) for n in range(SIZE)]
         before = minus(entry, matvec(blocks, swap(x)))
         for v in range(VARS):
-            put(new_ref, BELOW + v, row(up_ref, v) + before[v])
-            put(new_ref, ABOVE + v, row(above_ref, v) + after[v])
-        sent_ref[...] = new_ref[:FIELD, :]
+            put(new_ref, BELOW + v, row(source_ref, KEPT + v) + before[v])
+            put(new_ref, ABOVE + v, row(source_ref, KEPT + UP // 8 + v) + after[v])
+    arrive(copies)
 
 
 def call(kernel, shapes, *args, scratch=(), flops=100_000, limit=8, far=0, sent=()):
@@ -474,7 +497,7 @@
         kernel,
         out_shape=outs,
         in_specs=specs,
-        out_specs=[pl.BlockSpec(memory_space=pltpu.VMEM)] * len(outs),
+        out_specs=[pl.BlockSpec(memory_space=pltpu.HBM if n in sent else pltpu.VMEM) for n in range(len(outs))],
         scratch_shapes=[pltpu.VMEM(item, F32) if isinstance(item, tuple) else item for item in scratch],
         cost_estimate=pl.CostEstimate(flops=flops, bytes_accessed=moved, transcendentals=0),
         compiler_params=pltpu.CompilerParams(vmem_limit_bytes=limit * 1024 * 1024),
@@ -501,46 +524,51 @@
     raw_matrix = (VARS,) + raw_field
     cells_first = state[0].transpose(1, 0, 2)
     sent = cells_first.reshape(VARS, 2, STEPS, TILES, 128).transpose(0, 1, 3, 2, 4).reshape(FIELD, 128)
-    u, edges, halos, lines, packed_maps = call(
+    u, last_line, first_line = call(
+        pack_kernel, [(FIELD, 128), edge, edge], cells_first,
+        scratch=[raw_field, pltpu.SemaphoreType.DMA((VARS,))], far=1,
+    )
+    halos, lines, packed_maps = call(
         maps_kernel,
-        [(FIELD, 128), (16, 128), (UP + halo[0], 128), (LINES, 128), (SEGMENTS * FULL_GROUPS, 128)],
-        cells_first, coupling[0].transpose(1, 2, 0, 3), back_coupling[0].transpose(1, 2, 0, 3),
+        [(UP + halo[0], 128), (LINES, 128), (SEGMENTS * FULL_GROUPS, 128)],
+        u, coupling[0].transpose(1, 2, 0, 3), back_coupling[0].transpose(1, 2, 0, 3),
         pivot_inverse[0].transpose(1, 2, 0, 3), source_terms[0].transpose(1, 0, 2), wall_flags,
         scratch=[
-            (MATRIX, 128), (STEPS * 8, 128), raw_field, raw_matrix, raw_matrix, raw_matrix, raw_field,
-            pltpu.VMEM((2 * STEPS, TILES * 128), jnp.int32), pltpu.SemaphoreType.DMA((5 * VARS + 1,)),
+            (MATRIX, 128), (STEPS * 8, 128), raw_matrix, raw_matrix, raw_matrix, raw_field,
+            pltpu.VMEM((2 * STEPS, TILES * 128), jnp.int32), (SEGMENTS * FULL_GROUPS, 128),
+            pltpu.SemaphoreType.DMA((4 * VARS + 2,)),
         ],
         flops=8_000_000,
         limit=16,
-        far=6,
-        sent=(4,),
+        far=5,
+        sent=(2,),
     )
+    stage = [(FIELD, 128), pltpu.SemaphoreType.DMA((INST,))]
     for sweep in range(SWEEPS):
         first = sweep == 0
         last = sweep == SWEEPS - 1
         spread = exchange(sent, "inst", INST)
+        left = moved(last_line, "span", 1, True)
         if first:
-            term, left, right, up, above = call(
+            term, right, up, above = call(
                 lambda *refs: time_kernel(weights, *refs),
-                [(FIELD, 128), edge, edge, (UP, 128), halo], spread, edges, halos, sent=(0,),
+                [(FIELD, 128), edge, (UP, 128), halo], spread, left, first_line, halos, scratch=stage, sent=(0,),
             )
             up = moved(up, "axial", 1, False)
             above = moved(above, "axial", -1, False)
-            left = moved(left, "span", 1, True)
         else:
-            left = moved(last_line, "span", 1, True)
             term, right = call(
                 lambda *refs: late_time_kernel(weights, *refs), [(FIELD, 128), edge], spread, left, first_line,
-                sent=(0,),
+                scratch=stage, sent=(0,),
             )
         right = moved(right, "span", -1, True)
         time = exchange(term, "inst", INST)
         groups = FULL_GROUPS if first else VEC_GROUPS
         source, packed = call(
             local_kernel,
-            [(FIELD + 2 * VARS * 8, 128), (SEGMENTS * groups, 128)],
+            [(KEPT * 8 + (UP + halo[0] if first else 0), 128), (SEGMENTS * groups, 128)],
             time, u, lines, left, right, *((up, above, packed_maps) if first else ()),
-            scratch=[(FIELD, 128)] + ([pltpu.SemaphoreType.DMA] if first else []), far=1 if first else 0,
+            scratch=[(FIELD, 128)] + ([pltpu.SemaphoreType.DMA((4,))] if first else []), far=1 if first else 0,
         )
         recv = exchange(packed, "axial", SEGMENTS)
         if first:
@@ -554,12 +582,13 @@
         common = (back_recv, u, source, lines)
         if last:
             (result,) = call(
-                lambda *refs: finish_kernel(True, *refs), [raw_field], *common, scratch=[(FIELD, 128)],
+                lambda *refs: finish_kernel(True, *refs), [raw_field], *common,
+                scratch=[(FIELD, 128), raw_field, pltpu.SemaphoreType.DMA((VARS,))], sent=(0,),
             )
         else:
             sent, last_line, first_line, u = call(
                 lambda *refs: finish_kernel(False, *refs), [(FIELD, 128), edge, edge, (FIELD + 2 * halo[0], 128)],
-                *common, above, up, scratch=[(UP, 128), pltpu.SemaphoreType.DMA], far=1, sent=(0,),
+                *common, scratch=[pltpu.SemaphoreType.DMA((STEPS,))], sent=(0,),
             )
     return result.transpose(1, 0, 2)[None]
 

time: 127 us -> 125 us (0.984)
  waiting for transfers between devices: 14.3 us -> 10.7 us
  starting transfers between devices: 46.3 us -> 48.6 us
    all_to_all x4, waiting for transfers between devices: 10.2 us -> 6.58 us  [exchange(): lax.all_to_all(value.reshape(count, shape[0] // count, 128), axis, 0, 0)]
    all_to_all x4, starting transfers between devices: 24.7 us -> 27.9 us  [exchange(): lax.all_to_all(value.reshape(count, shape[0] // count, 128), axis, 0, 0)]
    pallas_call x9 -> x10, Pallas kernels: 11.5 us -> 11.2 us  [call(): pl.pallas_call(kernel, out_shape=outs, in_specs=specs, out_specs=[pl.Bloc...]
  transfers between devices with their start and end apart: 10 -> 10, of which waited for: 6 -> 6; matrix products, arithmetic and copies ran while one was open for 0% -> 0% of each run, Pallas kernels for 3% -> 4%
where the time goes in v8:
time: 125 us; the launch traced here: 124 us
  blocking collectives  53.7 us (43%)
  starting transfers between devices  48.6 us (39%)
  Pallas kernels  11.2 us (9%)
  waiting for transfers between devices  10.7 us (9%)
    all_to_all x4, blocking collectives, exchange(): lax.all_to_all(value.reshape(count, shape[0] // count, 128), axis, 0, 0)  53.7 us
    all_to_all x4, starting transfers between devices, exchange(): lax.all_to_all(value.reshape(count, shape[0] // count, 128), axis, 0, 0)  27.9 us
    ppermute x6, starting transfers between devices, moved(): return lax.ppermute(value, axis, pairs)  20.7 us
    pallas_call x10, Pallas kernels, call(): pl.pallas_call(kernel, out_shape=outs, in_specs=specs, out_specs=[pl.Bloc...  11.2 us
    all_to_all x4, waiting for transfers between devices, exchange(): lax.all_to_all(value.reshape(count, shape[0] // count, 128), axis, 0, 0)  6.58 us
    ppermute x6, waiting for transfers between devices, moved(): return lax.ppermute(value, axis, pairs)  4.16 us
  transfers between devices with their start and end apart: 10, of which 6 were waited for; matrix products, arithmetic and copies ran while one was open for 0% of the time, Pallas kernels for 4%

profile of v8, /device:TPU:1, one launch (start us, length us, event | category | flops | bytes accessed | tf_op | source)
XLA Modules:
  0.0 124.4 jit_solution(16456445864211318939)
XLA Ops:
  0.0 10.9 %all-to-all-start = ((f32[8,40,128]{2,1,0:T(8,128)}), f32[8,40,128]{2,1,0:T(8,128)S(1)}, u32[]{:S(2)}, u32[]{:S(2)}) async-start(f32[8,40,128]{2,1,0:T(8,128)} %bitcast.55), calls=%async_computation | async-start | bytes 327680 | tf_op jit(solution)/shard_map/all_to_all | solution.py:509
  10.9 1.1 shard_map.64
  11.9 3.1 %collective-permute-start = (f32[8,128]{1,0:T(8,128)S(1)}, f32[8,128]{1,0:T(8,128)S(1)}, u32[]{:S(2)}, u32[]{:S(2)}) collective-permute-start(f32[8,128]{1,0:T(8,128)S(1)} %get-tuple-element.25), channel_id=1, source_target_pairs={{0,1},{1,2},{2,3},{3,0},{4,5},{5,6},{6,7},{7,4},{8,9},{9,10},{10,1... | collective-permute-start | bytes 12296 | tf_op jit(solution)/shard_map/ppermute | solution.py:516
  15.1 3.7 %shard_map.65 = (f32[184,128]{1,0:T(8,128)S(1)}, f32[5720,128]{1,0:T(8,128)S(1)}, f32[384,128]{1,0:T(8,128)}) custom-call(f32[320,128]{1,0:T(8,128)S(1)} %get-tuple-element.27.u_ref.refs_1_, f32[5,5,16,512]{3,2,1,0:T(8,128)} %bitcast.52, f32[5,5,16,512]{3,2,1,0:T(8,128)} %bitcast.53, f32[5,5,16,512]{3,2,1,0:T(8,128)} %bitcast.54, f32[5,16,512]{2,1,0:T(8,128)} %bitcast.57, ...), custom_call_target="tpu_custom_call" | custom-call | flops 8000000 | bytes 6037504 | tf_op jit(solution)/shard_map/pallas_call | solution.py:496
  18.8 0.3 all-to-all-done
  19.0 0.8 shard_map.66
  19.8 6.4 %all-to-all-start.1 = ((f32[8,40,128]{2,1,0:T(8,128)}), f32[8,40,128]{2,1,0:T(8,128)S(1)}, u32[]{:S(2)}, u32[]{:S(2)}) async-start(f32[8,40,128]{2,1,0:T(8,128)} %bitcast.58), calls=%async_computation.1 | async-start | bytes 327680 | tf_op jit(solution)/shard_map/all_to_all | solution.py:509
  26.2 4.9 %collective-permute-start.2 = (f32[144,128]{1,0:T(8,128)S(1)}, f32[144,128]{1,0:T(8,128)S(1)}, u32[]{:S(2)}, u32[]{:S(2)}) collective-permute-start(f32[144,128]{1,0:T(8,128)S(1)} %get-tuple-element.32), channel_id=1, source_target_pairs={{0,4},{4,8},{8,12},{12,16},{16,20},{20,24},{24,28},{28,32},{32,36}... | collective-permute-start | bytes 221192 | tf_op jit(solution)/shard_map/ppermute | solution.py:516
  31.1 1.9 %collective-permute-start.3 = (f32[40,128]{1,0:T(8,128)S(1)}, f32[40,128]{1,0:T(8,128)S(1)}, u32[]{:S(2)}, u32[]{:S(2)}) collective-permute-start(f32[40,128]{1,0:T(8,128)S(1)} %get-tuple-element.33), channel_id=1, source_target_pairs={{4,0},{8,4},{12,8},{16,12},{20,16},{24,20},{28,24},{32,28},{36,32}... | collective-permute-start | bytes 61448 | tf_op jit(solution)/shard_map/ppermute | solution.py:516
  33.0 3.4 %collective-permute-start.1 = (f32[8,128]{1,0:T(8,128)S(1)}, f32[8,128]{1,0:T(8,128)S(1)}, u32[]{:S(2)}, u32[]{:S(2)}) collective-permute-start(f32[8,128]{1,0:T(8,128)S(1)} %get-tuple-element.31), channel_id=1, source_target_pairs={{0,3},{1,0},{2,1},{3,2},{4,7},{5,4},{6,5},{7,6},{8,11},{9,8},{10,9... | collective-permute-start | bytes 12296 | tf_op jit(solution)/shard_map/ppermute | solution.py:516
  36.4 1.0 collective-permute-done.1.right_ref
  37.4 0.0 collective-permute-done.3.rest_1_
  37.4 0.0 collective-permute-done.2.rest_0_
  37.4 1.2 shard_map.67
  38.6 20.1 %all_to_all.40 = f32[16,24,128]{2,1,0:T(8,128)S(1)} all-to-all(f32[16,24,128]{2,1,0:T(8,128)S(1)} %bitcast.45), channel_id=1, replica_groups=mesh['inst'=8,'axial'=16,'span'=4] {'axial'}, dimensions={0} | all-to-all | bytes 393216 | tf_op jit(solution)/shard_map/all_to_all | solution.py:509
  58.7 0.7 shard_map.68
  59.4 10.1 %all_to_all.41 = f32[16,4,128]{2,1,0:T(4,128)S(1)} all-to-all(f32[16,4,128]{2,1,0:T(4,128)S(1)} %bitcast.47), channel_id=1, replica_groups=mesh['inst'=8,'axial'=16,'span'=4] {'axial'}, dimensions={0} | all-to-all | bytes 65536 | tf_op jit(solution)/shard_map/all_to_all | solution.py:509
  69.4 0.9 shard_map.69
  70.4 6.9 %all-to-all-start.4 = ((f32[8,40,128]{2,1,0:T(8,128)}), f32[8,40,128]{2,1,0:T(8,128)S(1)}, u32[]{:S(2)}, u32[]{:S(2)}) async-start(f32[8,40,128]{2,1,0:T(8,128)} %bitcast.59), calls=%async_computation.4 | async-start | bytes 327680 | tf_op jit(solution)/shard_map/all_to_all | solution.py:509
  77.3 3.1 %collective-permute-start.4 = (f32[8,128]{1,0:T(8,128)S(1)}, f32[8,128]{1,0:T(8,128)S(1)}, u32[]{:S(2)}, u32[]{:S(2)}) collective-permute-start(f32[8,128]{1,0:T(8,128)S(1)} %get-tuple-element.38), channel_id=1, source_target_pairs={{0,1},{1,2},{2,3},{3,0},{4,5},{5,6},{6,7},{7,4},{8,9},{9,10},{10,1... | collective-permute-start | bytes 12296 | tf_op jit(solution)/shard_map/ppermute | solution.py:516
  80.4 2.4 %collective-permute-done.4.refs_1_.left_ref = f32[8,128]{1,0:T(8,128)S(1)} collective-permute-done((f32[8,128]{1,0:T(8,128)S(1)}, f32[8,128]{1,0:T(8,128)S(1)}, u32[]{:S(2)}, u32[]{:S(2)}) %collective-permute-start.4) | collective-permute-done | bytes 4128 | tf_op jit(solution)/shard_map/ppermute | solution.py:516
  82.9 3.0 %all-to-all-done.4 = f32[8,40,128]{2,1,0:T(8,128)S(1)} async-done(((f32[8,40,128]{2,1,0:T(8,128)}), f32[8,40,128]{2,1,0:T(8,128)S(1)}, u32[]{:S(2)}, u32[]{:S(2)}) %all-to-all-start.4) | async-done | bytes 163872 | tf_op jit(solution)/shard_map/all_to_all | solution.py:509
  85.9 0.8 shard_map.70
  86.6 3.6 %all-to-all-start.5 = ((f32[8,40,128]{2,1,0:T(8,128)}), f32[8,40,128]{2,1,0:T(8,128)S(1)}, u32[]{:S(2)}, u32[]{:S(2)}) async-start(f32[8,40,128]{2,1,0:T(8,128)} %bitcast.60), calls=%async_computation.5 | async-start | bytes 327680 | tf_op jit(solution)/shard_map/all_to_all | solution.py:509
  90.3 4.3 %collective-permute-start.5 = (f32[8,128]{1,0:T(8,128)S(1)}, f32[8,128]{1,0:T(8,128)S(1)}, u32[]{:S(2)}, u32[]{:S(2)}) collective-permute-start(f32[8,128]{1,0:T(8,128)S(1)} %get-tuple-element.42), channel_id=1, source_target_pairs={{0,3},{1,0},{2,1},{3,2},{4,7},{5,4},{6,5},{7,6},{8,11},{9,8},{10,9... | collective-permute-start | bytes 12296 | tf_op jit(solution)/shard_map/ppermute | solution.py:516
  94.6 0.7 collective-permute-done.5.right_ref
  95.4 3.3 %all-to-all-done.5 = f32[8,40,128]{2,1,0:T(8,128)S(1)} async-done(((f32[8,40,128]{2,1,0:T(8,128)}), f32[8,40,128]{2,1,0:T(8,128)S(1)}, u32[]{:S(2)}, u32[]{:S(2)}) %all-to-all-start.5) | async-done | bytes 163872 | tf_op jit(solution)/shard_map/all_to_all | solution.py:509
  98.7 0.6 shard_map.71
  99.2 13.3 %all_to_all.42 = f32[16,4,128]{2,1,0:T(4,128)S(1)} all-to-all(f32[16,4,128]{2,1,0:T(4,128)S(1)} %bitcast.51), channel_id=1, replica_groups=mesh['inst'=8,'axial'=16,'span'=4] {'axial'}, dimensions={0} | all-to-all | bytes 65536 | tf_op jit(solution)/shard_map/all_to_all | solution.py:509
  112.5 0.7 shard_map.72
  113.2 10.3 %all_to_all.43 = f32[16,4,128]{2,1,0:T(4,128)S(1)} all-to-all(f32[16,4,128]{2,1,0:T(4,128)S(1)} %bitcast.49), channel_id=1, replica_groups=mesh['inst'=8,'axial'=16,'span'=4] {'axial'}, dimensions={0} | all-to-all | bytes 65536 | tf_op jit(solution)/shard_map/all_to_all | solution.py:509
  123.5 1.0 shard_map.73
  (2 shorter events, 0.0 us)
Async XLA Ops:
  0.0 19.0 %all-to-all-start = ((f32[8,40,128]{2,1,0:T(8,128)}), f32[8,40,128]{2,1,0:T(8,128)S(1)}, u32[]{:S(2)}, u32[]{:S(2)}) async-start(f32[8,40,128]{2,1,0:T(8,128)} %bitcast.55), calls=%async_computation | async-start | bytes 327680 | tf_op jit(solution)/shard_map/all_to_all | solution.py:509
  11.9 6.8 %collective-permute-start = (f32[8,128]{1,0:T(8,128)S(1)}, f32[8,128]{1,0:T(8,128)S(1)}, u32[]{:S(2)}, u32[]{:S(2)}) collective-permute-start(f32[8,128]{1,0:T(8,128)S(1)} %get-tuple-element.25), channel_id=1, source_target_pairs={{0,1},{1,2},{2,3},{3,0},{4,5},{5,6},{6,7},{7,4},{8,9},{9,10},{10,1... | collective-permute-start | bytes 12296 | tf_op jit(solution)/shard_map/ppermute | solution.py:516
  19.8 17.6 %all-to-all-start.1 = ((f32[8,40,128]{2,1,0:T(8,128)}), f32[8,40,128]{2,1,0:T(8,128)S(1)}, u32[]{:S(2)}, u32[]{:S(2)}) async-start(f32[8,40,128]{2,1,0:T(8,128)} %bitcast.58), calls=%async_computation.1 | async-start | bytes 327680 | tf_op jit(solution)/shard_map/all_to_all | solution.py:509
  26.2 11.2 %collective-permute-start.2 = (f32[144,128]{1,0:T(8,128)S(1)}, f32[144,128]{1,0:T(8,128)S(1)}, u32[]{:S(2)}, u32[]{:S(2)}) collective-permute-start(f32[144,128]{1,0:T(8,128)S(1)} %get-tuple-element.32), channel_id=1, source_target_pairs={{0,4},{4,8},{8,12},{12,16},{16,20},{20,24},{24,28},{28,32},{32,36}... | collective-permute-start | bytes 221192 | tf_op jit(solution)/shard_map/ppermute | solution.py:516
  31.1 6.3 %collective-permute-start.3 = (f32[40,128]{1,0:T(8,128)S(1)}, f32[40,128]{1,0:T(8,128)S(1)}, u32[]{:S(2)}, u32[]{:S(2)}) collective-permute-start(f32[40,128]{1,0:T(8,128)S(1)} %get-tuple-element.33), channel_id=1, source_target_pairs={{4,0},{8,4},{12,8},{16,12},{20,16},{24,20},{28,24},{32,28},{36,32}... | collective-permute-start | bytes 61448 | tf_op jit(solution)/shard_map/ppermute | solution.py:516
  33.0 4.4 %collective-permute-start.1 = (f32[8,128]{1,0:T(8,128)S(1)}, f32[8,128]{1,0:T(8,128)S(1)}, u32[]{:S(2)}, u32[]{:S(2)}) collective-permute-start(f32[8,128]{1,0:T(8,128)S(1)} %get-tuple-element.31), channel_id=1, source_target_pairs={{0,3},{1,0},{2,1},{3,2},{4,7},{5,4},{6,5},{7,6},{8,11},{9,8},{10,9... | collective-permute-start | bytes 12296 | tf_op jit(solution)/shard_map/ppermute | solution.py:516
  70.4 15.5 %all-to-all-start.4 = ((f32[8,40,128]{2,1,0:T(8,128)}), f32[8,40,128]{2,1,0:T(8,128)S(1)}, u32[]{:S(2)}, u32[]{:S(2)}) async-start(f32[8,40,128]{2,1,0:T(8,128)} %bitcast.59), calls=%async_computation.4 | async-start | bytes 327680 | tf_op jit(solution)/shard_map/all_to_all | solution.py:509
  77.3 5.6 %collective-permute-start.4 = (f32[8,128]{1,0:T(8,128)S(1)}, f32[8,128]{1,0:T(8,128)S(1)}, u32[]{:S(2)}, u32[]{:S(2)}) collective-permute-start(f32[8,128]{1,0:T(8,128)S(1)} %get-tuple-element.38), channel_id=1, source_target_pairs={{0,1},{1,2},{2,3},{3,0},{4,5},{5,6},{6,7},{7,4},{8,9},{9,10},{10,1... | collective-permute-start | bytes 12296 | tf_op jit(solution)/shard_map/ppermute | solution.py:516
  86.6 12.0 %all-to-all-start.5 = ((f32[8,40,128]{2,1,0:T(8,128)}), f32[8,40,128]{2,1,0:T(8,128)S(1)}, u32[]{:S(2)}, u32[]{:S(2)}) async-start(f32[8,40,128]{2,1,0:T(8,128)} %bitcast.60), calls=%async_computation.5 | async-start | bytes 327680 | tf_op jit(solution)/shard_map/all_to_all | solution.py:509
  90.3 5.1 %collective-permute-start.5 = (f32[8,128]{1,0:T(8,128)S(1)}, f32[8,128]{1,0:T(8,128)S(1)}, u32[]{:S(2)}, u32[]{:S(2)}) collective-permute-start(f32[8,128]{1,0:T(8,128)S(1)} %get-tuple-element.42), channel_id=1, source_target_pairs={{0,3},{1,0},{2,1},{3,2},{4,7},{5,4},{6,5},{7,6},{8,11},{9,8},{10,9... | collective-permute-start | bytes 12296 | tf_op jit(solution)/shard_map/ppermute | solution.py:516

commit v9 on v8

--- a/solution.py
+++ b/solution.py
@@ -20,8 +20,8 @@
 SIZE = VARS * VARS
 FULL_GROUPS = 24
 VEC_GROUPS = 4
-PACKED = 2 * MATRIX + 3 * SIZE * 8
-PIVOT = PACKED
+CHAIN = 2 * MATRIX
+PIVOT = 3 * SIZE * 8
 CELLS = PIVOT + MATRIX
 LINES = CELLS + FIELD
 UP = VARS * 8 + (SIZE + 1) // 2 * 8
@@ -69,12 +69,30 @@
     return [total(m[i * VARS + j] * v[j] for j in range(VARS)) for i in range(VARS)]
 
 
+def step_minus(source, m, v):
+    out = []
+    for i in range(VARS):
+        t = [m[i * VARS + j] * v[j] for j in range(VARS)]
+        out.append(((source[i] - t[0]) - (t[1] + t[2])) - (t[3] + t[4]))
+    return out
+
+
+def step_plus(source, m, v):
+    out = []
+    for i in range(VARS):
+        t = [m[i * VARS + j] * v[j] for j in range(VARS)]
+        out.append(((source[i] + t[0]) + (t[1] + t[2])) + (t[3] + t[4]))
+    return out
+
+
 def matmul(a, b):
-    return [
-        total(a[i * VARS + j] * b[j * VARS + m] for j in range(VARS))
-        for i in range(VARS)
-        for m in range(VARS)
-    ]
+    out = [None] * SIZE
+    for m in range(VARS):
+        column = [b[j * VARS + m] for j in range(VARS)]
+        for i in range(VARS):
+            t = [a[i * VARS + j] * column[j] for j in range(VARS)]
+            out[i * VARS + m] = (t[0] + t[1]) + (t[2] + t[3]) + t[4]
+    return out
 
 
 def plus(a, b):
@@ -160,11 +178,27 @@
         copy.wait()
 
 
-def pack_kernel(state_hbm, u_ref, last_ref, first_ref, state_ref, sems):
+def pack_kernel(
+    state_hbm, coupling_hbm, back_hbm, u_ref, last_ref, first_ref, chain_ref, up_ref, down_ref,
+    state_ref, coupling_raw, back_raw, sems,
+):
     sub, lane = iotas()
-    arrive(fetch(state_hbm, state_ref, sems, 0))
+    state_copies = fetch(state_hbm, state_ref, sems, 0)
+    coupling_copies = fetch(coupling_hbm, coupling_raw, sems, VARS)
+    back_copies = fetch(back_hbm, back_raw, sems, 2 * VARS)
+    arrive(state_copies)
     field_to_packed(state_ref, u_ref)
     edge_lines(sub, lane, rows(u_ref, 0, STEPS * VARS), last_ref, first_ref)
+    arrive(coupling_copies)
+    matrix_to_packed(coupling_raw, chain_ref, 0)
+    arrive(back_copies)
+    matrix_to_packed(back_raw, chain_ref, MATRIX)
+    up_ref[: VARS * 8, :] = u_ref[(STEPS - 1) * VARS * 8 :, :]
+    blocks = rows(chain_ref, (2 * STEPS - 1) * SIZE, SIZE)
+    for n in range(0, SIZE, 2):
+        pair = jnp.where(sub < TILES, pltpu.roll(blocks[n], 4, 0), blocks[min(n + 1, SIZE - 1)])
+        put(up_ref, VARS + n // 2, pair)
+    down_ref[...] = u_ref[: VARS * 8, :]
 
 
 def piece_out(stage_ref, out_hbm, sems, index, count):
@@ -184,46 +218,31 @@
     return copies
 
 
-def time_kernel(
-    weights, spread_ref, left_ref, line_ref, halos_ref,
-    out_hbm, first_ref, up_ref, down_ref, stage_ref, sems,
-):
+def time_kernel(weights, count, spread_ref, *rest):
+    out_hbm, *passed_refs, stage_ref, sems = rest[-3 - count :]
     copies = time_term(weights, spread_ref, out_hbm, stage_ref, sems)
-    first_ref[...] = line_ref[...]
-    up_ref[...] = halos_ref[:UP, :]
-    down_ref[...] = halos_ref[UP:, :]
+    for line_ref, passed_ref in zip(rest, passed_refs):
+        passed_ref[...] = line_ref[...]
     arrive(copies)
 
 
-def late_time_kernel(weights, spread_ref, left_ref, line_ref, out_hbm, first_ref, stage_ref, sems):
-    copies = time_term(weights, spread_ref, out_hbm, stage_ref, sems)
-    first_ref[...] = line_ref[...]
-    arrive(copies)
-
-
 def maps_kernel(
-    u_ref, coupling_hbm, back_hbm, pivot_hbm, source_hbm, flags_hbm,
-    halos_ref, lines_ref, packed_hbm,
-    prefix_ref, keep_ref, coupling_raw, back_raw, pivot_raw, source_raw, flags_ref, packed_ref, sems,
+    chain_ref, after_ref, pivot_hbm, source_hbm, flags_hbm,
+    lines_ref, packed_hbm,
+    prefix_ref, keep_ref, pivot_raw, source_raw, flags_ref, packed_ref, sems,
 ):
     sub, lane = iotas()
     block = lane // 32
-    coupling_copies = fetch(coupling_hbm, coupling_raw, sems, 0)
-    back_copies = fetch(back_hbm, back_raw, sems, VARS)
-    pivot_copies = fetch(pivot_hbm, pivot_raw, sems, 2 * VARS)
-    source_copies = fetch(source_hbm, source_raw, sems, 3 * VARS)
-    flags_copy = pltpu.make_async_copy(flags_hbm, flags_ref, sems.at[4 * VARS])
+    pivot_copies = fetch(pivot_hbm, pivot_raw, sems, 0)
+    source_copies = fetch(source_hbm, source_raw, sems, VARS)
+    flags_copy = pltpu.make_async_copy(flags_hbm, flags_ref, sems.at[2 * VARS])
     flags_copy.start()
     top = sub < TILES
-    arrive(coupling_copies)
-    matrix_to_packed(coupling_raw, lines_ref, 0)
-    arrive(back_copies)
-    matrix_to_packed(back_raw, lines_ref, MATRIX)
     def coupling(k):
-        return rows(lines_ref, k * SIZE, SIZE)
+        return rows(chain_ref, k * SIZE, SIZE)
 
     def back(k):
-        return rows(lines_ref, STEPS * SIZE + k * SIZE, SIZE)
+        return rows(chain_ref, STEPS * SIZE + k * SIZE, SIZE)
 
     def forward(k, p):
         p = [-x for x in matmul(coupling(k), p)]
@@ -246,11 +265,10 @@
         return [-x for x in matmul(back(STEPS - 2 - step), carry)]
 
     behind = lax.fori_loop(0, STEPS - 1, behind_step, [-x for x in back(STEPS - 1)])
-    base = 2 * STEPS * SIZE
     for n in range(SIZE):
-        put(lines_ref, base + n, ahead[n])
-        put(lines_ref, base + SIZE + n, mixed[n])
-        put(lines_ref, base + 2 * SIZE + n, behind[n])
+        put(lines_ref, n, ahead[n])
+        put(lines_ref, SIZE + n, mixed[n])
+        put(lines_ref, 2 * SIZE + n, behind[n])
     whole = matmul(swap(ahead), ahead)
     for n in range(SIZE):
         put(prefix_ref, n, whole[n])
@@ -261,7 +279,7 @@
     for n in range(SIZE):
         put(prefix_ref, 2 * SIZE + n, whole[n])
     pack_lines(packed_ref, 0, block, rows(prefix_ref, 0, 3 * SIZE), VEC_GROUPS, FULL_GROUPS)
-    packed_copy = pltpu.make_async_copy(packed_ref, packed_hbm, sems.at[4 * VARS + 1])
+    packed_copy = pltpu.make_async_copy(packed_ref, packed_hbm, sems.at[2 * VARS + 1])
     packed_copy.start()
     arrive(pivot_copies)
     matrix_to_packed(pivot_raw, lines_ref, PIVOT)
@@ -280,12 +298,6 @@
         return carry
 
     lax.fori_loop(0, STEPS, mask, 0)
-    halos_ref[: VARS * 8, :] = u_ref[(STEPS - 1) * VARS * 8 :, :]
-    last = back(STEPS - 1)
-    for n in range(0, SIZE, 2):
-        pair = jnp.where(top, pltpu.roll(last[n], 4, 0), last[min(n + 1, SIZE - 1)])
-        put(halos_ref, VARS + n // 2, pair)
-    halos_ref[UP:, :] = u_ref[: VARS * 8, :]
     packed_copy.wait()
 
 
@@ -317,7 +329,7 @@
             put(out_ref, n, value + row(time_ref, n))
 
 
-def local_kernel(time_ref, u_ref, lines_ref, left_ref, right_ref, *rest):
+def local_kernel(time_ref, u_ref, chain_ref, lines_ref, left_ref, right_ref, *rest):
     sub, lane = iotas()
     block = lane // 32
     if len(rest) > 3:
@@ -348,19 +360,18 @@
     y = rows(source_ref, 0, VARS)
     kept = [y]
     for k in range(1, STEPS):
-        y = minus(rows(source_ref, k * VARS, VARS), matvec(rows(lines_ref, k * SIZE, SIZE), y))
+        y = step_minus(rows(source_ref, k * VARS, VARS), rows(chain_ref, k * SIZE, SIZE), y)
         kept.append(y)
     end = y
     x = y
     for k in range(STEPS - 2, -1, -1):
-        x = minus(kept[k], matvec(rows(lines_ref, (STEPS + k) * SIZE, SIZE), x))
+        x = step_minus(kept[k], rows(chain_ref, (STEPS + k) * SIZE, SIZE), x)
     for v in range(VARS):
         put(source_ref, STEPS * VARS + v, end[v])
         put(source_ref, STEPS * VARS + VARS + v, x[v])
-    base = 2 * STEPS * SIZE
-    ahead = rows(lines_ref, base, SIZE)
-    mixed = rows(lines_ref, base + SIZE, SIZE)
-    behind = rows(lines_ref, base + 2 * SIZE, SIZE)
+    ahead = rows(lines_ref, 0, SIZE)
+    mixed = rows(lines_ref, SIZE, SIZE)
+    behind = rows(lines_ref, 2 * SIZE, SIZE)
     whole_end = plus(swap(end), matvec(swap(ahead), end))
     inner = plus(swap(x), matvec(swap(mixed), end))
     whole_first = plus(x, matvec(behind, inner))
@@ -400,9 +411,9 @@
         maps = rows(maps_ref, part * 3 * SIZE + which * SIZE, SIZE)
 
         def step(_, now):
-            return plus(source, matvec(maps, shift(sub, now, entry)))
-
-        out = lax.fori_loop(0, 7, step, plus(source, matvec(maps, shift(sub, zero, entry))))
+            return step_plus(source, maps, shift(sub, now, entry))
+
+        out = lax.fori_loop(0, 7, step, step_plus(source, maps, shift(sub, zero, entry)))
         return out, shift(sub, out, entry)
 
     ends = [[value(r, part) for r in range(VARS)] for part in range(2)]
@@ -423,7 +434,7 @@
             out_ref[pl.ds(part * 8 * VEC_GROUPS + g, 8, stride=VEC_GROUPS), :] = packed
 
 
-def finish_kernel(last, recv_ref, u_ref, source_ref, lines_ref, *rest):
+def finish_kernel(last, recv_ref, u_ref, source_ref, chain_ref, lines_ref, *rest):
     if last:
         out_hbm, new_ref, out_ref, sems = rest
     else:
@@ -446,24 +457,23 @@
 
     entry = [value(r) for r in range(VARS)]
     after = [value(VARS + r) for r in range(VARS)]
-    base = 2 * STEPS * SIZE
     end = rows(source_ref, STEPS * VARS, VARS)
     begin = rows(source_ref, STEPS * VARS + VARS, VARS)
-    middle = plus(end, matvec(rows(lines_ref, base, SIZE), entry))
+    middle = plus(end, matvec(rows(lines_ref, 0, SIZE), entry))
     start = pick(top, entry, swap(middle))
     follow = plus(
-        plus(begin, matvec(rows(lines_ref, base + SIZE, SIZE), start)),
-        matvec(rows(lines_ref, base + 2 * SIZE, SIZE), after),
+        plus(begin, matvec(rows(lines_ref, SIZE, SIZE), start)),
+        matvec(rows(lines_ref, 2 * SIZE, SIZE), after),
     )
     finish = pick(top, swap(follow), after)
     y = start
     kept = []
     for k in range(STEPS):
-        y = minus(rows(source_ref, k * VARS, VARS), matvec(rows(lines_ref, k * SIZE, SIZE), y))
+        y = step_minus(rows(source_ref, k * VARS, VARS), rows(chain_ref, k * SIZE, SIZE), y)
         kept.append(y)
     x = finish
     for k in range(STEPS - 1, -1, -1):
-        x = minus(kept[k], matvec(rows(lines_ref, (STEPS + k) * SIZE, SIZE), x))
+        x = step_minus(kept[k], rows(chain_ref, (STEPS + k) * SIZE, SIZE), x)
         for v in range(VARS):
             put(new_ref, k * VARS + v, row(u_ref, k * VARS + v) + x[v])
         if not last:
@@ -524,42 +534,45 @@
     raw_matrix = (VARS,) + raw_field
     cells_first = state[0].transpose(1, 0, 2)
     sent = cells_first.reshape(VARS, 2, STEPS, TILES, 128).transpose(0, 1, 3, 2, 4).reshape(FIELD, 128)
-    u, last_line, first_line = call(
-        pack_kernel, [(FIELD, 128), edge, edge], cells_first,
-        scratch=[raw_field, pltpu.SemaphoreType.DMA((VARS,))], far=1,
+    u, last_line, first_line, chain, up, above = call(
+        pack_kernel, [(FIELD, 128), edge, edge, (CHAIN, 128), (UP, 128), halo],
+        cells_first, coupling[0].transpose(1, 2, 0, 3), back_coupling[0].transpose(1, 2, 0, 3),
+        scratch=[raw_field, raw_matrix, raw_matrix, pltpu.SemaphoreType.DMA((3 * VARS,))], far=3,
+        limit=12,
     )
-    halos, lines, packed_maps = call(
-        maps_kernel,
-        [(UP + halo[0], 128), (LINES, 128), (SEGMENTS * FULL_GROUPS, 128)],
-        u, coupling[0].transpose(1, 2, 0, 3), back_coupling[0].transpose(1, 2, 0, 3),
-        pivot_inverse[0].transpose(1, 2, 0, 3), source_terms[0].transpose(1, 0, 2), wall_flags,
-        scratch=[
-            (MATRIX, 128), (STEPS * 8, 128), raw_matrix, raw_matrix, raw_matrix, raw_field,
-            pltpu.VMEM((2 * STEPS, TILES * 128), jnp.int32), (SEGMENTS * FULL_GROUPS, 128),
-            pltpu.SemaphoreType.DMA((4 * VARS + 2,)),
-        ],
-        flops=8_000_000,
-        limit=16,
-        far=5,
-        sent=(2,),
-    )
+    up = moved(up, "axial", 1, False)
+    above = moved(above, "axial", -1, False)
     stage = [(FIELD, 128), pltpu.SemaphoreType.DMA((INST,))]
     for sweep in range(SWEEPS):
         first = sweep == 0
         last = sweep == SWEEPS - 1
         spread = exchange(sent, "inst", INST)
-        left = moved(last_line, "span", 1, True)
         if first:
-            term, right, up, above = call(
-                lambda *refs: time_kernel(weights, *refs),
-                [(FIELD, 128), edge, (UP, 128), halo], spread, left, first_line, halos, scratch=stage, sent=(0,),
+            term, right, left = call(
+                lambda *refs: time_kernel(weights, 2, *refs), [(FIELD, 128), edge, edge],
+                spread, first_line, last_line, up, above, scratch=stage, sent=(0,),
             )
-            up = moved(up, "axial", 1, False)
-            above = moved(above, "axial", -1, False)
+            left = moved(left, "span", 1, True)
         else:
+            left = moved(last_line, "span", 1, True)
             term, right = call(
-                lambda *refs: late_time_kernel(weights, *refs), [(FIELD, 128), edge], spread, left, first_line,
-                scratch=stage, sent=(0,),
+                lambda *refs: time_kernel(weights, 1, *refs), [(FIELD, 128), edge],
+                spread, first_line, left, scratch=stage, sent=(0,),
+            )
+        if first:
+            lines, packed_maps = call(
+                maps_kernel,
+                [(LINES, 128), (SEGMENTS * FULL_GROUPS, 128)],
+                chain, right, pivot_inverse[0].transpose(1, 2, 0, 3), source_terms[0].transpose(1, 0, 2), wall_flags,
+                scratch=[
+                    (MATRIX, 128), (STEPS * 8, 128), raw_matrix, raw_field,
+                    pltpu.VMEM((2 * STEPS, TILES * 128), jnp.int32), (SEGMENTS * FULL_GROUPS, 128),
+                    pltpu.SemaphoreType.DMA((2 * VARS + 2,)),
+                ],
+                flops=8_000_000,
+                limit=16,
+                far=3,
+                sent=(1,),
             )
         right = moved(right, "span", -1, True)
         time = exchange(term, "inst", INST)
@@ -567,7 +580,7 @@
         source, packed = call(
             local_kernel,
             [(KEPT * 8 + (UP + halo[0] if first else 0), 128), (SEGMENTS * groups, 128)],
-            time, u, lines, left, right, *((up, above, packed_maps) if first else ()),
+            time, u, chain, lines, left, right, *((up, above, packed_maps) if first else ()),
             scratch=[(FIELD, 128)] + ([pltpu.SemaphoreType.DMA((4,))] if first else []), far=1 if first else 0,
         )
         recv = exchange(packed, "axial", SEGMENTS)
@@ -579,7 +592,7 @@
             scratch=[(6 * SIZE * 8, 128)],
         )
         back_recv = exchange(solved, "axial", SEGMENTS)
-        common = (back_recv, u, source, lines)
+        common = (back_recv, u, source, chain, lines)
         if last:
             (result,) = call(
                 lambda *refs: finish_kernel(True, *refs), [raw_field], *common,

time: 125 us -> 124 us (level)
  waiting for transfers between devices: 10.7 us -> 13.3 us
  blocking collectives: 53.7 us -> 51.9 us
    ppermute x6, waiting for transfers between devices: 4.16 us -> 6.55 us  [moved(): return lax.ppermute(value, axis, pairs)]
    all_to_all x4, blocking collectives: 53.7 us -> 51.9 us  [exchange(): lax.all_to_all(value.reshape(count, shape[0] // count, 128), axis, 0, 0)]
  transfers between devices with their start and end apart: 10 -> 10, of which waited for: 6 -> 6; matrix products, arithmetic and copies ran while one was open for 0% -> 0% of each run, Pallas kernels for 4% -> 3%
where the time goes in v9:
time: 124 us; the launch traced here: 123 us
  blocking collectives  51.9 us (42%)
  starting transfers between devices  47.5 us (38%)
  waiting for transfers between devices  13.3 us (11%)
  Pallas kernels  10.2 us (8%)
    all_to_all x4, blocking collectives, exchange(): lax.all_to_all(value.reshape(count, shape[0] // count, 128), axis, 0, 0)  51.9 us
    all_to_all x4, starting transfers between devices, exchange(): lax.all_to_all(value.reshape(count, shape[0] // count, 128), axis, 0, 0)  28 us
    ppermute x6, starting transfers between devices, moved(): return lax.ppermute(value, axis, pairs)  19.5 us
    pallas_call x10, Pallas kernels, call(): pl.pallas_call(kernel, out_shape=outs, in_specs=specs, out_specs=[pl.Bloc...  10.2 us
    all_to_all x4, waiting for transfers between devices, exchange(): lax.all_to_all(value.reshape(count, shape[0] // count, 128), axis, 0, 0)  6.77 us
    ppermute x6, waiting for transfers between devices, moved(): return lax.ppermute(value, axis, pairs)  6.55 us
  transfers between devices with their start and end apart: 10, of which 6 were waited for; matrix products, arithmetic and copies ran while one was open for 0% of the time, Pallas kernels for 3%

profile of v9, /device:TPU:1, one launch (start us, length us, event | category | flops | bytes accessed | tf_op | source)
XLA Modules:
  0.0 123.1 jit_solution(2995529847418147176)
XLA Ops:
  0.0 10.9 %all-to-all-start = ((f32[8,40,128]{2,1,0:T(8,128)}), f32[8,40,128]{2,1,0:T(8,128)S(1)}, u32[]{:S(2)}, u32[]{:S(2)}) async-start(f32[8,40,128]{2,1,0:T(8,128)} %bitcast.55), calls=%async_computation | async-start | bytes 327680 | tf_op jit(solution)/shard_map/all_to_all | solution.py:519
  10.9 1.8 %shard_map.64 = (f32[320,128]{1,0:T(8,128)S(1)}, f32[8,128]{1,0:T(8,128)S(1)}, f32[8,128]{1,0:T(8,128)S(1)}, f32[3200,128]{1,0:T(8,128)S(1)}, f32[144,128]{1,0:T(8,128)S(1)}, /*index=5*/f32[40,128]{1,0:T(8,128)S(1)}) custom-call(f32[5,16,512]{2,1,0:T(8,128)} %bitcast.56, f32[5,5,16,512]{3,2,1,0:T(8,128)} %bitcast.52, f32[5,5,16,512]{3,2,1,0:T(8,128)} %bitcast.53), custom_call_target="tpu_custom_call" | custom-call | flops 100000 | bytes 3706880 | tf_op jit(solution)/shard_map/pallas_call | solution.py:506
  12.7 4.0 %collective-permute-start = (f32[144,128]{1,0:T(8,128)S(1)}, f32[144,128]{1,0:T(8,128)S(1)}, u32[]{:S(2)}, u32[]{:S(2)}) collective-permute-start(f32[144,128]{1,0:T(8,128)S(1)} %get-tuple-element.28), channel_id=1, source_target_pairs={{0,4},{4,8},{8,12},{12,16},{16,20},{20,24},{24,28},{28,32},{32,36}... | collective-permute-start | bytes 221192 | tf_op jit(solution)/shard_map/ppermute | solution.py:526
  16.7 1.9 %collective-permute-start.1 = (f32[40,128]{1,0:T(8,128)S(1)}, f32[40,128]{1,0:T(8,128)S(1)}, u32[]{:S(2)}, u32[]{:S(2)}) collective-permute-start(f32[40,128]{1,0:T(8,128)S(1)} %get-tuple-element.29), channel_id=1, source_target_pairs={{4,0},{8,4},{12,8},{16,12},{20,16},{24,20},{28,24},{32,28},{36,32}... | collective-permute-start | bytes 61448 | tf_op jit(solution)/shard_map/ppermute | solution.py:526
  18.7 3.2 %collective-permute-done.1.refs_4_.rest_1_ = f32[40,128]{1,0:T(8,128)S(1)} collective-permute-done((f32[40,128]{1,0:T(8,128)S(1)}, f32[40,128]{1,0:T(8,128)S(1)}, u32[]{:S(2)}, u32[]{:S(2)}) %collective-permute-start.1) | collective-permute-done | bytes 20512 | tf_op jit(solution)/shard_map/ppermute | solution.py:526
  21.8 0.0 collective-permute-done.refs_3_.rest_0_
  21.8 0.0 all-to-all-done
  21.8 0.8 shard_map.65
  22.6 6.9 %all-to-all-start.1 = ((f32[8,40,128]{2,1,0:T(8,128)}), f32[8,40,128]{2,1,0:T(8,128)S(1)}, u32[]{:S(2)}, u32[]{:S(2)}) async-start(f32[8,40,128]{2,1,0:T(8,128)} %bitcast.57), calls=%async_computation.1 | async-start | bytes 327680 | tf_op jit(solution)/shard_map/all_to_all | solution.py:519
  29.6 3.1 %collective-permute-start.2 = (f32[8,128]{1,0:T(8,128)S(1)}, f32[8,128]{1,0:T(8,128)S(1)}, u32[]{:S(2)}, u32[]{:S(2)}) collective-permute-start(f32[8,128]{1,0:T(8,128)S(1)} %get-tuple-element.35), channel_id=1, source_target_pairs={{0,1},{1,2},{2,3},{3,0},{4,5},{5,6},{6,7},{7,4},{8,9},{9,10},{10,1... | collective-permute-start | bytes 12296 | tf_op jit(solution)/shard_map/ppermute | solution.py:526
  32.7 3.4 %collective-permute-start.3 = (f32[8,128]{1,0:T(8,128)S(1)}, f32[8,128]{1,0:T(8,128)S(1)}, u32[]{:S(2)}, u32[]{:S(2)}) collective-permute-start(f32[8,128]{1,0:T(8,128)S(1)} %get-tuple-element.33.after_ref), channel_id=1, source_target_pairs={{0,3},{1,0},{2,1},{3,2},{4,7},{5,4},{6,5},{7,6},{8,11},{9,8},{10,9... | collective-permute-start | bytes 12296 | tf_op jit(solution)/shard_map/ppermute | solution.py:526
  36.0 2.0 %shard_map.66 = (f32[2520,128]{1,0:T(8,128)S(1)}, f32[384,128]{1,0:T(8,128)}) custom-call(f32[3200,128]{1,0:T(8,128)S(1)} %get-tuple-element.32.chain_ref.refs_3_, f32[8,128]{1,0:T(8,128)S(1)} %get-tuple-element.33.after_ref, f32[5,5,16,512]{3,2,1,0:T(8,128)} %bitcast.54, f32[5,16,512]{2,1,0:T(8,128)} %bitcast.60, s32[16,512]{1,0:T(8,128)} %flags_hbm.1), custom_call_target="tpu_custom_call" | custom-call | flops 8000000 | bytes 4145152 | tf_op jit(solution)/shard_map/pallas_call | solution.py:506
  38.1 0.2 all-to-all-done.1
  38.3 1.2 shard_map.67
  39.5 18.3 %all_to_all.40 = f32[16,24,128]{2,1,0:T(8,128)S(1)} all-to-all(f32[16,24,128]{2,1,0:T(8,128)S(1)} %bitcast.45), channel_id=1, replica_groups=mesh['inst'=8,'axial'=16,'span'=4] {'axial'}, dimensions={0} | all-to-all | bytes 393216 | tf_op jit(solution)/shard_map/all_to_all | solution.py:519
  57.8 0.6 shard_map.68
  58.4 10.1 %all_to_all.41 = f32[16,4,128]{2,1,0:T(4,128)S(1)} all-to-all(f32[16,4,128]{2,1,0:T(4,128)S(1)} %bitcast.47), channel_id=1, replica_groups=mesh['inst'=8,'axial'=16,'span'=4] {'axial'}, dimensions={0} | all-to-all | bytes 65536 | tf_op jit(solution)/shard_map/all_to_all | solution.py:519
  68.5 0.9 shard_map.69
  69.4 6.5 %all-to-all-start.4 = ((f32[8,40,128]{2,1,0:T(8,128)}), f32[8,40,128]{2,1,0:T(8,128)S(1)}, u32[]{:S(2)}, u32[]{:S(2)}) async-start(f32[8,40,128]{2,1,0:T(8,128)} %bitcast.58), calls=%async_computation.4 | async-start | bytes 327680 | tf_op jit(solution)/shard_map/all_to_all | solution.py:519
  76.0 2.9 %collective-permute-start.4 = (f32[8,128]{1,0:T(8,128)S(1)}, f32[8,128]{1,0:T(8,128)S(1)}, u32[]{:S(2)}, u32[]{:S(2)}) collective-permute-start(f32[8,128]{1,0:T(8,128)S(1)} %get-tuple-element.41), channel_id=1, source_target_pairs={{0,1},{1,2},{2,3},{3,0},{4,5},{5,6},{6,7},{7,4},{8,9},{9,10},{10,1... | collective-permute-start | bytes 12296 | tf_op jit(solution)/shard_map/ppermute | solution.py:526
  78.9 2.6 %collective-permute-done.4.refs_2_.left_ref = f32[8,128]{1,0:T(8,128)S(1)} collective-permute-done((f32[8,128]{1,0:T(8,128)S(1)}, f32[8,128]{1,0:T(8,128)S(1)}, u32[]{:S(2)}, u32[]{:S(2)}) %collective-permute-start.4) | collective-permute-done | bytes 4128 | tf_op jit(solution)/shard_map/ppermute | solution.py:526
  81.5 3.0 %all-to-all-done.4 = f32[8,40,128]{2,1,0:T(8,128)S(1)} async-done(((f32[8,40,128]{2,1,0:T(8,128)}), f32[8,40,128]{2,1,0:T(8,128)S(1)}, u32[]{:S(2)}, u32[]{:S(2)}) %all-to-all-start.4) | async-done | bytes 163872 | tf_op jit(solution)/shard_map/all_to_all | solution.py:519
  84.6 0.8 shard_map.70
  85.3 3.6 %all-to-all-start.5 = ((f32[8,40,128]{2,1,0:T(8,128)}), f32[8,40,128]{2,1,0:T(8,128)S(1)}, u32[]{:S(2)}, u32[]{:S(2)}) async-start(f32[8,40,128]{2,1,0:T(8,128)} %bitcast.59), calls=%async_computation.5 | async-start | bytes 327680 | tf_op jit(solution)/shard_map/all_to_all | solution.py:519
  89.0 4.1 %collective-permute-start.5 = (f32[8,128]{1,0:T(8,128)S(1)}, f32[8,128]{1,0:T(8,128)S(1)}, u32[]{:S(2)}, u32[]{:S(2)}) collective-permute-start(f32[8,128]{1,0:T(8,128)S(1)} %get-tuple-element.44), channel_id=1, source_target_pairs={{0,3},{1,0},{2,1},{3,2},{4,7},{5,4},{6,5},{7,6},{8,11},{9,8},{10,9... | collective-permute-start | bytes 12296 | tf_op jit(solution)/shard_map/ppermute | solution.py:526
  93.1 0.7 collective-permute-done.5.right_ref
  93.9 3.5 %all-to-all-done.5 = f32[8,40,128]{2,1,0:T(8,128)S(1)} async-done(((f32[8,40,128]{2,1,0:T(8,128)}), f32[8,40,128]{2,1,0:T(8,128)S(1)}, u32[]{:S(2)}, u32[]{:S(2)}) %all-to-all-start.5) | async-done | bytes 163872 | tf_op jit(solution)/shard_map/all_to_all | solution.py:519
  97.3 0.6 shard_map.71
  97.9 13.3 %all_to_all.42 = f32[16,4,128]{2,1,0:T(4,128)S(1)} all-to-all(f32[16,4,128]{2,1,0:T(4,128)S(1)} %bitcast.51), channel_id=1, replica_groups=mesh['inst'=8,'axial'=16,'span'=4] {'axial'}, dimensions={0} | all-to-all | bytes 65536 | tf_op jit(solution)/shard_map/all_to_all | solution.py:519
  111.2 0.6 shard_map.72
  111.9 10.3 %all_to_all.43 = f32[16,4,128]{2,1,0:T(4,128)S(1)} all-to-all(f32[16,4,128]{2,1,0:T(4,128)S(1)} %bitcast.49), channel_id=1, replica_groups=mesh['inst'=8,'axial'=16,'span'=4] {'axial'}, dimensions={0} | all-to-all | bytes 65536 | tf_op jit(solution)/shard_map/all_to_all | solution.py:519
  122.1 0.9 shard_map.73
  (2 shorter events, 0.0 us)
Async XLA Ops:
  0.0 21.8 %all-to-all-start = ((f32[8,40,128]{2,1,0:T(8,128)}), f32[8,40,128]{2,1,0:T(8,128)S(1)}, u32[]{:S(2)}, u32[]{:S(2)}) async-start(f32[8,40,128]{2,1,0:T(8,128)} %bitcast.55), calls=%async_computation | async-start | bytes 327680 | tf_op jit(solution)/shard_map/all_to_all | solution.py:519
  12.7 9.2 %collective-permute-start = (f32[144,128]{1,0:T(8,128)S(1)}, f32[144,128]{1,0:T(8,128)S(1)}, u32[]{:S(2)}, u32[]{:S(2)}) collective-permute-start(f32[144,128]{1,0:T(8,128)S(1)} %get-tuple-element.28), channel_id=1, source_target_pairs={{0,4},{4,8},{8,12},{12,16},{16,20},{20,24},{24,28},{28,32},{32,36}... | collective-permute-start | bytes 221192 | tf_op jit(solution)/shard_map/ppermute | solution.py:526
  16.7 5.1 %collective-permute-start.1 = (f32[40,128]{1,0:T(8,128)S(1)}, f32[40,128]{1,0:T(8,128)S(1)}, u32[]{:S(2)}, u32[]{:S(2)}) collective-permute-start(f32[40,128]{1,0:T(8,128)S(1)} %get-tuple-element.29), channel_id=1, source_target_pairs={{4,0},{8,4},{12,8},{16,12},{20,16},{24,20},{28,24},{32,28},{36,32}... | collective-permute-start | bytes 61448 | tf_op jit(solution)/shard_map/ppermute | solution.py:526
  22.6 15.7 %all-to-all-start.1 = ((f32[8,40,128]{2,1,0:T(8,128)}), f32[8,40,128]{2,1,0:T(8,128)S(1)}, u32[]{:S(2)}, u32[]{:S(2)}) async-start(f32[8,40,128]{2,1,0:T(8,128)} %bitcast.57), calls=%async_computation.1 | async-start | bytes 327680 | tf_op jit(solution)/shard_map/all_to_all | solution.py:519
  29.6 8.5 %collective-permute-start.2 = (f32[8,128]{1,0:T(8,128)S(1)}, f32[8,128]{1,0:T(8,128)S(1)}, u32[]{:S(2)}, u32[]{:S(2)}) collective-permute-start(f32[8,128]{1,0:T(8,128)S(1)} %get-tuple-element.35), channel_id=1, source_target_pairs={{0,1},{1,2},{2,3},{3,0},{4,5},{5,6},{6,7},{7,4},{8,9},{9,10},{10,1... | collective-permute-start | bytes 12296 | tf_op jit(solution)/shard_map/ppermute | solution.py:526
  32.7 5.4 %collective-permute-start.3 = (f32[8,128]{1,0:T(8,128)S(1)}, f32[8,128]{1,0:T(8,128)S(1)}, u32[]{:S(2)}, u32[]{:S(2)}) collective-permute-start(f32[8,128]{1,0:T(8,128)S(1)} %get-tuple-element.33.after_ref), channel_id=1, source_target_pairs={{0,3},{1,0},{2,1},{3,2},{4,7},{5,4},{6,5},{7,6},{8,11},{9,8},{10,9... | collective-permute-start | bytes 12296 | tf_op jit(solution)/shard_map/ppermute | solution.py:526
  69.4 15.1 %all-to-all-start.4 = ((f32[8,40,128]{2,1,0:T(8,128)}), f32[8,40,128]{2,1,0:T(8,128)S(1)}, u32[]{:S(2)}, u32[]{:S(2)}) async-start(f32[8,40,128]{2,1,0:T(8,128)} %bitcast.58), calls=%async_computation.4 | async-start | bytes 327680 | tf_op jit(solution)/shard_map/all_to_all | solution.py:519
  76.0 5.5 %collective-permute-start.4 = (f32[8,128]{1,0:T(8,128)S(1)}, f32[8,128]{1,0:T(8,128)S(1)}, u32[]{:S(2)}, u32[]{:S(2)}) collective-permute-start(f32[8,128]{1,0:T(8,128)S(1)} %get-tuple-element.41), channel_id=1, source_target_pairs={{0,1},{1,2},{2,3},{3,0},{4,5},{5,6},{6,7},{7,4},{8,9},{9,10},{10,1... | collective-permute-start | bytes 12296 | tf_op jit(solution)/shard_map/ppermute | solution.py:526
  85.3 12.0 %all-to-all-start.5 = ((f32[8,40,128]{2,1,0:T(8,128)}), f32[8,40,128]{2,1,0:T(8,128)S(1)}, u32[]{:S(2)}, u32[]{:S(2)}) async-start(f32[8,40,128]{2,1,0:T(8,128)} %bitcast.59), calls=%async_computation.5 | async-start | bytes 327680 | tf_op jit(solution)/shard_map/all_to_all | solution.py:519
  89.0 4.9 %collective-permute-start.5 = (f32[8,128]{1,0:T(8,128)S(1)}, f32[8,128]{1,0:T(8,128)S(1)}, u32[]{:S(2)}, u32[]{:S(2)}) collective-permute-start(f32[8,128]{1,0:T(8,128)S(1)} %get-tuple-element.44), channel_id=1, source_target_pairs={{0,3},{1,0},{2,1},{3,2},{4,7},{5,4},{6,5},{7,6},{8,11},{9,8},{10,9... | collective-permute-start | bytes 12296 | tf_op jit(solution)/shard_map/ppermute | solution.py:526

commit v10 on v9

--- a/solution.py
+++ b/solution.py
@@ -178,8 +178,28 @@
         copy.wait()
 
 
+def halo_kernel(state_hbm, back_hbm, up_ref, down_ref, state_ref, back_ref, sems):
+    copies = fetch(state_hbm, state_ref, sems, 0)
+    for i in range(VARS):
+        upper = back_hbm.at[i, :, pl.ds(STEPS, STEPS), :]
+        copies.append(pltpu.make_async_copy(upper, back_ref.at[i], sems.at[VARS + i]))
+        copies[-1].start()
+    up_ref[...] = jnp.zeros(up_ref.shape, F32)
+    down_ref[...] = jnp.zeros(down_ref.shape, F32)
+    arrive(copies)
+    for t in range(TILES):
+        lines = slice(t * 128, (t + 1) * 128)
+        for v in range(VARS):
+            begin = v * 8 + TILES + t
+            up_ref[begin : begin + 1, :] = state_ref[v, 2 * STEPS - 1 : 2 * STEPS, lines]
+            down_ref[v * 8 + t : v * 8 + t + 1, :] = state_ref[v, 0:1, lines]
+        for n in range(SIZE):
+            begin = (VARS + n // 2) * 8 + n % 2 * TILES + t
+            up_ref[begin : begin + 1, :] = back_ref[n // VARS, n % VARS, STEPS - 1 : STEPS, lines]
+
+
 def pack_kernel(
-    state_hbm, coupling_hbm, back_hbm, u_ref, last_ref, first_ref, chain_ref, up_ref, down_ref,
+    state_hbm, coupling_hbm, back_hbm, u_ref, last_ref, first_ref, chain_ref,
     state_ref, coupling_raw, back_raw, sems,
 ):
     sub, lane = iotas()
@@ -193,12 +213,6 @@
     matrix_to_packed(coupling_raw, chain_ref, 0)
     arrive(back_copies)
     matrix_to_packed(back_raw, chain_ref, MATRIX)
-    up_ref[: VARS * 8, :] = u_ref[(STEPS - 1) * VARS * 8 :, :]
-    blocks = rows(chain_ref, (2 * STEPS - 1) * SIZE, SIZE)
-    for n in range(0, SIZE, 2):
-        pair = jnp.where(sub < TILES, pltpu.roll(blocks[n], 4, 0), blocks[min(n + 1, SIZE - 1)])
-        put(up_ref, VARS + n // 2, pair)
-    down_ref[...] = u_ref[: VARS * 8, :]
 
 
 def piece_out(stage_ref, out_hbm, sems, index, count):
@@ -356,7 +370,7 @@
             put(source_ref, k * VARS + v, value)
         return carry
 
-    lax.fori_loop(0, STEPS, source_step, 0)
+    lax.fori_loop(0, STEPS, source_step, 0, unroll=True)
     y = rows(source_ref, 0, VARS)
     kept = [y]
     for k in range(1, STEPS):
@@ -413,7 +427,7 @@
         def step(_, now):
             return step_plus(source, maps, shift(sub, now, entry))
 
-        out = lax.fori_loop(0, 7, step, step_plus(source, maps, shift(sub, zero, entry)))
+        out = lax.fori_loop(0, 7, step, step_plus(source, maps, shift(sub, zero, entry)), unroll=True)
         return out, shift(sub, out, entry)
 
     ends = [[value(r, part) for r in range(VARS)] for part in range(2)]
@@ -534,9 +548,14 @@
     raw_matrix = (VARS,) + raw_field
     cells_first = state[0].transpose(1, 0, 2)
     sent = cells_first.reshape(VARS, 2, STEPS, TILES, 128).transpose(0, 1, 3, 2, 4).reshape(FIELD, 128)
-    u, last_line, first_line, chain, up, above = call(
-        pack_kernel, [(FIELD, 128), edge, edge, (CHAIN, 128), (UP, 128), halo],
-        cells_first, coupling[0].transpose(1, 2, 0, 3), back_coupling[0].transpose(1, 2, 0, 3),
+    backs = back_coupling[0].transpose(1, 2, 0, 3)
+    up, above = call(
+        halo_kernel, [(UP, 128), halo], cells_first, backs,
+        scratch=[raw_field, (VARS, VARS, STEPS, TILES * 128), pltpu.SemaphoreType.DMA((2 * VARS,))], far=2,
+    )
+    u, last_line, first_line, chain = call(
+        pack_kernel, [(FIELD, 128), edge, edge, (CHAIN, 128)],
+        cells_first, coupling[0].transpose(1, 2, 0, 3), backs,
         scratch=[raw_field, raw_matrix, raw_matrix, pltpu.SemaphoreType.DMA((3 * VARS,))], far=3,
         limit=12,
     )

time: 124 us -> 123 us (level)
  waiting for transfers between devices: 13.3 us -> 11.5 us
    ppermute x6, waiting for transfers between devices: 6.55 us -> 4.74 us  [moved(): return lax.ppermute(value, axis, pairs)]
    pallas_call x10 -> x11, Pallas kernels: 10.2 us -> 11 us  [call(): pl.pallas_call(kernel, out_shape=outs, in_specs=specs, out_specs=[pl.Bloc...]
  transfers between devices with their start and end apart: 10 -> 10, of which waited for: 6 -> 6; matrix products, arithmetic and copies ran while one was open for 0% -> 0% of each run, Pallas kernels for 3% -> 4%
where the time goes in v10:
time: 123 us; the launch traced here: 122 us
  blocking collectives  52.2 us (42%)
  starting transfers between devices  47.6 us (39%)
  waiting for transfers between devices  11.5 us (9%)
  Pallas kernels  11 us (9%)
    all_to_all x4, blocking collectives, exchange(): lax.all_to_all(value.reshape(count, shape[0] // count, 128), axis, 0, 0)  52.2 us
    all_to_all x4, starting transfers between devices, exchange(): lax.all_to_all(value.reshape(count, shape[0] // count, 128), axis, 0, 0)  28 us
    ppermute x6, starting transfers between devices, moved(): return lax.ppermute(value, axis, pairs)  19.5 us
    pallas_call x11, Pallas kernels, call(): pl.pallas_call(kernel, out_shape=outs, in_specs=specs, out_specs=[pl.Bloc...  11 us
    all_to_all x4, waiting for transfers between devices, exchange(): lax.all_to_all(value.reshape(count, shape[0] // count, 128), axis, 0, 0)  6.77 us
    ppermute x6, waiting for transfers between devices, moved(): return lax.ppermute(value, axis, pairs)  4.74 us
  transfers between devices with their start and end apart: 10, of which 6 were waited for; matrix products, arithmetic and copies ran while one was open for 0% of the time, Pallas kernels for 4%

profile of v10, /device:TPU:1, one launch (start us, length us, event | category | flops | bytes accessed | tf_op | source)
XLA Modules:
  0.0 122.4 jit_solution(13363830251187074923)
XLA Ops:
  0.0 10.9 %all-to-all-start = ((f32[8,40,128]{2,1,0:T(8,128)}), f32[8,40,128]{2,1,0:T(8,128)S(1)}, u32[]{:S(2)}, u32[]{:S(2)}) async-start(f32[8,40,128]{2,1,0:T(8,128)} %bitcast.54), calls=%async_computation | async-start | bytes 327680 | tf_op jit(solution)/shard_map/all_to_all | solution.py:533
  10.9 1.3 %shard_map.65 = (f32[144,128]{1,0:T(8,128)S(1)}, f32[40,128]{1,0:T(8,128)S(1)}) custom-call(f32[5,16,512]{2,1,0:T(8,128)} %bitcast.55, f32[5,5,16,512]{3,2,1,0:T(8,128)} %bitcast.52), custom_call_target="tpu_custom_call" | custom-call | flops 100000 | bytes 1077248 | tf_op jit(solution)/shard_map/pallas_call | solution.py:520
  12.2 4.0 %collective-permute-start = (f32[144,128]{1,0:T(8,128)S(1)}, f32[144,128]{1,0:T(8,128)S(1)}, u32[]{:S(2)}, u32[]{:S(2)}) collective-permute-start(f32[144,128]{1,0:T(8,128)S(1)} %get-tuple-element.28), channel_id=1, source_target_pairs={{0,4},{4,8},{8,12},{12,16},{16,20},{20,24},{24,28},{28,32},{32,36}... | collective-permute-start | bytes 221192 | tf_op jit(solution)/shard_map/ppermute | solution.py:540
  16.2 1.9 %collective-permute-start.1 = (f32[40,128]{1,0:T(8,128)S(1)}, f32[40,128]{1,0:T(8,128)S(1)}, u32[]{:S(2)}, u32[]{:S(2)}) collective-permute-start(f32[40,128]{1,0:T(8,128)S(1)} %get-tuple-element.29), channel_id=1, source_target_pairs={{4,0},{8,4},{12,8},{16,12},{20,16},{24,20},{28,24},{32,28},{36,32}... | collective-permute-start | bytes 61448 | tf_op jit(solution)/shard_map/ppermute | solution.py:540
  18.1 1.8 %shard_map.64 = (f32[320,128]{1,0:T(8,128)S(1)}, f32[8,128]{1,0:T(8,128)S(1)}, f32[8,128]{1,0:T(8,128)S(1)}, f32[3200,128]{1,0:T(8,128)S(1)}) custom-call(f32[5,16,512]{2,1,0:T(8,128)} %bitcast.56, f32[5,5,16,512]{3,2,1,0:T(8,128)} %bitcast.57, f32[5,5,16,512]{3,2,1,0:T(8,128)} %bitcast.53), custom_call_target="tpu_custom_call" | custom-call | flops 100000 | bytes 3612672 | tf_op jit(solution)/shard_map/pallas_call | solution.py:520
  19.9 1.4 %collective-permute-done.1.refs_4_.rest_1_ = f32[40,128]{1,0:T(8,128)S(1)} collective-permute-done((f32[40,128]{1,0:T(8,128)S(1)}, f32[40,128]{1,0:T(8,128)S(1)}, u32[]{:S(2)}, u32[]{:S(2)}) %collective-permute-start.1) | collective-permute-done | bytes 20512 | tf_op jit(solution)/shard_map/ppermute | solution.py:540
  21.3 0.8 shard_map.66
  22.1 6.9 %all-to-all-start.1 = ((f32[8,40,128]{2,1,0:T(8,128)}), f32[8,40,128]{2,1,0:T(8,128)S(1)}, u32[]{:S(2)}, u32[]{:S(2)}) async-start(f32[8,40,128]{2,1,0:T(8,128)} %bitcast.59), calls=%async_computation.1 | async-start | bytes 327680 | tf_op jit(solution)/shard_map/all_to_all | solution.py:533
  29.0 3.1 %collective-permute-start.2 = (f32[8,128]{1,0:T(8,128)S(1)}, f32[8,128]{1,0:T(8,128)S(1)}, u32[]{:S(2)}, u32[]{:S(2)}) collective-permute-start(f32[8,128]{1,0:T(8,128)S(1)} %get-tuple-element.35), channel_id=1, source_target_pairs={{0,1},{1,2},{2,3},{3,0},{4,5},{5,6},{6,7},{7,4},{8,9},{9,10},{10,1... | collective-permute-start | bytes 12296 | tf_op jit(solution)/shard_map/ppermute | solution.py:540
  32.1 3.4 %collective-permute-start.3 = (f32[8,128]{1,0:T(8,128)S(1)}, f32[8,128]{1,0:T(8,128)S(1)}, u32[]{:S(2)}, u32[]{:S(2)}) collective-permute-start(f32[8,128]{1,0:T(8,128)S(1)} %get-tuple-element.33.after_ref), channel_id=1, source_target_pairs={{0,3},{1,0},{2,1},{3,2},{4,7},{5,4},{6,5},{7,6},{8,11},{9,8},{10,9... | collective-permute-start | bytes 12296 | tf_op jit(solution)/shard_map/ppermute | solution.py:540
  35.5 2.0 %shard_map.67 = (f32[2520,128]{1,0:T(8,128)S(1)}, f32[384,128]{1,0:T(8,128)}) custom-call(f32[3200,128]{1,0:T(8,128)S(1)} %get-tuple-element.32.chain_ref.refs_3_, f32[8,128]{1,0:T(8,128)S(1)} %get-tuple-element.33.after_ref, f32[5,5,16,512]{3,2,1,0:T(8,128)} %bitcast.58, f32[5,16,512]{2,1,0:T(8,128)} %bitcast.62, s32[16,512]{1,0:T(8,128)} %flags_hbm.1), custom_call_target="tpu_custom_call" | custom-call | flops 8000000 | bytes 4145152 | tf_op jit(solution)/shard_map/pallas_call | solution.py:520
  37.5 0.0 collective-permute-done.2.left_ref
  37.6 0.2 all-to-all-done.1
  37.8 1.2 shard_map.68
  39.0 18.6 %all_to_all.40 = f32[16,24,128]{2,1,0:T(8,128)S(1)} all-to-all(f32[16,24,128]{2,1,0:T(8,128)S(1)} %bitcast.45), channel_id=1, replica_groups=mesh['inst'=8,'axial'=16,'span'=4] {'axial'}, dimensions={0} | all-to-all | bytes 393216 | tf_op jit(solution)/shard_map/all_to_all | solution.py:533
  57.6 0.4 shard_map.69
  58.0 10.1 %all_to_all.41 = f32[16,4,128]{2,1,0:T(4,128)S(1)} all-to-all(f32[16,4,128]{2,1,0:T(4,128)S(1)} %bitcast.47), channel_id=1, replica_groups=mesh['inst'=8,'axial'=16,'span'=4] {'axial'}, dimensions={0} | all-to-all | bytes 65536 | tf_op jit(solution)/shard_map/all_to_all | solution.py:533
  68.1 0.9 shard_map.70
  69.0 6.6 %all-to-all-start.4 = ((f32[8,40,128]{2,1,0:T(8,128)}), f32[8,40,128]{2,1,0:T(8,128)S(1)}, u32[]{:S(2)}, u32[]{:S(2)}) async-start(f32[8,40,128]{2,1,0:T(8,128)} %bitcast.60), calls=%async_computation.4 | async-start | bytes 327680 | tf_op jit(solution)/shard_map/all_to_all | solution.py:533
  75.6 2.9 %collective-permute-start.4 = (f32[8,128]{1,0:T(8,128)S(1)}, f32[8,128]{1,0:T(8,128)S(1)}, u32[]{:S(2)}, u32[]{:S(2)}) collective-permute-start(f32[8,128]{1,0:T(8,128)S(1)} %get-tuple-element.41), channel_id=1, source_target_pairs={{0,1},{1,2},{2,3},{3,0},{4,5},{5,6},{6,7},{7,4},{8,9},{9,10},{10,1... | collective-permute-start | bytes 12296 | tf_op jit(solution)/shard_map/ppermute | solution.py:540
  78.5 2.6 %collective-permute-done.4.refs_2_.left_ref = f32[8,128]{1,0:T(8,128)S(1)} collective-permute-done((f32[8,128]{1,0:T(8,128)S(1)}, f32[8,128]{1,0:T(8,128)S(1)}, u32[]{:S(2)}, u32[]{:S(2)}) %collective-permute-start.4) | collective-permute-done | bytes 4128 | tf_op jit(solution)/shard_map/ppermute | solution.py:540
  81.2 3.0 %all-to-all-done.4 = f32[8,40,128]{2,1,0:T(8,128)S(1)} async-done(((f32[8,40,128]{2,1,0:T(8,128)}), f32[8,40,128]{2,1,0:T(8,128)S(1)}, u32[]{:S(2)}, u32[]{:S(2)}) %all-to-all-start.4) | async-done | bytes 163872 | tf_op jit(solution)/shard_map/all_to_all | solution.py:533
  84.2 0.8 shard_map.71
  85.0 3.6 %all-to-all-start.5 = ((f32[8,40,128]{2,1,0:T(8,128)}), f32[8,40,128]{2,1,0:T(8,128)S(1)}, u32[]{:S(2)}, u32[]{:S(2)}) async-start(f32[8,40,128]{2,1,0:T(8,128)} %bitcast.61), calls=%async_computation.5 | async-start | bytes 327680 | tf_op jit(solution)/shard_map/all_to_all | solution.py:533
  88.6 4.2 %collective-permute-start.5 = (f32[8,128]{1,0:T(8,128)S(1)}, f32[8,128]{1,0:T(8,128)S(1)}, u32[]{:S(2)}, u32[]{:S(2)}) collective-permute-start(f32[8,128]{1,0:T(8,128)S(1)} %get-tuple-element.44), channel_id=1, source_target_pairs={{0,3},{1,0},{2,1},{3,2},{4,7},{5,4},{6,5},{7,6},{8,11},{9,8},{10,9... | collective-permute-start | bytes 12296 | tf_op jit(solution)/shard_map/ppermute | solution.py:540
  92.8 0.7 collective-permute-done.5.right_ref
  93.5 3.5 %all-to-all-done.5 = f32[8,40,128]{2,1,0:T(8,128)S(1)} async-done(((f32[8,40,128]{2,1,0:T(8,128)}), f32[8,40,128]{2,1,0:T(8,128)S(1)}, u32[]{:S(2)}, u32[]{:S(2)}) %all-to-all-start.5) | async-done | bytes 163872 | tf_op jit(solution)/shard_map/all_to_all | solution.py:533
  97.0 0.4 shard_map.72
  97.4 13.3 %all_to_all.42 = f32[16,4,128]{2,1,0:T(4,128)S(1)} all-to-all(f32[16,4,128]{2,1,0:T(4,128)S(1)} %bitcast.51), channel_id=1, replica_groups=mesh['inst'=8,'axial'=16,'span'=4] {'axial'}, dimensions={0} | all-to-all | bytes 65536 | tf_op jit(solution)/shard_map/all_to_all | solution.py:533
  110.7 0.4 shard_map.73
  111.2 10.3 %all_to_all.43 = f32[16,4,128]{2,1,0:T(4,128)S(1)} all-to-all(f32[16,4,128]{2,1,0:T(4,128)S(1)} %bitcast.49), channel_id=1, replica_groups=mesh['inst'=8,'axial'=16,'span'=4] {'axial'}, dimensions={0} | all-to-all | bytes 65536 | tf_op jit(solution)/shard_map/all_to_all | solution.py:533
  121.4 0.9 shard_map.74
  (3 shorter events, 0.0 us)
Async XLA Ops:
  0.0 21.3 %all-to-all-start = ((f32[8,40,128]{2,1,0:T(8,128)}), f32[8,40,128]{2,1,0:T(8,128)S(1)}, u32[]{:S(2)}, u32[]{:S(2)}) async-start(f32[8,40,128]{2,1,0:T(8,128)} %bitcast.54), calls=%async_computation | async-start | bytes 327680 | tf_op jit(solution)/shard_map/all_to_all | solution.py:533
  12.2 9.2 %collective-permute-start = (f32[144,128]{1,0:T(8,128)S(1)}, f32[144,128]{1,0:T(8,128)S(1)}, u32[]{:S(2)}, u32[]{:S(2)}) collective-permute-start(f32[144,128]{1,0:T(8,128)S(1)} %get-tuple-element.28), channel_id=1, source_target_pairs={{0,4},{4,8},{8,12},{12,16},{16,20},{20,24},{24,28},{28,32},{32,36}... | collective-permute-start | bytes 221192 | tf_op jit(solution)/shard_map/ppermute | solution.py:540
  16.2 5.1 %collective-permute-start.1 = (f32[40,128]{1,0:T(8,128)S(1)}, f32[40,128]{1,0:T(8,128)S(1)}, u32[]{:S(2)}, u32[]{:S(2)}) collective-permute-start(f32[40,128]{1,0:T(8,128)S(1)} %get-tuple-element.29), channel_id=1, source_target_pairs={{4,0},{8,4},{12,8},{16,12},{20,16},{24,20},{28,24},{32,28},{36,32}... | collective-permute-start | bytes 61448 | tf_op jit(solution)/shard_map/ppermute | solution.py:540
  22.1 15.7 %all-to-all-start.1 = ((f32[8,40,128]{2,1,0:T(8,128)}), f32[8,40,128]{2,1,0:T(8,128)S(1)}, u32[]{:S(2)}, u32[]{:S(2)}) async-start(f32[8,40,128]{2,1,0:T(8,128)} %bitcast.59), calls=%async_computation.1 | async-start | bytes 327680 | tf_op jit(solution)/shard_map/all_to_all | solution.py:533
  29.0 8.5 %collective-permute-start.2 = (f32[8,128]{1,0:T(8,128)S(1)}, f32[8,128]{1,0:T(8,128)S(1)}, u32[]{:S(2)}, u32[]{:S(2)}) collective-permute-start(f32[8,128]{1,0:T(8,128)S(1)} %get-tuple-element.35), channel_id=1, source_target_pairs={{0,1},{1,2},{2,3},{3,0},{4,5},{5,6},{6,7},{7,4},{8,9},{9,10},{10,1... | collective-permute-start | bytes 12296 | tf_op jit(solution)/shard_map/ppermute | solution.py:540
  32.1 5.4 %collective-permute-start.3 = (f32[8,128]{1,0:T(8,128)S(1)}, f32[8,128]{1,0:T(8,128)S(1)}, u32[]{:S(2)}, u32[]{:S(2)}) collective-permute-start(f32[8,128]{1,0:T(8,128)S(1)} %get-tuple-element.33.after_ref), channel_id=1, source_target_pairs={{0,3},{1,0},{2,1},{3,2},{4,7},{5,4},{6,5},{7,6},{8,11},{9,8},{10,9... | collective-permute-start | bytes 12296 | tf_op jit(solution)/shard_map/ppermute | solution.py:540
  69.0 15.2 %all-to-all-start.4 = ((f32[8,40,128]{2,1,0:T(8,128)}), f32[8,40,128]{2,1,0:T(8,128)S(1)}, u32[]{:S(2)}, u32[]{:S(2)}) async-start(f32[8,40,128]{2,1,0:T(8,128)} %bitcast.60), calls=%async_computation.4 | async-start | bytes 327680 | tf_op jit(solution)/shard_map/all_to_all | solution.py:533
  75.6 5.5 %collective-permute-start.4 = (f32[8,128]{1,0:T(8,128)S(1)}, f32[8,128]{1,0:T(8,128)S(1)}, u32[]{:S(2)}, u32[]{:S(2)}) collective-permute-start(f32[8,128]{1,0:T(8,128)S(1)} %get-tuple-element.41), channel_id=1, source_target_pairs={{0,1},{1,2},{2,3},{3,0},{4,5},{5,6},{6,7},{7,4},{8,9},{9,10},{10,1... | collective-permute-start | bytes 12296 | tf_op jit(solution)/shard_map/ppermute | solution.py:540
  85.0 12.0 %all-to-all-start.5 = ((f32[8,40,128]{2,1,0:T(8,128)}), f32[8,40,128]{2,1,0:T(8,128)S(1)}, u32[]{:S(2)}, u32[]{:S(2)}) async-start(f32[8,40,128]{2,1,0:T(8,128)} %bitcast.61), calls=%async_computation.5 | async-start | bytes 327680 | tf_op jit(solution)/shard_map/all_to_all | solution.py:533
  88.6 4.9 %collective-permute-start.5 = (f32[8,128]{1,0:T(8,128)S(1)}, f32[8,128]{1,0:T(8,128)S(1)}, u32[]{:S(2)}, u32[]{:S(2)}) collective-permute-start(f32[8,128]{1,0:T(8,128)S(1)} %get-tuple-element.44), channel_id=1, source_target_pairs={{0,3},{1,0},{2,1},{3,2},{4,7},{5,4},{6,5},{7,6},{8,11},{9,8},{10,9... | collective-permute-start | bytes 12296 | tf_op jit(solution)/shard_map/ppermute | solution.py:540
